TPU v7x, 32 devices: a whole 2x2x4 slice. The times are simulated.
32 devices in a mesh: leaf: 4 (over x, core), row: 2 (over y), col: 4 (over z).
Axes of the slice: x: 2, y: 2, z: 4, core: 2. Of those that a mesh axis runs over, the one named last changes fastest.
Arguments:
- top_inverse: float32 [4096, 4096], P('row', ('leaf', 'col')), as said below
- pattern: int32 [4, 16], P('leaf'), may hold values from 0 to 31, as said below
- panel: float32 [4, 2048, 2048], P('leaf', None, 'col'), may hold values from -1.6 to 1.6
- diag_inverse: float32 [4, 2048, 2048], P('leaf', 'row', 'col'), as said below
Outputs:
- sigma_top: float32 [4096, 4096], P('row', ('leaf', 'col'))
- sigma_panel: float32 [4, 2048, 2048], P('leaf', 'row', 'col')
- sigma_diag: float32 [4, 2048, 2048], P('leaf', 'row', 'col')
Inputs may be any that keep to these rules, and one draw needn't show every extreme that they name: `pattern`: each row holds 16 distinct block indices in rising order, among them 0 and 31. `top_inverse`: lower triangular with a positive diagonal. `diag_inverse`: each group's block is symmetric.
All inputs are finite; a program needn't handle non-finite values.
Results may differ from a plain program's by a relative error of at most 0.00016.
Values sent between devices are 32-bit elements; how exact they have to be, the bound alone decides.
No kernel may reach another device: no remote copies, remote signals or barrier semaphores. Data moves between devices by JAX's collectives and lax.ppermute only.
A program may use at most 128 MiB of HBM per device.

v0:
```python
import jax
import jax.numpy as jnp
from jax import lax
from jax.sharding import PartitionSpec as P

BLK = 128


def contract_rows(left, right):
    return lax.dot_general(
        left,
        right,
        (((0,), (0,)), ((), ())),
        precision=lax.Precision.HIGHEST,
        preferred_element_type=jnp.float32,
    )


def per_device(top_inverse, pattern, panel, diag_inverse):
    exact = lax.Precision.HIGHEST
    rows_here = lax.all_gather(top_inverse, ("leaf", "col"), axis=1, tiled=True)
    columns = rows_here
    sigma_top = lax.psum_scatter(
        contract_rows(columns, top_inverse), "row", scatter_dimension=0, tiled=True
    )
    offsets = jnp.arange(BLK, dtype=jnp.int32)
    wanted = (pattern[0][:, None] * BLK + offsets[None, :]).reshape(-1)
    selected = jnp.take(rows_here, wanted, axis=1)
    normed = panel[0]
    image = jnp.dot(selected, normed, precision=exact, preferred_element_type=jnp.float32)
    panel_count = normed.shape[0] // lax.axis_size("row")
    columns = selected
    sigma_panel = lax.psum_scatter(
        -contract_rows(columns, image), "row", scatter_dimension=0, tiled=True
    )
    own_rows = lax.dynamic_slice_in_dim(normed, lax.axis_index("row") * panel_count, panel_count, 0)
    whole_rows = lax.all_gather(own_rows, "col", axis=1, tiled=True)
    columns = whole_rows
    update = -lax.psum_scatter(
        contract_rows(columns, sigma_panel), "row", scatter_dimension=0, tiled=True
    )
    sigma_diag = diag_inverse[0] + update
    return (sigma_top, sigma_panel[None], sigma_diag[None])


def solution(mesh):
    placed = (
        P("row", ("leaf", "col")),
        P("leaf", None),
        P("leaf", None, "col"),
        P("leaf", "row", "col"),
    )
    return jax.shard_map(
        per_device,
        mesh=mesh,
        in_specs=placed,
        out_specs=(P("row", ("leaf", "col")), P("leaf", "row", "col"), P("leaf", "row", "col")),
        check_vma=False,
    )
```

profile of v0, /device:TPU:0, one launch (start us, length us, event | category | flops | bytes accessed | tf_op | source)
XLA Modules:
  0.0 533.9 jit_solution(8787381201068351722)
XLA Ops:
  7.2 0.0 all-gather.4.cloned.1.call-start
  7.2 2.9 copy.7
  10.1 0.0 copy-start.3
  10.1 0.0 all-gather.4.cloned.1.call-update
  10.1 0.0 all-gather.6.cloned.1.call-start
  10.2 3.1 constant_dynamic-slice_fusion
  13.3 0.0 all-gather.6.cloned.1.call-update
  13.3 0.0 reduce-scatter.6.cloned.1.call-start
  13.3 0.0 copy-done.3
  13.4 0.1 compare_and_fusion
  13.4 0.1 iota_add_fusion
  13.5 177.4 %all-gather.4.cloned.1.call-done = f32[2048,4096]{0,1:T(8,128)} async-done(((f32[2048,256]{0,1:T(8,128)}), f32[2048,4096]{0,1:T(8,128)}) %all-gather.4.cloned.1.call-update) | async-done | bytes 33554448 | tf_op jit(solution)/shard_map/all_gather | solution.py:21
  190.9 27.9 %gather_fusion = f32[2048,2048]{1,0:T(8,128)} fusion(f32[2048,4096]{0,1:T(8,128)} %all-gather.4.cloned.1.call-done, s32[2048]{0:T(1024)S(1)} %broadcast_clamp_fusion), kind=kCustom, calls=%fused_computation | custom fusion | bytes 33562624 | tf_op jit(solution)/shard_map/jit(_take)/gather | solution.py:28
  218.9 0.0 copy-start
  218.9 33.7 %fusion = f32[2048,512]{1,0:T(8,128)S(1)} fusion(f32[2048,2048]{1,0:T(8,128)} %gather_fusion, pred[2048]{0:T(1024)(128)(4,1)S(1)} %compare_and_fusion, f32[1,2048,512]{2,1,0:T(8,128)} %param.6), kind=kOutput, calls=%fused_computation.1 | convolution fusion | flops 25773998080 | bytes 25167872 | tf_op jit(solution)/shard_map/dot_general | solution.py:30
  252.6 0.0 copy-done
  252.6 29.6 %fusion.11 = f32[2048,512]{1,0:T(8,128)} fusion(f32[2048,512]{1,0:T(8,128)S(1)} %fusion, f32[2048,2048]{1,0:T(8,128)S(1)} %copy-done, pred[2048]{0:T(1024)(128)(4,1)S(1)} %compare_and_fusion), kind=kOutput, calls=%fused_computation.12 | convolution fusion | flops 25775046656 | bytes 25167872 | tf_op jit(solution)/shard_map/dot_general | solution.py:10
  282.2 0.0 reduce-scatter.6.cloned.1.call-update
  282.2 0.0 reduce-scatter.8.cloned.1.call-start
  282.2 60.5 %all-gather.6.cloned.1.call-done = f32[1,1024,2048]{2,1,0:T(8,128)} async-done(((f32[1,1024,512]{2,1,0:T(8,128)}), f32[1,1024,2048]{2,1,0:T(8,128)}) %all-gather.6.cloned.1.call-update) | async-done | bytes 8388624 | tf_op jit(solution)/shard_map/all_gather | solution.py:37
  342.7 55.4 %reduce-scatter.6.cloned.1.call-done = f32[1024,512]{1,0:T(8,128)} async-done(((f32[2048,512]{1,0:T(8,128)}), f32[1024,512]{1,0:T(8,128)}) %reduce-scatter.6.cloned.1.call-update) | async-done | bytes 2097168 | tf_op jit(solution)/shard_map/reduce_scatter | solution.py:33
  398.1 17.7 %fusion.4 = f32[2048,512]{1,0:T(8,128)} fusion(f32[1024,512]{1,0:T(8,128)} %reduce-scatter.6.cloned.1.call-done, f32[1,1024,2048]{2,1,0:T(8,128)} %all-gather.6.cloned.1.call-done), kind=kOutput, calls=%fused_computation.5 | convolution fusion | flops 12884901888 | bytes 14680064 | tf_op jit(solution)/shard_map/dot_general | solution.py:10
  415.8 0.0 copy-start.1
  415.8 0.0 reduce-scatter.8.cloned.1.call-update
  415.8 0.0 reduce-scatter.4.cloned.1.call-start
  415.9 1.5 copy-done.1
  417.4 31.0 %fusion.17 = f32[4096,256]{1,0:T(8,128)} fusion(f32[2048,4096]{0,1:T(8,128)} %all-gather.4.cloned.1.call-done, f32[2048,256]{1,0:T(8,128)S(1)} %copy-done.1), kind=kOutput, calls=%fused_computation.24 | convolution fusion | flops 25769803776 | bytes 39845888 | tf_op jit(solution)/shard_map/dot_general | solution.py:10
  448.4 0.0 reduce-scatter.4.cloned.1.call-update
  448.4 21.8 %reduce-scatter.8.cloned.1.call-done = f32[1024,512]{1,0:T(8,128)} async-done(((f32[2048,512]{1,0:T(8,128)}), f32[1024,512]{1,0:T(8,128)}) %reduce-scatter.8.cloned.1.call-update) | async-done | bytes 2097168 | tf_op jit(solution)/shard_map/reduce_scatter | solution.py:39
  470.3 0.0 copy-done.2
  470.3 3.4 fusion.14
  473.7 53.7 %reduce-scatter.4.cloned.1.call-done = f32[2048,256]{1,0:T(8,128)} async-done(((f32[4096,256]{1,0:T(8,128)}), f32[2048,256]{1,0:T(8,128)}) %reduce-scatter.4.cloned.1.call-update) | async-done | bytes 2097168 | tf_op jit(solution)/shard_map/reduce_scatter | solution.py:23
  (4 shorter events, 0.0 us)
Async XLA Ops:
  7.2 183.7 %all-gather.4.cloned.1.call-start = ((), (), s32[]{:S(2)}) async-start(), calls=%async_computation.3 | async-start | bytes 35651584 | tf_op jit(solution)/shard_map/all_gather | solution.py:21
  10.1 3.2 copy-start.3
  10.1 332.6 %all-gather.6.cloned.1.call-start = ((), (), s32[]{:S(2)}) async-start(), calls=%async_computation.7 | async-start | bytes 10485760 | tf_op jit(solution)/shard_map/all_gather | solution.py:37
  13.3 384.8 %reduce-scatter.6.cloned.1.call-start = ((), (), s32[]{:S(2)}) async-start(), calls=%async_computation.5 | async-start | bytes 6291456 | tf_op jit(solution)/shard_map/reduce_scatter | solution.py:33
  218.9 33.7 %copy-start = (f32[2048,2048]{1,0:T(8,128)S(1)}, f32[2048,2048]{1,0:T(8,128)}, u32[]{:S(2)}) copy-start(f32[2048,2048]{1,0:T(8,128)} %gather_fusion) | copy-start | bytes 50331652
  282.2 188.1 %reduce-scatter.8.cloned.1.call-start = ((), (), s32[]{:S(2)}) async-start(), calls=%async_computation.6 | async-start | bytes 6291456 | tf_op jit(solution)/shard_map/reduce_scatter | solution.py:39
  415.8 1.6 copy-start.1
  415.8 111.5 %reduce-scatter.4.cloned.1.call-start = ((), (), s32[]{:S(2)}) async-start(), calls=%async_computation.4 | async-start | bytes 6291456 | tf_op jit(solution)/shard_map/reduce_scatter | solution.py:23
  448.4 21.8 %copy-start.2 = (f32[1,1024,512]{2,1,0:T(8,128)S(1)}, f32[1,1024,512]{2,1,0:T(8,128)}, u32[]{:S(2)}) copy-start(f32[1,1024,512]{2,1,0:T(8,128)} %param.7) | copy-start | bytes 6291460
Sparse Core Ops, SparseCore 0:
  10.2 180.6 all-gather.3
  193.0 149.6 all-gather.5
  345.6 52.4 reduce-scatter.5
  415.9 54.2 reduce-scatter.7
  473.0 54.3 reduce-scatter.3
where the time goes:
time: 534 us
  waiting for transfers between devices  369 us (69%)
  matrix products  112 us (21%)
  local copies, waits for them, and re-layouts  35.4 us (7%)
  between operations  13.8 us (3%)
    all_gather x1, waiting for transfers between devices, per_device(): rows_here = lax.all_gather(top_inverse, ('leaf', 'col'), axis=1, tiled=True)  177 us
    dot_general x3, matrix products, contract_rows(): lax.dot_general(left, right, (((0,), (0,)), ((), ())), precision=lax.Prec...  78.3 us
    all_gather x1, waiting for transfers between devices, per_device(): whole_rows = lax.all_gather(own_rows, 'col', axis=1, tiled=True)  60.5 us
    reduce_scatter x1, waiting for transfers between devices, per_device(): lax.psum_scatter(-contract_rows(columns, image), 'row', scatter_dimension...  55.4 us
    reduce_scatter x1, waiting for transfers between devices, per_device(): lax.psum_scatter(contract_rows(columns, top_inverse), 'row', scatter_dime...  53.7 us
    dot_general x1, matrix products, per_device(): jnp.dot(selected, normed, precision=exact, preferred_element_type=jnp.flo...  33.7 us
    gather x1, local copies, waits for them, and re-layouts, per_device(): selected = jnp.take(rows_here, wanted, axis=1)  27.9 us
    reduce_scatter x1, waiting for transfers between devices, per_device(): lax.psum_scatter(contract_rows(columns, sigma_panel), 'row', scatter_dime...  21.8 us
  transfers between devices with their start and end apart: 5, of which 5 were waited for; matrix products, arithmetic and copies ran while one was open for 24% of the time, Pallas kernels for 0%

commit v1 on v0

v1 whole, which is shorter than its diff:
```python
import jax
import jax.numpy as jnp
from jax import lax
from jax.sharding import PartitionSpec as P

BLK = 128


def contract_rows(left, right):
    return lax.dot_general(
        left,
        right,
        (((0,), (0,)), ((), ())),
        precision=lax.Precision.HIGH,
        preferred_element_type=jnp.float32,
    )


def shift(value, axis, pairs):
    return lax.ppermute(value, axis, pairs)


def line_gather(own, axis):
    count = lax.axis_size(axis)
    right, left = [own], [own]
    for step in range(count - 1):
        right.append(shift(right[-1], axis, [(i, i + 1) for i in range(step, count - 1)]))
        left.append(shift(left[-1], axis, [(i, i - 1) for i in range(1, count - step)]))
    me = lax.axis_index(axis)
    return [own] + [jnp.where(me >= t, right[t], left[count - t]) for t in range(1, count)]


def sum_scatter(part, axis):
    count = lax.axis_size(axis)
    me = lax.axis_index(axis)
    sent = []
    for away in range(1, count):
        pairs = [(i, (i + away) % count) for i in range(count)]
        sent.append(shift(part((me + away) % count), axis, pairs))
    total = part(me)
    for term in sent:
        total = total + term
    return total


def rows_of(array, index, count):
    return lax.dynamic_slice_in_dim(array, index * count, count, 0)


def per_device(top_inverse, pattern, panel, diag_inverse):
    rows = lax.axis_size("row")
    normed = panel[0]
    panel_count = normed.shape[0] // rows
    own_rows = rows_of(normed, lax.axis_index("row"), panel_count)
    pieces = line_gather(own_rows, "col")

    rows_here = lax.all_gather(top_inverse, ("leaf", "col"), axis=1, tiled=True)
    offsets = jnp.arange(BLK, dtype=jnp.int32)
    wanted = (pattern[0][:, None] * BLK + offsets[None, :]).reshape(-1)
    selected = jnp.take(rows_here, wanted, axis=1, mode="clip")
    image = jnp.dot(
        selected, normed, precision=lax.Precision.HIGH, preferred_element_type=jnp.float32
    )
    width = selected.shape[1] // rows
    sigma_panel = -sum_scatter(
        lambda i: contract_rows(lax.dynamic_slice_in_dim(selected, i * width, width, 1), image), "row"
    )
    top_width = rows_here.shape[1] // rows
    sigma_top = sum_scatter(
        lambda i: contract_rows(lax.dynamic_slice_in_dim(rows_here, i * top_width, top_width, 1), top_inverse),
        "row",
    )
    cols = lax.axis_size("col")
    me = lax.axis_index("col")
    wide = own_rows.shape[1]
    whole = jnp.concatenate(pieces[::-1] + pieces[::-1], axis=1)
    whole_rows = lax.dynamic_slice_in_dim(whole, (cols - 1 - me) * wide, cols * wide, 1)
    diag_width = whole_rows.shape[1] // rows
    update = sum_scatter(
        lambda i: contract_rows(
            lax.dynamic_slice_in_dim(whole_rows, i * diag_width, diag_width, 1), sigma_panel
        ),
        "row",
    )
    sigma_diag = diag_inverse[0] - update
    return (sigma_top, sigma_panel[None], sigma_diag[None])


def solution(mesh):
    placed = (
        P("row", ("leaf", "col")),
        P("leaf", None),
        P("leaf", None, "col"),
        P("leaf", "row", "col"),
    )
    return jax.shard_map(
        per_device,
        mesh=mesh,
        in_specs=placed,
        out_specs=(P("row", ("leaf", "col")), P("leaf", "row", "col"), P("leaf", "row", "col")),
        check_vma=False,
    )
```

time: 534 us -> 533 us (level); the launches traced: 534 us -> 527 us
  matrix products: 112 us -> 80.8 us
  other arithmetic: 3.57 us -> 20.8 us
  starting transfers between devices: 0.21 us -> 16.9 us
  waiting for transfers between devices: 369 us -> 357 us
    ppermute x0 -> x9, waiting for transfers between devices: none -> 201 us  [shift(): return lax.ppermute(value, axis, pairs)]
    reduce_scatter x3 -> x0, waiting for transfers between devices: 131 us -> none  [the longest x1 55.4 us: per_device(): lax.psum_scatter(-contract_rows(columns, image), 'row', scatter_dimension...]
    all_gather x1 -> x0, waiting for transfers between devices: 60.5 us -> none  [per_device(): whole_rows = lax.all_gather(own_rows, 'col', axis=1, tiled=True)]
    all_gather x1, waiting for transfers between devices: 177 us -> 156 us  [per_device(): rows_here = lax.all_gather(top_inverse, ('leaf', 'col'), axis=1, tiled=True)]
    unnamed x0 -> x6, other arithmetic: none -> 20.7 us
    ppermute x0 -> x9, starting transfers between devices: none -> 16.9 us  [shift(): return lax.ppermute(value, axis, pairs)]
    dot_general x1, matrix products: 33.7 us -> 17.5 us  [per_device(): jnp.dot(selected, normed, precision=lax.Precision.HIGH, preferred_element...]
    dot_general x3 -> x6, matrix products: 78.3 us -> 63.2 us  [contract_rows(): lax.dot_general(left, right, (((0,), (0,)), ((), ())), precision=lax.Prec...]
  transfers between devices with their start and end apart: 5 -> 10, of which waited for: 5 -> 7; matrix products, arithmetic and copies ran while one was open for 24% -> 23% of each run, Pallas kernels for 0% -> 0%
where the time goes in v1:
time: 533 us; the launch traced here: 527 us
  waiting for transfers between devices  357 us (67%)
  matrix products  80.8 us (15%)
  local copies, waits for them, and re-layouts  36.8 us (7%)
  other arithmetic  20.8 us (4%)
  starting transfers between devices  16.9 us (3%)
  between operations  14.4 us (3%)
    ppermute x9, waiting for transfers between devices, shift(): return lax.ppermute(value, axis, pairs)  201 us
    all_gather x1, waiting for transfers between devices, per_device(): rows_here = lax.all_gather(top_inverse, ('leaf', 'col'), axis=1, tiled=True)  156 us
    dot_general x6, matrix products, contract_rows(): lax.dot_general(left, right, (((0,), (0,)), ((), ())), precision=lax.Prec...  63.2 us
    gather x1, local copies, waits for them, and re-layouts, per_device(): selected = jnp.take(rows_here, wanted, axis=1, mode='clip')  27.1 us
    unnamed x6, other arithmetic  20.7 us
    dot_general x1, matrix products, per_device(): jnp.dot(selected, normed, precision=lax.Precision.HIGH, preferred_element...  17.5 us
    ppermute x9, starting transfers between devices, shift(): return lax.ppermute(value, axis, pairs)  16.9 us
  transfers between devices with their start and end apart: 10, of which 7 were waited for; matrix products, arithmetic and copies ran while one was open for 23% of the time, Pallas kernels for 0%

profile of v1, /device:TPU:0, one launch (start us, length us, event | category | flops | bytes accessed | tf_op | source)
XLA Modules:
  0.0 527.1 jit_solution(2215084556235930035)
XLA Ops:
  7.2 2.9 copy.7
  10.1 1.8 dynamic-slice_bitcast_fusion
  11.9 5.1 collective-permute-start.2
  17.0 1.3 collective-permute-start.5
  18.3 65.0 %collective-permute-done.2 = f32[1024,512]{1,0:T(8,128)S(1)} collective-permute-done((f32[1024,512]{1,0:T(8,128)S(1)}, f32[1024,512]{1,0:T(8,128)S(1)}, u32[]{:S(2)}, u32[]{:S(2)}) %collective-permute-start.2) | collective-permute-done | bytes 2097184 | tf_op jit(solution)/shard_map/ppermute | solution.py:20
  83.3 2.0 collective-permute-start.3
  85.3 3.6 collective-permute-done.5
  90.2 2.1 collective-permute-start.4
  92.3 68.5 %collective-permute-done.6 = f32[1024,512]{1,0:T(8,128)} collective-permute-done((f32[1024,512]{1,0:T(8,128)}, f32[1024,512]{1,0:T(8,128)}, u32[]{:S(2)}, u32[]{:S(2)}) %collective-permute-start.6) | collective-permute-done | bytes 2097184 | tf_op jit(solution)/shard_map/ppermute | solution.py:20
  162.1 3.4 fusion.22
  165.5 3.5 fusion.24
  169.0 156.2 %all-gather.2.cloned.1.call-done = f32[2048,4096]{0,1:T(8,128)} async-done(((f32[2048,256]{0,1:T(8,128)}), f32[2048,4096]{0,1:T(8,128)}) %all-gather.2.cloned.1.call-update) | async-done | bytes 33554448 | tf_op jit(solution)/shard_map/all_gather | solution.py:57
  325.2 27.1 %gather_fusion = f32[2048,2048]{1,0:T(8,128)} fusion(f32[2048,4096]{0,1:T(8,128)} %all-gather.2.cloned.1.call-done, s32[2048]{0:T(1024)S(1)} %bitcast_clamp_fusion), kind=kCustom, calls=%fused_computation | custom fusion | bytes 33562624 | tf_op jit(solution)/shard_map/jit(_take)/gather | solution.py:60
  352.4 17.5 %fusion.8 = f32[2048,512]{1,0:T(8,128)S(1)} fusion(f32[2048,2048]{1,0:T(8,128)} %gather_fusion, f32[1,2048,512]{2,1,0:T(8,128)} %param.6), kind=kOutput, calls=%fused_computation.9 | convolution fusion | flops 12884901888 | bytes 25165824 | tf_op jit(solution)/shard_map/dot_general | solution.py:61
  369.9 2.0 copy-done.6
  371.9 6.7 %fusion.4 = f32[1024,512]{1,0:T(8,128)S(1)} fusion(f32[2048,512]{1,0:T(8,128)S(1)} %fusion.8, f32[2048,2048]{1,0:T(8,128)S(1)} %copy-done, s32[]{:T(128)S(6)} %select_n.59), kind=kOutput, calls=%fused_computation.5 | convolution fusion | flops 6442450944 | bytes 14680068 | tf_op jit(solution)/shard_map/dot_general | solution.py:10
  378.6 1.6 collective-permute-start.1
  380.2 3.4 fusion.26
  383.6 1.5 constant_dynamic-update-slice_fusion.1
  385.1 3.4 fusion.23
  388.5 3.4 fusion.25
  391.9 3.6 fusion.27
  395.5 1.5 constant_dynamic-update-slice_fusion
  397.0 12.1 %fusion = f32[2048,256]{1,0:T(8,128)} fusion(f32[2048,256]{1,0:T(8,128)S(1)} %copy-done.4, f32[2048,4096]{0,1:T(8,128)} %all-gather.2.cloned.1.call-done, s32[]{:T(128)S(6)} %select_n.57), kind=kOutput, calls=%fused_computation.1 | convolution fusion | flops 6442450944 | bytes 20971524 | tf_op jit(solution)/shard_map/dot_general | solution.py:10
  410.0 17.3 %collective-permute-done.1 = f32[1024,512]{1,0:T(8,128)S(1)} collective-permute-done((f32[1024,512]{1,0:T(8,128)S(1)}, f32[1024,512]{1,0:T(8,128)S(1)}, u32[]{:S(2)}, u32[]{:S(2)}) %collective-permute-start.1) | collective-permute-done | bytes 2097184 | tf_op jit(solution)/shard_map/ppermute | solution.py:20
  427.2 9.6 %add_negate_fusion = f32[1024,512]{1,0:T(8,128)S(1)} fusion(f32[1024,512]{1,0:T(8,128)S(1)} %collective-permute-done.1, f32[2048,512]{1,0:T(8,128)} %copy-done.6, f32[2048,2048]{1,0:T(8,128)S(1)} %copy-done, s32[]{:T(128)S(6)} %select_n.58), kind=kOutput, calls=%fused_computation.19 | convolution fusion | flops 6443499520 | bytes 16777220 | tf_op jit(solution)/shard_map/dot_general | solution.py:10
  436.9 9.5 %fusion.10 = f32[1024,512]{1,0:T(8,128)} fusion(f32[1024,512]{1,0:T(8,128)S(1)} %add_negate_fusion, f32[1024,4096]{1,0:T(8,128)} %constant_dynamic-update-slice_fusion, s32[]{:T(128)S(6)} %dynamic_slice.38), kind=kOutput, calls=%fused_computation.11 | convolution fusion | flops 3221225472 | bytes 8388612 | tf_op jit(solution)/shard_map/dot_general | solution.py:10
  446.4 1.5 collective-permute-start.8
  447.9 24.4 %collective-permute-done = f32[2048,256]{1,0:T(8,128)} collective-permute-done((f32[2048,256]{1,0:T(8,128)}, f32[2048,256]{1,0:T(8,128)}, u32[]{:S(2)}, u32[]{:S(2)}) %collective-permute-start) | collective-permute-done | bytes 2097184 | tf_op jit(solution)/shard_map/ppermute | solution.py:20
  472.3 12.1 %fusion.14 = f32[2048,256]{1,0:T(8,128)} fusion(f32[2048,256]{1,0:T(8,128)} %collective-permute-done, f32[2048,256]{1,0:T(8,128)} %param.4, f32[2048,4096]{0,1:T(8,128)} %all-gather.2.cloned.1.call-done, s32[]{:T(128)S(6)} %select_n.55), kind=kOutput, calls=%fused_computation.15 | convolution fusion | flops 6442975232 | bytes 23068676 | tf_op jit(solution)/shard_map/dot_general | solution.py:10
  484.4 22.4 %collective-permute-done.8 = f32[1024,512]{1,0:T(8,128)} collective-permute-done((f32[1024,512]{1,0:T(8,128)}, f32[1024,512]{1,0:T(8,128)}, u32[]{:S(2)}, u32[]{:S(2)}) %collective-permute-start.8) | collective-permute-done | bytes 2097184 | tf_op jit(solution)/shard_map/ppermute | solution.py:20
  506.8 13.2 %fusion.17 = f32[1,1024,512]{2,1,0:T(8,128)} fusion(f32[1,1024,512]{2,1,0:T(8,128)S(1)} %copy-done.3, f32[1024,512]{1,0:T(8,128)} %collective-permute-done.8, f32[1024,512]{1,0:T(8,128)S(1)} %add_negate_fusion, f32[1024,4096]{1,0:T(8,128)} %constant_dynamic-update-slice_fusion, s32[]{:T(128)S(6)} %dynamic_slice.36), kind=kOutput, calls=%fused_computation.17 | convolution fusion | flops 3222274048 | bytes 12582916 | tf_op jit(solution)/shard_map/dot_general | solution.py:10
  (23 shorter events, 3.5 us)
Async XLA Ops:
  7.2 318.1 %all-gather.2.cloned.1.call-start = ((), (), s32[]{:S(2)}) async-start(), calls=%async_computation | async-start | bytes 35651584 | tf_op jit(solution)/shard_map/all_gather | solution.py:57
  10.1 82.2 %copy-start.5 = (s32[1,16]{1,0:T(1,128)S(1)}, s32[1,16]{1,0:T(1,128)}, u32[]{:S(2)}) copy-start(s32[1,16]{1,0:T(1,128)} %param.5) | copy-start | bytes 196
  11.9 71.4 %collective-permute-start.2 = (f32[1024,512]{1,0:T(8,128)S(1)}, f32[1024,512]{1,0:T(8,128)S(1)}, u32[]{:S(2)}, u32[]{:S(2)}) collective-permute-start(f32[1024,512]{1,0:T(8,128)S(1)} %dynamic-slice_bitcast_fusion), channel_id=1, source_target_pairs={{0,1},{1,2},{2,3},{4,5},{5,6},{6,7},{8,9},{9,10},{10,11},{12,13},{... | collective-permute-start | bytes 6291464 | tf_op jit(solution)/shard_map/ppermute | solution.py:20
  17.0 71.9 %collective-permute-start.5 = (f32[1024,512]{1,0:T(8,128)S(1)}, f32[1024,512]{1,0:T(8,128)}, u32[]{:S(2)}, u32[]{:S(2)}) collective-permute-start(f32[1024,512]{1,0:T(8,128)S(1)} %dynamic-slice_bitcast_fusion), channel_id=1, source_target_pairs={{1,0},{2,1},{3,2},{5,4},{6,5},{7,6},{9,8},{10,9},{11,10},{13,12},{... | collective-permute-start | bytes 6291464 | tf_op jit(solution)/shard_map/ppermute | solution.py:20
  83.3 6.9 %collective-permute-start.3 = (f32[1024,512]{1,0:T(8,128)S(1)}, f32[1024,512]{1,0:T(8,128)}, u32[]{:S(2)}, u32[]{:S(2)}) collective-permute-start(f32[1024,512]{1,0:T(8,128)S(1)} %collective-permute-done.2), channel_id=1, source_target_pairs={{1,2},{2,3},{5,6},{6,7},{9,10},{10,11},{13,14},{14,15},{17,18},{18... | collective-permute-start | bytes 6291464 | tf_op jit(solution)/shard_map/ppermute | solution.py:20
  88.9 71.9 %collective-permute-start.6 = (f32[1024,512]{1,0:T(8,128)}, f32[1024,512]{1,0:T(8,128)}, u32[]{:S(2)}, u32[]{:S(2)}) collective-permute-start(f32[1024,512]{1,0:T(8,128)} %collective-permute-done.5), channel_id=1, source_target_pairs={{1,0},{2,1},{5,4},{6,5},{9,8},{10,9},{13,12},{14,13},{17,16},{18,1... | collective-permute-start | bytes 6291464 | tf_op jit(solution)/shard_map/ppermute | solution.py:20
  90.2 71.9 %collective-permute-start.4 = (f32[1024,512]{1,0:T(8,128)}, f32[1024,512]{1,0:T(8,128)}, u32[]{:S(2)}, u32[]{:S(2)}) collective-permute-start(f32[1024,512]{1,0:T(8,128)} %collective-permute-done.3), channel_id=1, source_target_pairs={{2,3},{6,7},{10,11},{14,15},{18,19},{22,23},{26,27},{30,31}} | collective-permute-start | bytes 6291464 | tf_op jit(solution)/shard_map/ppermute | solution.py:20
  160.8 219.4 %collective-permute-start.7 = (f32[1024,512]{1,0:T(8,128)}, f32[1024,512]{1,0:T(8,128)}, u32[]{:S(2)}, u32[]{:S(2)}) collective-permute-start(f32[1024,512]{1,0:T(8,128)} %collective-permute-done.6), channel_id=1, source_target_pairs={{1,0},{5,4},{9,8},{13,12},{17,16},{21,20},{25,24},{29,28}} | collective-permute-start | bytes 6291464 | tf_op jit(solution)/shard_map/ppermute | solution.py:20
  352.4 19.6 %copy-start = (f32[2048,2048]{1,0:T(8,128)S(1)}, f32[2048,2048]{1,0:T(8,128)}, u32[]{:S(2)}) copy-start(f32[2048,2048]{1,0:T(8,128)} %gather_fusion) | copy-start | bytes 50331652
  369.9 2.0 copy-start.6
  378.6 5.0 copy-start.1
  378.6 48.6 %collective-permute-start.1 = (f32[1024,512]{1,0:T(8,128)S(1)}, f32[1024,512]{1,0:T(8,128)S(1)}, u32[]{:S(2)}, u32[]{:S(2)}) collective-permute-start(f32[1024,512]{1,0:T(8,128)S(1)} %fusion.4), channel_id=1, source_target_pairs={{0,4},{4,0},{1,5},{5,1},{2,6},{6,2},{3,7},{7,3},{8,12},{12,8},{9,1... | collective-permute-start | bytes 6291464 | tf_op jit(solution)/shard_map/ppermute | solution.py:20
  391.9 5.1 copy-start.4
  409.2 63.1 %collective-permute-start = (f32[2048,256]{1,0:T(8,128)}, f32[2048,256]{1,0:T(8,128)}, u32[]{:S(2)}, u32[]{:S(2)}) collective-permute-start(f32[2048,256]{1,0:T(8,128)} %fusion), channel_id=1, source_target_pairs={{0,4},{4,0},{1,5},{5,1},{2,6},{6,2},{3,7},{7,3},{8,12},{12,8},{9,1... | collective-permute-start | bytes 6291464 | tf_op jit(solution)/shard_map/ppermute | solution.py:20
  436.9 69.9 %copy-start.2 = (f32[1024,512]{1,0:T(8,128)}, f32[1024,512]{1,0:T(8,128)S(1)}, u32[]{:S(2)}) copy-start(f32[1024,512]{1,0:T(8,128)S(1)} %add_negate_fusion) | copy-start | bytes 6291460
  446.4 60.5 %collective-permute-start.8 = (f32[1024,512]{1,0:T(8,128)}, f32[1024,512]{1,0:T(8,128)}, u32[]{:S(2)}, u32[]{:S(2)}) collective-permute-start(f32[1024,512]{1,0:T(8,128)} %fusion.10), channel_id=1, source_target_pairs={{0,4},{4,0},{1,5},{5,1},{2,6},{6,2},{3,7},{7,3},{8,12},{12,8},{9,1... | collective-permute-start | bytes 6291464 | tf_op jit(solution)/shard_map/ppermute | solution.py:20
  447.9 58.9 %copy-start.3 = (f32[1,1024,512]{2,1,0:T(8,128)S(1)}, f32[1,1024,512]{2,1,0:T(8,128)}, u32[]{:S(2)}) copy-start(f32[1,1024,512]{2,1,0:T(8,128)} %param.7) | copy-start | bytes 6291460
Sparse Core Ops, SparseCore 0:
  10.2 314.9 all-gather.1

commit v2 on v0

v2 whole, which is shorter than its diff:
```python
import functools

import jax
import jax.numpy as jnp
import numpy as np
from jax import lax
from jax.experimental import pallas as pl
from jax.experimental.pallas import tpu as pltpu
from jax.sharding import PartitionSpec as P

BLK = 128
VMEM_BYTES = 58 * 1024 * 1024


def halves(value):
    high = value.astype(jnp.bfloat16)
    low = (value - high.astype(jnp.float32)).astype(jnp.bfloat16)
    return high, low


def dot(left, right):
    return jnp.dot(left, right, preferred_element_type=jnp.float32)


def contract_rows(left, right):
    return lax.dot_general(
        left,
        right,
        (((0,), (0,)), ((), ())),
        precision=lax.Precision.HIGH,
        preferred_element_type=jnp.float32,
    )


class Layout:
    def __init__(self, rows, leaves, cols, half, width):
        self.leaves, self.cols, self.half, self.width = leaves, cols, half, width
        self.part = half // leaves
        self.span = width * cols
        self.counts, self.holder, self.source = [], [], []
        for r in range(rows):
            count = [min(leaves, (q * half + half - 1) // self.span + 1) for q in (2 * r + 1, 2 * (rows - 1 - r))]
            assert count[0] + count[1] <= leaves + 1
            free = list(range(count[1], leaves))
            moved = [leaf for leaf in range(1, count[0]) if leaf not in free]
            slot = {leaf: leaf for leaf in range(1, count[0]) if leaf in free}
            left = [s for s in free if s not in slot]
            slot.update(zip(moved, left))
            self.counts.append(count)
            self.holder.append(slot)
        table = np.full((rows, 2, leaves, leaves), -1, np.int32)
        for r in range(rows):
            for j in range(leaves):
                table[r, 0, 0, j] = j * (leaves + 1) + leaves
                for leaf, slot in self.holder[r].items():
                    table[r, 0, leaf, j] = slot * (leaves + 1) + j
                for leaf in range(self.counts[r][1]):
                    table[r, 1, leaf, j] = leaf * (leaves + 1) + j
        self.table = table


def panel_kernel(lay, pat, tab, shift, *refs):
    count = len(refs) - 9
    gathered = refs[:count]
    p_ref, y_ref, t, th, tl, image, turned_high, turned_low, sems = refs[count:]
    number, parts, part = t.shape[0], t.shape[2], t.shape[3]
    half = parts * part

    def place(k):
        first = pat[k] * BLK
        leaf = first // lay.span
        rest = first - leaf * lay.span
        col = rest // lay.width
        return leaf, col, (rest - col * lay.width) // BLK

    def valid(k, s):
        return tab[s, place(k)[0], 0] >= 0

    @pl.loop(0, number)
    def _(k):
        leaf, col, sub = place(k)
        for s in range(2):
            here = tab[s, leaf, 0] >= 0

            @pl.when(here)
            def _():
                for j in range(parts):
                    entry = tab[s, leaf, j]
                    slot = entry // (parts + 1)
                    position = entry - slot * (parts + 1)
                    for which in range(count):

                        @pl.when(sub == which)
                        def _():
                            pltpu.make_async_copy(
                                gathered[which].at[slot * lay.cols + col, position],
                                t.at[k, s, j],
                                sems.at[k, s],
                            ).start()

            @pl.when(jnp.logical_not(here))
            def _():
                t[k, s] = jnp.zeros(t.shape[2:], t.dtype)

    image[...] = jnp.zeros_like(image)

    @pl.loop(0, number // 2)
    def _(kp):
        rows = pl.ds(pl.multiple_of(kp * 2 * BLK, 2 * BLK), 2 * BLK)
        p_high, p_low = halves(p_ref[rows, :])
        stacked = jnp.concatenate([p_high, p_low, p_high], axis=0)
        for s in range(2):
            for m in range(2):

                @pl.when(valid(2 * kp + m, s))
                def _():
                    pltpu.make_async_copy(t.at[2 * kp + m, s], t.at[2 * kp + m, s], sems.at[2 * kp + m, s]).wait()

            @pl.when(jnp.logical_or(valid(2 * kp, s), valid(2 * kp + 1, s)))
            def _():
                @pl.loop(0, parts)
                def _(j):
                    both = jnp.concatenate([t[2 * kp, s, j], t[2 * kp + 1, s, j]], axis=1)
                    high, low = halves(both)
                    th[kp, s, j] = high
                    tl[kp, s, j] = low
                    image[s, j] += dot(jnp.concatenate([high, high, low], axis=1), stacked)

    for s in range(2):

        @pl.loop(0, parts)
        def _(j):
            high, low = halves(image[s, j].T)
            turned_high[s, j] = high
            turned_low[s, j] = low

    @pl.loop(0, number // 2)
    def _(kp):
        def term(s, j):
            high, low = th[kp, s, j], tl[kp, s, j]
            left = jnp.concatenate([turned_high[s, j], turned_low[s, j], turned_high[s, j]], axis=1)
            return dot(left, jnp.concatenate([high, high, low], axis=0))

        out = y_ref.at[lax.rem(kp + shift[0], number // 2)]
        out[...] = jnp.zeros(out.shape, out.dtype)
        for s in range(2):

            @pl.when(jnp.logical_or(valid(2 * kp, s), valid(2 * kp + 1, s)))
            def _():
                total = term(s, 0)
                for j in range(1, parts):
                    total = total + term(s, j)
                out[...] += total.T


def panel_product(lay, pattern, table, shift, gathered, normed):
    number, wide = pattern.shape[0], normed.shape[1]
    half, part, parts = lay.half, lay.part, lay.leaves
    any_space = pl.BlockSpec(memory_space=pl.ANY)
    vmem = pl.BlockSpec(memory_space=pltpu.VMEM)
    smem = pl.BlockSpec(memory_space=pltpu.SMEM)
    return pl.pallas_call(
        functools.partial(panel_kernel, lay),
        out_shape=jax.ShapeDtypeStruct((number // 2, 2 * BLK, wide), jnp.float32),
        in_specs=[smem] * 3 + [any_space] * len(gathered) + [vmem],
        out_specs=vmem,
        scratch_shapes=[
            pltpu.VMEM((number, 2, parts, part, BLK), jnp.float32),
            pltpu.VMEM((number // 2, 2, parts, part, 2 * BLK), jnp.bfloat16),
            pltpu.VMEM((number // 2, 2, parts, part, 2 * BLK), jnp.bfloat16),
            pltpu.VMEM((2, parts, part, wide), jnp.float32),
            pltpu.VMEM((2, parts, wide, part), jnp.bfloat16),
            pltpu.VMEM((2, parts, wide, part), jnp.bfloat16),
            pltpu.SemaphoreType.DMA((number, 2)),
        ],
        compiler_params=pltpu.CompilerParams(vmem_limit_bytes=VMEM_BYTES),
        cost_estimate=pl.CostEstimate(
            flops=12 * 2 * half * number * BLK * wide,
            bytes_accessed=4 * (2 * half * number * BLK + 2 * number * BLK * wide),
            transcendentals=0,
        ),
    )(pattern, table, shift, *gathered, normed)


def top_kernel(lay, tab, info, g_ref, own_ref, out_ref, own_turned):
    blocks, _, part, _ = g_ref.shape
    parts = lay.leaves
    for s in range(2):

        @pl.loop(0, parts)
        def _(j):
            high, low = halves(own_ref[s, j].T)
            own_turned[s, j] = jnp.concatenate([high, low, high], axis=1)

    @pl.loop(0, blocks // 2)
    def _(pair):
        block = 2 * pair
        leaf = block // lay.cols
        col = block - leaf * lay.cols
        out = out_ref.at[lax.rem(pair + info[0], blocks // 2)]
        out[...] = jnp.zeros(out.shape, out.dtype)
        for s in range(2):

            @pl.when(jnp.logical_and(tab[s, leaf, 0] >= 0, tab[s, info[1], 0] >= 0))
            def _():
                total = None
                for j in range(parts):
                    entry = tab[s, leaf, j]
                    slot = entry // (parts + 1)
                    position = entry - slot * (parts + 1)
                    at = slot * lay.cols + col
                    both = jnp.concatenate([g_ref[at, position], g_ref[at + 1, position]], axis=1)
                    high, low = halves(both)
                    term = dot(own_turned[s, j], jnp.concatenate([high, high, low], axis=0))
                    total = term if total is None else total + term
                out[...] += total.T


def top_product(lay, table, info, gathered, own):
    blocks = gathered.shape[0]
    parts, part, width = lay.leaves, lay.part, lay.width
    vmem = pl.BlockSpec(memory_space=pltpu.VMEM)
    smem = pl.BlockSpec(memory_space=pltpu.SMEM)
    return pl.pallas_call(
        functools.partial(top_kernel, lay),
        out_shape=jax.ShapeDtypeStruct((blocks // 2, 2 * BLK, width), jnp.float32),
        in_specs=[smem, smem, vmem, vmem],
        out_specs=vmem,
        scratch_shapes=[pltpu.VMEM((2, parts, width, 3 * part), jnp.bfloat16)],
        compiler_params=pltpu.CompilerParams(vmem_limit_bytes=VMEM_BYTES),
        cost_estimate=pl.CostEstimate(
            flops=6 * 2 * lay.half * blocks * BLK * width,
            bytes_accessed=4 * gathered.size,
            transcendentals=0,
        ),
    )(table, info, gathered, own)


def exchange(value, axis, away):
    count = lax.axis_size(axis)
    return lax.ppermute(value, axis, [(i, (i + away) % count) for i in range(count)])


def sum_rotated(value):
    rows = lax.axis_size("row")
    each = value.shape[0] // rows
    received = [exchange(value[(away - 1) * each : away * each], "row", away) for away in range(1, rows)]
    total = value[(rows - 1) * each :]
    for term in received:
        total = total + term
    return total


def per_device(lay, top_inverse, pattern, panel, diag_inverse):
    rows, cols, leaves = (lax.axis_size(axis) for axis in ("row", "col", "leaf"))
    me_row, me_col, me_leaf = (lax.axis_index(axis) for axis in ("row", "col", "leaf"))
    half, width, parts, part = lay.half, lay.width, lay.leaves, lay.part
    normed = panel[0]

    table = jnp.asarray(lay.table)[me_row]
    second = jnp.asarray([count[1] for count in lay.counts], jnp.int32)[me_row]
    is_moved = np.zeros((rows, leaves), bool)
    pairs = []
    for r in range(rows):
        for leaf, slot in lay.holder[r].items():
            if leaf != slot:
                is_moved[r, slot] = True
                pairs.append((leaf * rows + r, slot * rows + r))
    moved_here = jnp.asarray(is_moved)[me_row, me_leaf]
    gathered, own = [], []
    for sub in range(width // BLK):
        lanes = slice(sub * BLK, (sub + 1) * BLK)
        lower, upper = top_inverse[half:, lanes], top_inverse[:half, lanes]
        swapped = lax.ppermute(upper, "row", [(r, rows - 1 - r) for r in range(rows)])
        moved = lax.ppermute(lower, ("leaf", "row"), pairs) if pairs else lower
        whole = jnp.where(me_leaf < second, swapped, jnp.where(moved_here, moved, lower))
        extra = lower[:part]
        for j in range(1, parts):
            sent = lax.ppermute(lower[j * part : (j + 1) * part], "leaf", [(0, j)])
            extra = jnp.where(me_leaf == j, sent, extra)
        held = jnp.concatenate([whole.reshape(parts, part, BLK), extra[None]], axis=0)
        gathered.append(lax.all_gather(held, ("leaf", "col"), axis=0, tiled=False))
        own.append(jnp.stack([lower, swapped]))
    own = jnp.concatenate(own, axis=2).reshape(2, parts, part, width)

    own_rows = lax.dynamic_slice_in_dim(normed, me_row * (normed.shape[0] // rows), normed.shape[0] // rows, 0)
    right, left = [own_rows], [own_rows]
    for step in range(cols - 1):
        if step == 1:
            right[-1], left[-1], gathered[-1] = lax.optimization_barrier((right[-1], left[-1], gathered[-1]))
        right.append(lax.ppermute(right[-1], "col", [(i, i + 1) for i in range(step, cols - 1)]))
        left.append(lax.ppermute(left[-1], "col", [(i, i - 1) for i in range(1, cols - step)]))

    blocks = gathered[0].shape[0] // 2
    info = jnp.stack([(rows - 1 - me_row) * (blocks // rows), me_leaf]).astype(jnp.int32)
    tops = [sum_rotated(top_product(lay, table, info, part_of, own)) for part_of in gathered]
    tops = [top.reshape(-1, 1, BLK, width) for top in tops]
    sigma_top = jnp.concatenate(tops, axis=1).reshape(-1, width)

    pairs_of = pattern.shape[1] // 2
    shift = ((rows - 1 - me_row) * (pairs_of // rows)).astype(jnp.int32)[None]
    product = panel_product(lay, pattern[0], table, shift, gathered, normed)
    sigma_panel = -sum_rotated(product).reshape(-1, normed.shape[1])

    updates = [contract_rows(own_rows, sigma_panel)]
    for t in range(1, cols):
        piece = jnp.where(me_col >= t, right[t], left[cols - t])
        updates.append(contract_rows(piece, sigma_panel))
    ordered = jnp.stack(updates[::-1] + updates[::-1])
    first = (cols - 1 - me_col + (me_row + 1) * (cols // rows)) % cols
    update = sum_rotated(lax.dynamic_slice_in_dim(ordered, first, cols, 0))
    sigma_diag = diag_inverse[0] - update.reshape(diag_inverse.shape[1:])
    return (sigma_top, sigma_panel[None], sigma_diag[None])


def solution(mesh):
    placed = (
        P("row", ("leaf", "col")),
        P("leaf", None),
        P("leaf", None, "col"),
        P("leaf", "row", "col"),
    )

    def whole(top_inverse, pattern, panel, diag_inverse):
        rows, leaves, cols = (mesh.shape[axis] for axis in ("row", "leaf", "col"))
        size = top_inverse.shape[0]
        lay = Layout(rows, leaves, cols, size // rows // 2, size // leaves // cols)
        return jax.shard_map(
            functools.partial(per_device, lay),
            mesh=mesh,
            in_specs=placed,
            out_specs=(P("row", ("leaf", "col")), P("leaf", "row", "col"), P("leaf", "row", "col")),
            check_vma=False,
        )(top_inverse, pattern, panel, diag_inverse)

    return whole
```

time: 534 us -> 479 us (0.90)
  matrix products: 112 us -> 13.7 us
  Pallas kernels: 0 us -> 66.9 us
  waiting for transfers between devices: 369 us -> 305 us
  starting transfers between devices: 0.21 us -> 36 us
  local copies, waits for them, and re-layouts: 35.4 us -> 21 us
  other arithmetic: 3.57 us -> 16.8 us
    ppermute x0 -> x20, waiting for transfers between devices: none -> 176 us  [the longest x3 75.1 us: per_device(): lax.ppermute(right[-1], 'col', [(i, i + 1) for i in range(step, cols - 1)])]
    reduce_scatter x3 -> x0, waiting for transfers between devices: 131 us -> none  [the longest x1 55.4 us: per_device(): lax.psum_scatter(-contract_rows(columns, image), 'row', scatter_dimension...]
    all_gather x2, waiting for transfers between devices: 238 us -> 129 us  [per_device(): gathered.append(lax.all_gather(held, ('leaf', 'col'), axis=0, tiled=False))]
    pallas_call x0 -> x3, Pallas kernels: none -> 66.9 us  [the longest x1 38.5 us: panel_product(): pl.pallas_call(functools.partial(panel_kernel, lay), out_shape=jax.ShapeD...]
    dot_general x3 -> x4, matrix products: 78.3 us -> 13.7 us  [contract_rows(): lax.dot_general(left, right, (((0,), (0,)), ((), ())), precision=lax.Prec...]
    ppermute x0 -> x20, starting transfers between devices: none -> 35.9 us  [the longest x6 12.3 us: per_device(): sent = lax.ppermute(lower[j * part:(j + 1) * part], 'leaf', [(0, j)])]
    dot_general x1 -> x0, matrix products: 33.7 us -> none  [per_device(): jnp.dot(selected, normed, precision=exact, preferred_element_type=jnp.flo...]
    gather x1 -> x0, local copies, waits for them, and re-layouts: 27.9 us -> none  [per_device(): selected = jnp.take(rows_here, wanted, axis=1)]
  transfers between devices with their start and end apart: 5 -> 22, of which waited for: 5 -> 10; matrix products, arithmetic and copies ran while one was open for 24% -> 8% of each run, Pallas kernels for 0% -> 14%
where the time goes in v2:
time: 479 us; the launch traced here: 474 us
  waiting for transfers between devices  305 us (64%)
  Pallas kernels  66.9 us (14%)
  starting transfers between devices  36 us (8%)
  local copies, waits for them, and re-layouts  21 us (4%)
  other arithmetic  16.8 us (4%)
  between operations  15.1 us (3%)
  matrix products  13.7 us (3%)
    all_gather x2, waiting for transfers between devices, per_device(): gathered.append(lax.all_gather(held, ('leaf', 'col'), axis=0, tiled=False))  129 us
    ppermute x3, waiting for transfers between devices, per_device(): lax.ppermute(right[-1], 'col', [(i, i + 1) for i in range(step, cols - 1)])  75.1 us
    ppermute x4, waiting for transfers between devices, exchange(): lax.ppermute(value, axis, [(i, (i + away) % count) for i in range(count)])  69.8 us
    pallas_call x1, Pallas kernels, panel_product(): pl.pallas_call(functools.partial(panel_kernel, lay), out_shape=jax.ShapeD...  38.5 us
    pallas_call x2, Pallas kernels, top_product(): pl.pallas_call(functools.partial(top_kernel, lay), out_shape=jax.ShapeDty...  28.5 us
    ppermute x3, waiting for transfers between devices, per_device(): lax.ppermute(left[-1], 'col', [(i, i - 1) for i in range(1, cols - step)])  24.4 us
    dot_general x4, matrix products, contract_rows(): lax.dot_general(left, right, (((0,), (0,)), ((), ())), precision=lax.Prec...  13.7 us
    ppermute x6, starting transfers between devices, per_device(): sent = lax.ppermute(lower[j * part:(j + 1) * part], 'leaf', [(0, j)])  12.3 us
  transfers between devices with their start and end apart: 22, of which 10 were waited for; matrix products, arithmetic and copies ran while one was open for 8% of the time, Pallas kernels for 14%

profile of v2, /device:TPU:0, one launch (start us, length us, event | category | flops | bytes accessed | tf_op | source)
XLA Modules:
  0.0 474.4 jit_solution(1647075406131333772)
XLA Ops:
  7.2 2.2 fusion.19
  9.4 3.0 collective-permute-start
  14.6 2.4 collective-permute-start.2
  18.7 1.9 collective-permute-start.4
  22.6 1.9 collective-permute-done
  28.9 3.3 collective-permute-start.10
  36.1 2.8 collective-permute-done.11
  44.0 4.8 %collective-permute-start.7 = (f32[1024,512]{1,0:T(8,128)S(1)}, f32[1024,512]{1,0:T(8,128)}, u32[]{:S(2)}, u32[]{:S(2)}) collective-permute-start(f32[1024,512]{1,0:T(8,128)S(1)} %dynamic-slice_bitcast_fusion), channel_id=1, source_target_pairs={{0,1},{1,2},{2,3},{4,5},{5,6},{6,7},{8,9},{9,10},{10,11},{12,13},{... | collective-permute-start | bytes 6291464 | tf_op jit(solution)/shard_map/ppermute | solution.py:291
  50.7 75.1 %collective-permute-done.7 = f32[1024,512]{1,0:T(8,128)} collective-permute-done((f32[1024,512]{1,0:T(8,128)S(1)}, f32[1024,512]{1,0:T(8,128)}, u32[]{:S(2)}, u32[]{:S(2)}) %collective-permute-start.7) | collective-permute-done | bytes 2097184 | tf_op jit(solution)/shard_map/ppermute | solution.py:291
  125.8 24.4 %collective-permute-done.8 = f32[1024,512]{1,0:T(8,128)} collective-permute-done((f32[1024,512]{1,0:T(8,128)S(1)}, f32[1024,512]{1,0:T(8,128)}, u32[]{:S(2)}, u32[]{:S(2)}) %collective-permute-start.8) | collective-permute-done | bytes 2097184 | tf_op jit(solution)/shard_map/ppermute | solution.py:292
  150.2 13.3 %all-gather.7.cloned.1.call-done = f32[80,256,128]{2,1,0:T(8,128)} async-done(((f32[5,256,128]{2,1,0:T(8,128)}), f32[80,256,128]{2,1,0:T(8,128)}) %all-gather.7.cloned.1.call-update) | async-done | bytes 10485776 | tf_op jit(solution)/shard_map/all_gather | solution.py:282
  163.6 1.9 collective-permute-start.15
  166.8 115.9 %all-gather.5.cloned.1.call-done = f32[80,256,128]{2,1,0:T(8,128)} async-done(((f32[5,256,128]{2,1,0:T(8,128)}), f32[80,256,128]{2,1,0:T(8,128)}) %all-gather.5.cloned.1.call-update) | async-done | bytes 10485776 | tf_op jit(solution)/shard_map/all_gather | solution.py:282
  282.7 38.5 %shard_map.96 = f32[8,256,512]{2,1,0:T(8,128)} custom-call(s32[16]{0:T(128)} %bitcast.66, s32[2,4,4]{2,1,0:T(4,128)} %dynamic-slice_bitcast_fusion.1.tab, s32[1]{0:T(128)} %bitcast.1.shift, f32[16,5,256,128]{3,2,1,0:T(8,128)} %bitcast.64, f32[16,5,256,128]{3,2,1,0:T(8,128)} %bitcast.62, f32[2048,512]{1,0:T(8,128)} %bitcast.61), custom_call_target="tpu_custom_call" | custom-call | flops 25769803776 | bytes 25165824 | tf_op jit(solution)/shard_map/pallas_call | solution.py:162
  321.2 3.1 slice.93
  324.3 2.0 collective-permute-start.16
  328.4 2.7 maximum_maximum_fusion
  331.1 14.3 %shard_map.94 = f32[8,256,256]{2,1,0:T(8,128)} custom-call(s32[2,4,4]{2,1,0:T(4,128)} %dynamic-slice_bitcast_fusion.1.tab, s32[2]{0:T(128)} %pad_add_fusion.info, f32[16,5,256,128]{3,2,1,0:T(8,128)} %bitcast.65, f32[2,4,256,256]{3,2,1,0:T(8,128)} %bitcast.54), custom_call_target="tpu_custom_call" | custom-call | flops 6442450944 | bytes 10485760 | tf_op jit(solution)/shard_map/pallas_call | solution.py:224
  345.4 2.3 slice.89
  347.7 2.0 collective-permute-start.6
  349.7 21.5 %collective-permute-done.14 = f32[4,256,512]{2,1,0:T(8,128)} collective-permute-done((f32[4,256,512]{2,1,0:T(8,128)}, f32[4,256,512]{2,1,0:T(8,128)}, u32[]{:S(2)}, u32[]{:S(2)}) %collective-permute-start.14) | collective-permute-done | bytes 2097184 | tf_op jit(solution)/shard_map/ppermute | solution.py:241
  371.2 2.1 fusion
  373.3 4.4 constant_dynamic-update-slice_fusion.7
  377.7 3.6 constant_dynamic-update-slice_fusion.6
  381.4 3.8 constant_dynamic-update-slice_fusion.5
  385.2 1.9 constant_dynamic-update-slice_fusion.4
  387.4 3.3 copy-done.5
  392.2 14.2 %shard_map.95 = f32[8,256,256]{2,1,0:T(8,128)} custom-call(s32[2,4,4]{2,1,0:T(4,128)} %dynamic-slice_bitcast_fusion.1.tab, s32[2]{0:T(128)} %pad_add_fusion.info, f32[16,5,256,128]{3,2,1,0:T(8,128)} %bitcast.63, f32[2,4,256,256]{3,2,1,0:T(8,128)} %bitcast.55), custom_call_target="tpu_custom_call" | custom-call | flops 6442450944 | bytes 10485760 | tf_op jit(solution)/shard_map/pallas_call | solution.py:224
  406.4 2.3 slice.91
  408.7 2.0 collective-permute-start.13
  412.2 48.3 %collective-permute-done.13 = f32[4,256,256]{2,1,0:T(8,128)} collective-permute-done((f32[4,256,256]{2,1,0:T(8,128)}, f32[4,256,256]{2,1,0:T(8,128)}, u32[]{:S(2)}, u32[]{:S(2)}) %collective-permute-start.13) | collective-permute-done | bytes 1048608 | tf_op jit(solution)/shard_map/ppermute | solution.py:241
  463.5 2.2 dynamic-slice_add_fusion
  (76 shorter events, 31.8 us)
Async XLA Ops:
  7.2 13.5 %copy-start.12 = (s32[2]{0:T(128)S(1)}, s32[2]{0:T(128)}, u32[]{:S(2)}) copy-start(s32[2]{0:T(128)} %constant.45.clone) | copy-start | bytes 28
  7.2 14.8 %copy-start.11 = (pred[2,4]{1,0:T(4,128)(4,1)S(1)}, pred[2,4]{1,0:T(4,128)(4,1)}, u32[]{:S(2)}) copy-start(pred[2,4]{1,0:T(4,128)(4,1)} %constant.46.clone) | copy-start | bytes 28
  7.2 6.7 %copy-start.3 = (f32[2048,256]{1,0:T(8,128)S(1)}, f32[2048,256]{1,0:T(8,128)}, u32[]{:S(2)}) copy-start(f32[2048,256]{1,0:T(8,128)} %param.7) | copy-start | bytes 6291460
  7.2 156.4 %all-gather.7.cloned.1.call-start = ((), (), s32[]{:S(2)}) async-start(), calls=%async_computation.1 | async-start | bytes 11141120 | tf_op jit(solution)/shard_map/all_gather | solution.py:282
  9.4 15.1 %collective-permute-start = (f32[1024,128]{1,0:T(8,128)}, f32[1024,128]{1,0:T(8,128)S(1)}, u32[]{:S(2)}, u32[]{:S(2)}) collective-permute-start(f32[1024,128]{1,0:T(8,128)} %get-tuple-element.15), channel_id=1, source_target_pairs={{0,4},{4,0},{1,5},{5,1},{2,6},{6,2},{3,7},{7,3},{8,12},{12,8},{9,1... | collective-permute-start | bytes 1572872 | tf_op jit(solution)/shard_map/ppermute | solution.py:274
  12.4 12.1 %collective-permute-start.1 = (f32[1024,128]{1,0:T(8,128)S(1)}, f32[1024,128]{1,0:T(8,128)}, u32[]{:S(2)}, u32[]{:S(2)}) collective-permute-start(f32[1024,128]{1,0:T(8,128)S(1)} %get-tuple-element.14), channel_id=1, source_target_pairs={{8,24},{9,25},{10,26},{11,27}} | collective-permute-start | bytes 1572872 | tf_op jit(solution)/shard_map/ppermute | solution.py:275
  14.6 14.2 %collective-permute-start.2 = (f32[256,128]{1,0:T(8,128)}, f32[256,128]{1,0:T(8,128)S(1)}, u32[]{:S(2)}, u32[]{:S(2)}) collective-permute-start(f32[256,128]{1,0:T(8,128)} %get-tuple-element.22), channel_id=1, source_target_pairs={{0,24},{1,25},{2,26},{3,27},{4,28},{5,29},{6,30},{7,31}} | collective-permute-start | bytes 393224 | tf_op jit(solution)/shard_map/ppermute | solution.py:279
  17.0 11.8 %collective-permute-start.3 = (f32[256,128]{1,0:T(8,128)}, f32[256,128]{1,0:T(8,128)S(1)}, u32[]{:S(2)}, u32[]{:S(2)}) collective-permute-start(f32[256,128]{1,0:T(8,128)} %get-tuple-element.21), channel_id=1, source_target_pairs={{0,16},{1,17},{2,18},{3,19},{4,20},{5,21},{6,22},{7,23}} | collective-permute-start | bytes 393224 | tf_op jit(solution)/shard_map/ppermute | solution.py:279
  18.7 10.2 %collective-permute-start.4 = (f32[256,128]{1,0:T(8,128)S(1)}, f32[256,128]{1,0:T(8,128)}, u32[]{:S(2)}, u32[]{:S(2)}) collective-permute-start(f32[256,128]{1,0:T(8,128)S(1)} %get-tuple-element.20), channel_id=1, source_target_pairs={{0,8},{1,9},{2,10},{3,11},{4,12},{5,13},{6,14},{7,15}} | collective-permute-start | bytes 393224 | tf_op jit(solution)/shard_map/ppermute | solution.py:279
  26.4 13.2 %collective-permute-start.5 = (f32[1024,128]{1,0:T(8,128)S(1)}, f32[1024,128]{1,0:T(8,128)S(1)}, u32[]{:S(2)}, u32[]{:S(2)}) collective-permute-start(f32[1024,128]{1,0:T(8,128)S(1)} %get-tuple-element.12), channel_id=1, source_target_pairs={{0,4},{4,0},{1,5},{5,1},{2,6},{6,2},{3,7},{7,3},{8,12},{12,8},{9,1... | collective-permute-start | bytes 1572872 | tf_op jit(solution)/shard_map/ppermute | solution.py:274
  28.1 11.5 %collective-permute-start.9 = (f32[1024,128]{1,0:T(8,128)S(1)}, f32[1024,128]{1,0:T(8,128)S(1)}, u32[]{:S(2)}, u32[]{:S(2)}) collective-permute-start(f32[1024,128]{1,0:T(8,128)S(1)} %get-tuple-element.13), channel_id=1, source_target_pairs={{8,24},{9,25},{10,26},{11,27}} | collective-permute-start | bytes 1572872 | tf_op jit(solution)/shard_map/ppermute | solution.py:275
  28.9 7.2 %collective-permute-start.10 = (f32[256,128]{1,0:T(8,128)S(1)}, f32[256,128]{1,0:T(8,128)S(1)}, u32[]{:S(2)}, u32[]{:S(2)}) collective-permute-start(f32[256,128]{1,0:T(8,128)S(1)} %get-tuple-element.18), channel_id=1, source_target_pairs={{0,24},{1,25},{2,26},{3,27},{4,28},{5,29},{6,30},{7,31}} | collective-permute-start | bytes 393224 | tf_op jit(solution)/shard_map/ppermute | solution.py:279
  32.2 6.7 %collective-permute-start.11 = (f32[256,128]{1,0:T(8,128)S(1)}, f32[256,128]{1,0:T(8,128)S(1)}, u32[]{:S(2)}, u32[]{:S(2)}) collective-permute-start(f32[256,128]{1,0:T(8,128)S(1)} %get-tuple-element.17), channel_id=1, source_target_pairs={{0,16},{1,17},{2,18},{3,19},{4,20},{5,21},{6,22},{7,23}} | collective-permute-start | bytes 393224 | tf_op jit(solution)/shard_map/ppermute | solution.py:279
  33.5 5.4 %collective-permute-start.12 = (f32[256,128]{1,0:T(8,128)S(1)}, f32[256,128]{1,0:T(8,128)S(1)}, u32[]{:S(2)}, u32[]{:S(2)}) collective-permute-start(f32[256,128]{1,0:T(8,128)S(1)} %get-tuple-element.19), channel_id=1, source_target_pairs={{0,8},{1,9},{2,10},{3,11},{4,12},{5,13},{6,14},{7,15}} | collective-permute-start | bytes 393224 | tf_op jit(solution)/shard_map/ppermute | solution.py:279
  41.3 241.4 %all-gather.5.cloned.1.call-start = ((), (), s32[]{:S(2)}) async-start(), calls=%async_computation | async-start | bytes 11141120 | tf_op jit(solution)/shard_map/all_gather | solution.py:282
  42.2 7.9 %copy-start.10 = (s32[2,2,4,4]{3,2,1,0:T(4,128)S(1)}, s32[2,2,4,4]{3,2,1,0:T(4,128)}, u32[]{:S(2)}) copy-start(s32[2,2,4,4]{3,2,1,0:T(4,128)} %constant.44.clone) | copy-start | bytes 772
  44.0 277.2 %copy-start.1 = (f32[1024,512]{1,0:T(8,128)}, f32[1024,512]{1,0:T(8,128)S(1)}, u32[]{:S(2)}) copy-start(f32[1024,512]{1,0:T(8,128)S(1)} %dynamic-slice_bitcast_fusion) | copy-start | bytes 6291460
  44.0 81.8 %collective-permute-start.7 = (f32[1024,512]{1,0:T(8,128)S(1)}, f32[1024,512]{1,0:T(8,128)}, u32[]{:S(2)}, u32[]{:S(2)}) collective-permute-start(f32[1024,512]{1,0:T(8,128)S(1)} %dynamic-slice_bitcast_fusion), channel_id=1, source_target_pairs={{0,1},{1,2},{2,3},{4,5},{5,6},{6,7},{8,9},{9,10},{10,11},{12,13},{... | collective-permute-start | bytes 6291464 | tf_op jit(solution)/shard_map/ppermute | solution.py:291
  48.8 101.4 %collective-permute-start.8 = (f32[1024,512]{1,0:T(8,128)S(1)}, f32[1024,512]{1,0:T(8,128)}, u32[]{:S(2)}, u32[]{:S(2)}) collective-permute-start(f32[1024,512]{1,0:T(8,128)S(1)} %dynamic-slice_bitcast_fusion), channel_id=1, source_target_pairs={{1,0},{2,1},{3,2},{5,4},{6,5},{7,6},{9,8},{10,9},{11,10},{13,12},{... | collective-permute-start | bytes 6291464 | tf_op jit(solution)/shard_map/ppermute | solution.py:292
  163.6 160.8 %collective-permute-start.15 = (f32[1024,512]{1,0:T(8,128)}, f32[1024,512]{1,0:T(8,128)}, u32[]{:S(2)}, u32[]{:S(2)}) collective-permute-start(f32[1024,512]{1,0:T(8,128)} %collective-permute-done.7), channel_id=1, source_target_pairs={{1,2},{2,3},{5,6},{6,7},{9,10},{10,11},{13,14},{14,15},{17,18},{18... | collective-permute-start | bytes 6291464 | tf_op jit(solution)/shard_map/ppermute | solution.py:291
  165.5 160.8 %collective-permute-start.17 = (f32[1024,512]{1,0:T(8,128)}, f32[1024,512]{1,0:T(8,128)}, u32[]{:S(2)}, u32[]{:S(2)}) collective-permute-start(f32[1024,512]{1,0:T(8,128)} %collective-permute-done.8), channel_id=1, source_target_pairs={{1,0},{2,1},{5,4},{6,5},{9,8},{10,9},{13,12},{14,13},{17,16},{18,1... | collective-permute-start | bytes 6291464 | tf_op jit(solution)/shard_map/ppermute | solution.py:292
  321.2 7.2 %copy-start.9 = (f32[1024,128]{1,0:T(8,128)S(1)}, f32[1024,128]{1,0:T(8,128)}, u32[]{:S(2)}) copy-start(f32[1024,128]{1,0:T(8,128)} %copy-done.8) | copy-start | bytes 1572868
  324.3 46.9 %collective-permute-start.14 = (f32[4,256,512]{2,1,0:T(8,128)}, f32[4,256,512]{2,1,0:T(8,128)}, u32[]{:S(2)}, u32[]{:S(2)}) collective-permute-start(f32[4,256,512]{2,1,0:T(8,128)} %slice.93), channel_id=1, source_target_pairs={{0,4},{4,0},{1,5},{5,1},{2,6},{6,2},{3,7},{7,3},{8,12},{12,8},{9,1... | collective-permute-start | bytes 6291464 | tf_op jit(solution)/shard_map/ppermute | solution.py:241
  324.3 49.0 %collective-permute-start.16 = (f32[1024,512]{1,0:T(8,128)}, f32[1024,512]{1,0:T(8,128)}, u32[]{:S(2)}, u32[]{:S(2)}) collective-permute-start(f32[1024,512]{1,0:T(8,128)} %collective-permute-done.15), channel_id=1, source_target_pairs={{2,3},{6,7},{10,11},{14,15},{18,19},{22,23},{26,27},{30,31}} | collective-permute-start | bytes 6291464 | tf_op jit(solution)/shard_map/ppermute | solution.py:291
  326.3 55.0 %collective-permute-start.18 = (f32[1024,512]{1,0:T(8,128)}, f32[1024,512]{1,0:T(8,128)}, u32[]{:S(2)}, u32[]{:S(2)}) collective-permute-start(f32[1024,512]{1,0:T(8,128)} %collective-permute-done.17), channel_id=1, source_target_pairs={{1,0},{5,4},{9,8},{13,12},{17,16},{21,20},{25,24},{29,28}} | collective-permute-start | bytes 6291464 | tf_op jit(solution)/shard_map/ppermute | solution.py:292
  331.1 40.2 %copy-start.4 = (f32[8,256,512]{2,1,0:T(8,128)S(1)}, f32[8,256,512]{2,1,0:T(8,128)}, u32[]{:S(2)}) copy-start(f32[8,256,512]{2,1,0:T(8,128)} %shard_map.96) | copy-start | bytes 12582916
  347.7 63.0 %collective-permute-start.6 = (f32[4,256,256]{2,1,0:T(8,128)}, f32[4,256,256]{2,1,0:T(8,128)S(1)}, u32[]{:S(2)}, u32[]{:S(2)}) collective-permute-start(f32[4,256,256]{2,1,0:T(8,128)} %slice.89), channel_id=1, source_target_pairs={{0,4},{4,0},{1,5},{5,1},{2,6},{6,2},{3,7},{7,3},{8,12},{12,8},{9,1... | collective-permute-start | bytes 3145736 | tf_op jit(solution)/shard_map/ppermute | solution.py:241
  373.3 11.8 %copy-start = (f32[4,256,512]{2,1,0:T(8,128)}, f32[4,256,512]{2,1,0:T(8,128)S(1)}, u32[]{:S(2)}) copy-start(f32[4,256,512]{2,1,0:T(8,128)S(1)} %fusion) | copy-start | bytes 6291460
  381.4 3.8 copy-start.2
  392.2 71.3 %collective-permute-start.19 = (f32[2,512,512]{2,1,0:T(8,128)}, f32[2,512,512]{2,1,0:T(8,128)S(1)}, u32[]{:S(2)}, u32[]{:S(2)}) collective-permute-start(f32[2,512,512]{2,1,0:T(8,128)} %constant_dynamic-slice_fusion), channel_id=1, source_target_pairs={{0,4},{4,0},{1,5},{5,1},{2,6},{6,2},{3,7},{7,3},{8,12},{12,8},{9,1... | collective-permute-start | bytes 6291464 | tf_op jit(solution)/shard_map/ppermute | solution.py:241
  408.7 51.8 %collective-permute-start.13 = (f32[4,256,256]{2,1,0:T(8,128)}, f32[4,256,256]{2,1,0:T(8,128)}, u32[]{:S(2)}, u32[]{:S(2)}) collective-permute-start(f32[4,256,256]{2,1,0:T(8,128)} %slice.91), channel_id=1, source_target_pairs={{0,4},{4,0},{1,5},{5,1},{2,6},{6,2},{3,7},{7,3},{8,12},{12,8},{9,1... | collective-permute-start | bytes 3145736 | tf_op jit(solution)/shard_map/ppermute | solution.py:241
  410.7 49.8 %copy-start.7 = (f32[8,256,256]{2,1,0:T(8,128)S(1)}, f32[8,256,256]{2,1,0:T(8,128)}, u32[]{:S(2)}) copy-start(f32[8,256,256]{2,1,0:T(8,128)} %shard_map.95) | copy-start | bytes 6291460
  (3 other events, 7.4 us)
Sparse Core Ops, SparseCore 0:
  41.4 122.1 all-gather.6
  166.4 116.2 all-gather.4

commit v3 on v0

v3 whole, which is shorter than its diff:
```python
import functools

import jax
import jax.numpy as jnp
import numpy as np
from jax import lax
from jax.experimental import pallas as pl
from jax.experimental.pallas import tpu as pltpu
from jax.sharding import PartitionSpec as P

BLK = 128
VMEM_BYTES = 58 * 1024 * 1024


def halves(value):
    high = value.astype(jnp.bfloat16)
    low = (value - high.astype(jnp.float32)).astype(jnp.bfloat16)
    return high, low


def dot(left, right):
    return jnp.dot(left, right, preferred_element_type=jnp.float32)


class Layout:
    def __init__(self, rows, leaves, cols, half, width):
        self.leaves, self.cols, self.half, self.width = leaves, cols, half, width
        self.part = half // leaves
        self.span = width * cols
        self.counts, self.holder, self.source = [], [], []
        for r in range(rows):
            count = [min(leaves, (q * half + half - 1) // self.span + 1) for q in (2 * r + 1, 2 * (rows - 1 - r))]
            assert count[0] + count[1] <= leaves + 1
            free = list(range(count[1], leaves))
            moved = [leaf for leaf in range(1, count[0]) if leaf not in free]
            slot = {leaf: leaf for leaf in range(1, count[0]) if leaf in free}
            left = [s for s in free if s not in slot]
            slot.update(zip(moved, left))
            self.counts.append(count)
            self.holder.append(slot)
        table = np.full((rows, 2, leaves, leaves), -1, np.int32)
        for r in range(rows):
            for j in range(leaves):
                table[r, 0, 0, j] = j * (leaves + 1) + leaves
                for leaf, slot in self.holder[r].items():
                    table[r, 0, leaf, j] = slot * (leaves + 1) + j
                for leaf in range(self.counts[r][1]):
                    table[r, 1, leaf, j] = leaf * (leaves + 1) + j
        self.table = table


def place_of(lay, pat, k):
    first = pat[k] * BLK
    leaf = first // lay.span
    rest = first - leaf * lay.span
    col = rest // lay.width
    return leaf, col, (rest - col * lay.width) // BLK


def fetch_entry(lay, pat, tab, gathered, t, sems, k):
    leaf, col, sub = place_of(lay, pat, k)
    for s in range(2):
        here = tab[s, leaf, 0] >= 0

        @pl.when(here)
        def _():
            for j in range(lay.leaves):
                entry = tab[s, leaf, j]
                slot = entry // (lay.leaves + 1)
                position = entry - slot * (lay.leaves + 1)
                for which in range(len(gathered)):

                    @pl.when(sub == which)
                    def _():
                        pltpu.make_async_copy(
                            gathered[which].at[slot * lay.cols + col, position],
                            t.at[k, s, pl.ds(j * lay.part, lay.part)],
                            sems.at[k, s],
                        ).start()

        @pl.when(jnp.logical_not(here))
        def _():
            t[k, s] = jnp.zeros(t.shape[2:], t.dtype)


def any_valid(lay, pat, tab, kp, s):
    first = tab[s, place_of(lay, pat, 2 * kp)[0], 0] >= 0
    second = tab[s, place_of(lay, pat, 2 * kp + 1)[0], 0] >= 0
    return jnp.logical_or(first, second)


def wait_pair(lay, pat, tab, t, sems, kp, s):
    for m in range(2):
        k = 2 * kp + m

        @pl.when(tab[s, place_of(lay, pat, k)[0], 0] >= 0)
        def _():
            pltpu.make_async_copy(t.at[k, s], t.at[k, s], sems.at[k, s]).wait()


def back_product(turned_high, turned_low, high, low, s):
    return dot(turned_high[s], high) + dot(turned_low[s], high) + dot(turned_high[s], low)


def panel_kernel(lay, rows, pat, tab, order, *refs):
    count = lay.width // BLK
    gathered, p_ref = refs[:count], refs[count]
    outs = refs[count + 1 : count + rows]
    turned_high, turned_low, t, th, tl, image, sems = refs[count + rows :]
    number = t.shape[0]
    each = number // 2 // rows

    @pl.loop(0, number)
    def _(k):
        fetch_entry(lay, pat, tab, gathered, t, sems, k)

    image[...] = jnp.zeros_like(image)

    @pl.loop(0, number // 2)
    def _(kp):
        span = pl.ds(pl.multiple_of(kp * 2 * BLK, 2 * BLK), 2 * BLK)
        p_high, p_low = halves(p_ref[span, :])
        stacked = jnp.concatenate([p_high, p_low, p_high], axis=0)
        for s in range(2):
            wait_pair(lay, pat, tab, t, sems, kp, s)

            @pl.when(any_valid(lay, pat, tab, kp, s))
            def _():
                high, low = halves(jnp.concatenate([t[2 * kp, s], t[2 * kp + 1, s]], axis=1))
                th[kp, s] = high
                tl[kp, s] = low
                image[s] += dot(jnp.concatenate([high, high, low], axis=1), stacked)

    for s in range(2):
        high, low = halves(image[s].T)
        turned_high[s] = high
        turned_low[s] = low

    for a in range(rows - 1):

        @pl.loop(0, each)
        def _(i):
            kp = order[a] * each + i
            out = outs[a].at[i]
            out[...] = jnp.zeros(out.shape, out.dtype)
            for s in range(2):

                @pl.when(any_valid(lay, pat, tab, kp, s))
                def _():
                    out[...] += back_product(turned_high, turned_low, th[kp, s], tl[kp, s], s).T


def own_panel_kernel(lay, rows, pat, tab, order, *refs):
    count = lay.width // BLK
    gathered, (turned_high, turned_low, out_ref, t, sems) = refs[:count], refs[count:]
    each = t.shape[0] // 2 // rows
    first = order[rows - 1] * each

    @pl.loop(0, 2 * each)
    def _(i):
        fetch_entry(lay, pat, tab, gathered, t, sems, 2 * first + i)

    @pl.loop(0, each)
    def _(i):
        kp = first + i
        out = out_ref.at[i]
        out[...] = jnp.zeros(out.shape, out.dtype)
        for s in range(2):
            wait_pair(lay, pat, tab, t, sems, kp, s)

            @pl.when(any_valid(lay, pat, tab, kp, s))
            def _():
                high, low = halves(jnp.concatenate([t[2 * kp, s], t[2 * kp + 1, s]], axis=1))
                out[...] += back_product(turned_high, turned_low, high, low, s).T


ANY = pl.BlockSpec(memory_space=pl.ANY)
VMEM = pl.BlockSpec(memory_space=pltpu.VMEM)
SMEM = pl.BlockSpec(memory_space=pltpu.SMEM)


def estimate(flops, values):
    return pl.CostEstimate(flops=flops, bytes_accessed=4 * values, transcendentals=0)


def panel_product(lay, pattern, table, order, gathered, normed):
    number, wide, rows = pattern.shape[0], normed.shape[1], order.shape[0]
    half = lay.half
    pairs = number // 2
    block = jax.ShapeDtypeStruct((pairs // rows, 2 * BLK, wide), jnp.float32)
    turned = jax.ShapeDtypeStruct((2, wide, half), jnp.bfloat16)
    result = pl.pallas_call(
        functools.partial(panel_kernel, lay, rows),
        out_shape=[block] * (rows - 1) + [turned] * 2,
        in_specs=[SMEM] * 3 + [ANY] * len(gathered) + [VMEM],
        out_specs=[VMEM] * (rows + 1),
        scratch_shapes=[
            pltpu.VMEM((number, 2, half, BLK), jnp.float32),
            pltpu.VMEM((pairs, 2, half, 2 * BLK), jnp.bfloat16),
            pltpu.VMEM((pairs, 2, half, 2 * BLK), jnp.bfloat16),
            pltpu.VMEM((2, half, wide), jnp.float32),
            pltpu.SemaphoreType.DMA((number, 2)),
        ],
        compiler_params=pltpu.CompilerParams(vmem_limit_bytes=VMEM_BYTES),
        cost_estimate=estimate(18 * half * number * BLK * wide, 2 * half * number * BLK),
    )(pattern, table, order, *gathered, normed)
    return result[: rows - 1], result[rows - 1 :]


def own_panel_product(lay, pattern, table, order, gathered, turned):
    number, wide, rows = pattern.shape[0], turned[0].shape[1], order.shape[0]
    half = lay.half
    return pl.pallas_call(
        functools.partial(own_panel_kernel, lay, rows),
        out_shape=jax.ShapeDtypeStruct((number // 2 // rows, 2 * BLK, wide), jnp.float32),
        in_specs=[SMEM] * 3 + [ANY] * len(gathered) + [VMEM] * 2,
        out_specs=VMEM,
        scratch_shapes=[
            pltpu.VMEM((number, 2, half, BLK), jnp.float32),
            pltpu.SemaphoreType.DMA((number, 2)),
        ],
        compiler_params=pltpu.CompilerParams(vmem_limit_bytes=VMEM_BYTES),
        cost_estimate=estimate(6 * half * number * BLK * wide, half * number * BLK),
    )(pattern, table, order, *gathered, *turned)


def top_kernel(lay, rows, tab, info, g_ref, own_ref, *refs):
    outs, own_turned = refs[:rows], refs[rows]
    blocks = g_ref.shape[0]
    parts = lay.leaves
    each = blocks // 2 // rows
    for s in range(2):

        @pl.loop(0, parts)
        def _(j):
            high, low = halves(own_ref[s, j].T)
            own_turned[s, j] = jnp.concatenate([high, low, high], axis=1)

    for a in range(rows):

        @pl.loop(0, each)
        def _(i):
            block = 2 * (info[a] * each + i)
            leaf = block // lay.cols
            col = block - leaf * lay.cols
            out = outs[a].at[i]
            out[...] = jnp.zeros(out.shape, out.dtype)
            for s in range(2):

                @pl.when(jnp.logical_and(tab[s, leaf, 0] >= 0, tab[s, info[rows], 0] >= 0))
                def _():
                    total = None
                    for j in range(parts):
                        entry = tab[s, leaf, j]
                        slot = entry // (parts + 1)
                        position = entry - slot * (parts + 1)
                        at = slot * lay.cols + col
                        both = jnp.concatenate([g_ref[at, position], g_ref[at + 1, position]], axis=1)
                        high, low = halves(both)
                        term = dot(own_turned[s, j], jnp.concatenate([high, high, low], axis=0))
                        total = term if total is None else total + term
                    out[...] += total.T


def top_product(lay, table, info, gathered, own):
    blocks, rows = gathered.shape[0], info.shape[0] - 1
    parts, part, width = lay.leaves, lay.part, lay.width
    block = jax.ShapeDtypeStruct((blocks // 2 // rows, 2 * BLK, width), jnp.float32)
    return pl.pallas_call(
        functools.partial(top_kernel, lay, rows),
        out_shape=[block] * rows,
        in_specs=[SMEM, SMEM, VMEM, VMEM],
        out_specs=[VMEM] * rows,
        scratch_shapes=[pltpu.VMEM((2, parts, width, 3 * part), jnp.bfloat16)],
        compiler_params=pltpu.CompilerParams(vmem_limit_bytes=VMEM_BYTES),
        cost_estimate=estimate(12 * lay.half * blocks * BLK * width, gathered.size),
    )(table, info, gathered, own)


def diagonal_kernel(cols, info, *refs):
    lefts, own, rights = refs[: cols - 1], refs[cols - 1], refs[cols : 2 * cols - 1]
    sigma, out_ref, held, sems = refs[2 * cols - 1 :]
    each = out_ref.shape[0]
    sources = {0: own}
    for t in range(1, cols):
        sources[t], sources[-t] = lefts[t - 1], rights[t - 1]
    for i in range(each):
        away = info[0] * each + i - info[1]
        for step, source in sources.items():

            @pl.when(away == step)
            def _():
                pltpu.make_async_copy(source, held.at[i], sems.at[i]).start()

    turned_high, turned_low = halves(sigma[...].T)
    for i in range(each):
        pltpu.make_async_copy(held.at[i], held.at[i], sems.at[i]).wait()
        high, low = halves(held[i])
        total = dot(turned_high, high) + dot(turned_low, high) + dot(turned_high, low)
        out_ref[i] = total.T


def diagonal_product(info, rows, lefts, own, rights, sigma):
    cols = len(lefts) + 1
    each = cols // rows
    depth, wide = sigma.shape
    return pl.pallas_call(
        functools.partial(diagonal_kernel, cols),
        out_shape=jax.ShapeDtypeStruct((each, wide, wide), jnp.float32),
        in_specs=[SMEM] + [ANY] * (2 * cols - 1) + [VMEM],
        out_specs=VMEM,
        scratch_shapes=[pltpu.VMEM((each, depth, wide), jnp.float32), pltpu.SemaphoreType.DMA((each,))],
        compiler_params=pltpu.CompilerParams(vmem_limit_bytes=VMEM_BYTES),
        cost_estimate=estimate(6 * each * depth * wide * wide, (each + 1) * depth * wide),
    )(info, *lefts, own, *rights, sigma)


def after(value, *earlier):
    return pl.pallas_call(
        lambda *refs: None,
        out_shape=jax.ShapeDtypeStruct(value.shape, value.dtype),
        in_specs=[ANY] * (1 + len(earlier)),
        out_specs=ANY,
        input_output_aliases={0: 0},
        cost_estimate=estimate(0, 0),
    )(value, *earlier)


def sum_over_rows(sent, own):
    rows = lax.axis_size("row")
    for a, value in enumerate(sent):
        own = own + lax.ppermute(value, "row", [(i, (i + a + 1) % rows) for i in range(rows)])
    return own


def per_device(lay, top_inverse, pattern, panel, diag_inverse):
    rows, cols, leaves = (lax.axis_size(axis) for axis in ("row", "col", "leaf"))
    me_row, me_col, me_leaf = (lax.axis_index(axis) for axis in ("row", "col", "leaf"))
    half, width, parts, part = lay.half, lay.width, lay.leaves, lay.part
    normed = panel[0]

    own_rows = lax.dynamic_slice_in_dim(normed, me_row * (normed.shape[0] // rows), normed.shape[0] // rows, 0)

    def hop(value, step, way):
        if way > 0:
            return lax.ppermute(value, "col", [(i, i + 1) for i in range(step, cols - 1)])
        return lax.ppermute(value, "col", [(i, i - 1) for i in range(1, cols - step)])

    right, left = [hop(own_rows, 0, 1)], [hop(own_rows, 0, -1)]

    table = jnp.asarray(lay.table)[me_row]
    second = jnp.asarray([count[1] for count in lay.counts], jnp.int32)[me_row]
    is_moved = np.zeros((rows, leaves), bool)
    pairs = []
    for r in range(rows):
        for leaf, slot in lay.holder[r].items():
            if leaf != slot:
                is_moved[r, slot] = True
                pairs.append((leaf * rows + r, slot * rows + r))
    moved_here = jnp.asarray(is_moved)[me_row, me_leaf]
    gathered, own, held = [], [], None
    for sub in range(width // BLK):
        lanes = slice(sub * BLK, (sub + 1) * BLK)
        lower, upper = top_inverse[half:, lanes], top_inverse[:half, lanes]
        if held is not None:
            lower, upper = after(lower, held), after(upper, held)
        swapped = lax.ppermute(upper, "row", [(r, rows - 1 - r) for r in range(rows)])
        moved = lax.ppermute(lower, ("leaf", "row"), pairs) if pairs else lower
        whole = jnp.where(me_leaf < second, swapped, jnp.where(moved_here, moved, lower))
        extra = lower[:part]
        for j in range(1, parts):
            sent = lax.ppermute(lower[j * part : (j + 1) * part], "leaf", [(0, j)])
            extra = jnp.where(me_leaf == j, sent, extra)
        earlier = held
        held = jnp.concatenate([whole.reshape(parts, part, BLK), extra[None]], axis=0)
        if earlier is not None:
            held = after(held, right[0], left[0])
        gathered.append(lax.all_gather(held, ("leaf", "col"), axis=0, tiled=False))
        own.append(jnp.stack([lower, swapped]))
    own = jnp.concatenate(own, axis=2).reshape(2, parts, part, width)

    right[0], left[0] = after(right[0], gathered[-1]), after(left[0], gathered[-1])
    for step in range(1, cols - 1):
        right.append(hop(right[-1], step, 1))
        left.append(hop(left[-1], step, -1))

    order = ((me_row + 1 + jnp.arange(rows)) % rows).astype(jnp.int32)
    info = jnp.append(order, me_leaf.astype(jnp.int32))
    tops = [top_product(lay, table, info, part_of, own) for part_of in gathered[:-1]]
    tops = [sum_over_rows(top[:-1], top[-1]) for top in tops]
    if tops:
        order = after(order, tops[-1])

    sent, turned = panel_product(lay, pattern[0], table, order, gathered, normed)
    kept = own_panel_product(lay, pattern[0], table, order, gathered, turned)
    sigma_panel = -sum_over_rows(sent, kept).reshape(-1, normed.shape[1])

    *away, here = top_product(lay, table, after(info, kept), gathered[-1], own)
    tops.append(sum_over_rows([after(value, sigma_panel) for value in away], here))
    sigma_top = jnp.concatenate([top.reshape(-1, 1, BLK, width) for top in tops], axis=1).reshape(-1, width)

    terms = [
        diagonal_product(jnp.stack([order[a], me_col.astype(jnp.int32)]), rows, left, own_rows, right, sigma_panel)
        for a in range(rows)
    ]
    update = sum_over_rows(terms[:-1], terms[-1])
    sigma_diag = diag_inverse[0] - update.reshape(diag_inverse.shape[1:])
    return (sigma_top, sigma_panel[None], sigma_diag[None])


def solution(mesh):
    placed = (
        P("row", ("leaf", "col")),
        P("leaf", None),
        P("leaf", None, "col"),
        P("leaf", "row", "col"),
    )

    def whole(top_inverse, pattern, panel, diag_inverse):
        rows, leaves, cols = (mesh.shape[axis] for axis in ("row", "leaf", "col"))
        size = top_inverse.shape[0]
        lay = Layout(rows, leaves, cols, size // rows // 2, size // leaves // cols)
        return jax.shard_map(
            functools.partial(per_device, lay),
            mesh=mesh,
            in_specs=placed,
            out_specs=(P("row", ("leaf", "col")), P("leaf", "row", "col"), P("leaf", "row", "col")),
            check_vma=False,
        )(top_inverse, pattern, panel, diag_inverse)

    return whole
```

time: 534 us -> 439 us (0.82)
  matrix products: 112 us -> 0 us
  waiting for transfers between devices: 369 us -> 268 us
  Pallas kernels: 0 us -> 82.1 us
  starting transfers between devices: 0.21 us -> 39 us
  local copies, waits for them, and re-layouts: 35.4 us -> 12 us
  other arithmetic: 3.57 us -> 21.8 us
    ppermute x0 -> x20, waiting for transfers between devices: none -> 211 us  [the longest x4 86.8 us: sum_over_rows(): lax.ppermute(value, 'row', [(i, (i + a + 1) % rows) for i in range(rows)])]
    all_gather x2, waiting for transfers between devices: 238 us -> 56.9 us  [per_device(): gathered.append(lax.all_gather(held, ('leaf', 'col'), axis=0, tiled=False))]
    reduce_scatter x3 -> x0, waiting for transfers between devices: 131 us -> none  [the longest x1 55.4 us: per_device(): lax.psum_scatter(-contract_rows(columns, image), 'row', scatter_dimension...]
    dot_general x4 -> x0, matrix products: 112 us -> none  [the longest x3 78.3 us: contract_rows(): lax.dot_general(left, right, (((0,), (0,)), ((), ())), precision=lax.Prec...]
    pallas_call x0 -> x14, Pallas kernels: none -> 82.1 us  [the longest x2 28.2 us: top_product(): pl.pallas_call(functools.partial(top_kernel, lay, rows), out_shape=[block...]
    ppermute x0 -> x20, starting transfers between devices: none -> 38.9 us  [the longest x6 11.9 us: per_device(): sent = lax.ppermute(lower[j * part:(j + 1) * part], 'leaf', [(0, j)])]
    gather x1 -> x0, local copies, waits for them, and re-layouts: 27.9 us -> none  [per_device(): selected = jnp.take(rows_here, wanted, axis=1)]
    add x1 -> x3, other arithmetic: 0.07 us -> 6.25 us  [sum_over_rows(): own + lax.ppermute(value, 'row', [(i, (i + a + 1) % rows) for i in range(...]
  transfers between devices with their start and end apart: 5 -> 22, of which waited for: 5 -> 14; matrix products, arithmetic and copies ran while one was open for 24% -> 6% of each run, Pallas kernels for 0% -> 17%
where the time goes in v3:
time: 439 us; the launch traced here: 438 us
  waiting for transfers between devices  268 us (61%)
  Pallas kernels  82.1 us (19%)
  starting transfers between devices  39 us (9%)
  other arithmetic  21.8 us (5%)
  between operations  14.9 us (3%)
  local copies, waits for them, and re-layouts  12 us (3%)
    ppermute x4, waiting for transfers between devices, sum_over_rows(): lax.ppermute(value, 'row', [(i, (i + a + 1) % rows) for i in range(rows)])  86.8 us
    ppermute x3, waiting for transfers between devices, hop(): lax.ppermute(value, 'col', [(i, i + 1) for i in range(step, cols - 1)])  57.2 us
    all_gather x2, waiting for transfers between devices, per_device(): gathered.append(lax.all_gather(held, ('leaf', 'col'), axis=0, tiled=False))  56.9 us
    ppermute x3, waiting for transfers between devices, hop(): lax.ppermute(value, 'col', [(i, i - 1) for i in range(1, cols - step)])  54.2 us
    pallas_call x2, Pallas kernels, top_product(): pl.pallas_call(functools.partial(top_kernel, lay, rows), out_shape=[block...  28.2 us
    pallas_call x1, Pallas kernels, panel_product(): pl.pallas_call(functools.partial(panel_kernel, lay, rows), out_shape=[blo...  22.5 us
    pallas_call x2, Pallas kernels, diagonal_product(): pl.pallas_call(functools.partial(diagonal_kernel, cols), out_shape=jax.Sh...  17.1 us
    pallas_call x1, Pallas kernels, own_panel_product(): pl.pallas_call(functools.partial(own_panel_kernel, lay, rows), out_shape=...  14.2 us
  transfers between devices with their start and end apart: 22, of which 14 were waited for; matrix products, arithmetic and copies ran while one was open for 6% of the time, Pallas kernels for 17%

profile of v3, /device:TPU:0, one launch (start us, length us, event | category | flops | bytes accessed | tf_op | source)
XLA Modules:
  0.0 438.1 jit_solution(4386370284003007616)
XLA Ops:
  7.2 2.4 fusion.4
  9.6 3.0 collective-permute-start
  14.0 3.1 collective-permute-start.2
  18.5 2.0 collective-permute-start.4
  22.2 2.0 collective-permute-done.3
  27.5 3.1 dynamic-slice_bitcast_fusion.refs_3_
  30.7 3.8 collective-permute-start.11
  37.7 3.0 collective-permute-start.8
  41.6 5.8 %collective-permute-done.8 = f32[256,128]{1,0:T(8,128)S(1)} collective-permute-done((f32[256,128]{1,0:T(8,128)}, f32[256,128]{1,0:T(8,128)S(1)}, u32[]{:S(2)}, u32[]{:S(2)}) %collective-permute-start.8) | collective-permute-done | bytes 131104 | tf_op jit(solution)/shard_map/ppermute | solution.py:372
  48.7 3.9 collective-permute-done.9
  56.6 57.2 %collective-permute-done.11.refs_1_.refs_0_ = f32[1024,512]{1,0:T(8,128)S(1)} collective-permute-done((f32[1024,512]{1,0:T(8,128)}, f32[1024,512]{1,0:T(8,128)S(1)}, u32[]{:S(2)}, u32[]{:S(2)}) %collective-permute-start.11) | collective-permute-done | bytes 2097184 | tf_op jit(solution)/shard_map/ppermute | solution.py:346
  113.8 22.1 %collective-permute-done.12.refs_2_.refs_0_ = f32[1024,512]{1,0:T(8,128)} collective-permute-done((f32[1024,512]{1,0:T(8,128)}, f32[1024,512]{1,0:T(8,128)}, u32[]{:S(2)}, u32[]{:S(2)}) %collective-permute-start.12) | collective-permute-done | bytes 2097184 | tf_op jit(solution)/shard_map/ppermute | solution.py:347
  137.2 2.8 maximum_maximum_fusion
  139.9 9.7 %all-gather.5.cloned.1.call-done = f32[80,256,128]{2,1,0:T(8,128)} async-done(((f32[5,256,128]{2,1,0:T(8,128)}), f32[80,256,128]{2,1,0:T(8,128)}) %all-gather.5.cloned.1.call-update) | async-done | bytes 10485776 | tf_op jit(solution)/shard_map/all_gather | solution.py:378
  149.6 14.1 %shard_map.96 = (f32[4,256,256]{2,1,0:T(8,128)}, f32[4,256,256]{2,1,0:T(8,128)}) custom-call(s32[2,4,4]{2,1,0:T(4,128)} %dynamic-slice_bitcast_fusion.1.tab, s32[3]{0:T(128)} %pad_add_fusion.info.refs_0_, f32[16,5,256,128]{3,2,1,0:T(8,128)} %bitcast.42, f32[2,4,256,256]{3,2,1,0:T(8,128)} %bitcast.49), custom_call_target="tpu_custom_call" | custom-call | flops 6442450944 | bytes 10485760 | tf_op jit(solution)/shard_map/pallas_call | solution.py:269
  164.7 24.6 %collective-permute-done.6 = f32[4,256,256]{2,1,0:T(8,128)S(1)} collective-permute-done((f32[4,256,256]{2,1,0:T(8,128)}, f32[4,256,256]{2,1,0:T(8,128)S(1)}, u32[]{:S(2)}, u32[]{:S(2)}) %collective-permute-start.6) | collective-permute-done | bytes 1048608 | tf_op jit(solution)/shard_map/ppermute | solution.py:332
  189.3 2.7 add.44.refs_1_
  191.9 47.2 %all-gather.7.cloned.1.call-done = f32[80,256,128]{2,1,0:T(8,128)} async-done(((f32[5,256,128]{2,1,0:T(8,128)}), f32[80,256,128]{2,1,0:T(8,128)}) %all-gather.7.cloned.1.call-update) | async-done | bytes 10485776 | tf_op jit(solution)/shard_map/all_gather | solution.py:378
  240.5 2.0 collective-permute-start.17
  242.5 22.5 %shard_map.99 = (f32[4,256,512]{2,1,0:T(8,128)}, bf16[2,512,1024]{2,1,0:T(8,128)(2,1)}, bf16[2,512,1024]{2,1,0:T(8,128)(2,1)}) custom-call(s32[16]{0:T(128)} %bitcast.56, s32[2,4,4]{2,1,0:T(4,128)} %dynamic-slice_bitcast_fusion.1.tab, s32[2]{0:T(128)} %shard_map.97.order, f32[16,5,256,128]{3,2,1,0:T(8,128)} %bitcast.43, f32[16,5,256,128]{3,2,1,0:T(8,128)} %bitcast.34, ...), custom_call_target="tpu_custom_call" | custom-call | flops 19327352832 | bytes 16777216 | tf_op jit(solution)/shard_map/pallas_call | solution.py:192
  265.0 7.8 %collective-permute-start.13 = (f32[4,256,512]{2,1,0:T(8,128)}, f32[4,256,512]{2,1,0:T(8,128)}, u32[]{:S(2)}, u32[]{:S(2)}) collective-permute-start(f32[4,256,512]{2,1,0:T(8,128)} %get-tuple-element.16), channel_id=1, source_target_pairs={{0,4},{4,0},{1,5},{5,1},{2,6},{6,2},{3,7},{7,3},{8,12},{12,8},{9,1... | collective-permute-start | bytes 6291464 | tf_op jit(solution)/shard_map/ppermute | solution.py:332
  272.8 16.4 %collective-permute-done.15.refs_1_ = f32[1024,512]{1,0:T(8,128)} collective-permute-done((f32[1024,512]{1,0:T(8,128)}, f32[1024,512]{1,0:T(8,128)}, u32[]{:S(2)}, u32[]{:S(2)}) %collective-permute-start.15) | collective-permute-done | bytes 2097184 | tf_op jit(solution)/shard_map/ppermute | solution.py:347
  290.4 2.0 collective-permute-start.18
  294.1 14.2 %shard_map.100.refs_1_ = f32[4,256,512]{2,1,0:T(8,128)} custom-call(s32[16]{0:T(128)} %bitcast.57, s32[2,4,4]{2,1,0:T(4,128)} %dynamic-slice_bitcast_fusion.1.tab, s32[2]{0:T(128)} %shard_map.97.order, f32[16,5,256,128]{3,2,1,0:T(8,128)} %bitcast.44, f32[16,5,256,128]{3,2,1,0:T(8,128)} %bitcast.35, bf16[2,512,1024]{2,1,0:T(8,128)(2,1)} %get-tuple-element.12.refs_2_, ...), custom_call_target="tpu_custom_call" | custom-call | flops 6442450944 | bytes 8388608 | tf_op jit(solution)/shard_map/pallas_call | solution.py:213
  308.4 10.8 %collective-permute-done.13 = f32[4,256,512]{2,1,0:T(8,128)} collective-permute-done((f32[4,256,512]{2,1,0:T(8,128)}, f32[4,256,512]{2,1,0:T(8,128)}, u32[]{:S(2)}, u32[]{:S(2)}) %collective-permute-start.13) | collective-permute-done | bytes 2097184 | tf_op jit(solution)/shard_map/ppermute | solution.py:332
  319.1 3.4 add_negate_fusion
  322.5 15.8 %collective-permute-done.16.refs_2_ = f32[1024,512]{1,0:T(8,128)} collective-permute-done((f32[1024,512]{1,0:T(8,128)}, f32[1024,512]{1,0:T(8,128)}, u32[]{:S(2)}, u32[]{:S(2)}) %collective-permute-start.16) | collective-permute-done | bytes 2097184 | tf_op jit(solution)/shard_map/ppermute | solution.py:347
  338.3 8.6 %shard_map.107 = f32[2,512,512]{2,1,0:T(8,128)} custom-call(s32[2]{0:T(128)} %pad_add_fusion.2.info, f32[1024,512]{1,0:T(8,128)} %shard_map.104.refs_0_, f32[1024,512]{1,0:T(8,128)} %collective-permute-done.15.refs_1_, f32[1024,512]{1,0:T(8,128)} %collective-permute-done.16.refs_2_, f32[1024,512]{1,0:T(8,128)} %dynamic-slice_bitcast_fusion.refs_3_, ...), custom_call_target="tpu_custom_call" | custom-call | flops 3221225472 | bytes 6291456 | tf_op jit(solution)/shard_map/pallas_call | solution.py:307
  348.4 14.1 %shard_map.102 = (f32[4,256,256]{2,1,0:T(8,128)}, f32[4,256,256]{2,1,0:T(8,128)}) custom-call(s32[2,4,4]{2,1,0:T(4,128)} %dynamic-slice_bitcast_fusion.1.tab, s32[3]{0:T(128)} %shard_map.101.info, f32[16,5,256,128]{3,2,1,0:T(8,128)} %bitcast.36, f32[2,4,256,256]{3,2,1,0:T(8,128)} %bitcast.50), custom_call_target="tpu_custom_call" | custom-call | flops 6442450944 | bytes 10485760 | tf_op jit(solution)/shard_map/pallas_call | solution.py:269
  364.2 51.5 %collective-permute-done.14 = f32[4,256,256]{2,1,0:T(8,128)S(1)} collective-permute-done((f32[4,256,256]{2,1,0:T(8,128)}, f32[4,256,256]{2,1,0:T(8,128)S(1)}, u32[]{:S(2)}, u32[]{:S(2)}) %collective-permute-start.14) | collective-permute-done | bytes 1048608 | tf_op jit(solution)/shard_map/ppermute | solution.py:332
  418.7 8.5 %shard_map.106 = f32[2,512,512]{2,1,0:T(8,128)} custom-call(s32[2]{0:T(128)} %pad_add_fusion.1.info, f32[1024,512]{1,0:T(8,128)} %shard_map.104.refs_0_, f32[1024,512]{1,0:T(8,128)} %collective-permute-done.15.refs_1_, f32[1024,512]{1,0:T(8,128)} %collective-permute-done.16.refs_2_, f32[1024,512]{1,0:T(8,128)} %dynamic-slice_bitcast_fusion.refs_3_, ...), custom_call_target="tpu_custom_call" | custom-call | flops 3221225472 | bytes 6291456 | tf_op jit(solution)/shard_map/pallas_call | solution.py:307
  427.3 2.2 add.48
  (78 shorter events, 31.1 us)
Async XLA Ops:
  7.2 13.3 %copy-start.11 = (s32[2]{0:T(128)S(1)}, s32[2]{0:T(128)}, u32[]{:S(2)}) copy-start(s32[2]{0:T(128)} %constant.45.clone) | copy-start | bytes 28
  7.2 14.4 %copy-start.10 = (pred[2,4]{1,0:T(4,128)(4,1)S(1)}, pred[2,4]{1,0:T(4,128)(4,1)}, u32[]{:S(2)}) copy-start(pred[2,4]{1,0:T(4,128)(4,1)} %constant.46.clone) | copy-start | bytes 28
  7.2 6.1 %copy-start.4 = (f32[2048,256]{1,0:T(8,128)S(1)}, f32[2048,256]{1,0:T(8,128)}, u32[]{:S(2)}) copy-start(f32[2048,256]{1,0:T(8,128)} %param.7) | copy-start | bytes 6291460
  7.2 142.4 %all-gather.5.cloned.1.call-start = ((), (), s32[]{:S(2)}) async-start(), calls=%async_computation | async-start | bytes 11141120 | tf_op jit(solution)/shard_map/all_gather | solution.py:378
  9.6 15.1 %collective-permute-start = (f32[1024,128]{1,0:T(8,128)}, f32[1024,128]{1,0:T(8,128)S(1)}, u32[]{:S(2)}, u32[]{:S(2)}) collective-permute-start(f32[1024,128]{1,0:T(8,128)} %get-tuple-element.22), channel_id=1, source_target_pairs={{0,4},{4,0},{1,5},{5,1},{2,6},{6,2},{3,7},{7,3},{8,12},{12,8},{9,1... | collective-permute-start | bytes 1572872 | tf_op jit(solution)/shard_map/ppermute | solution.py:367
  12.6 12.1 %collective-permute-start.1 = (f32[1024,128]{1,0:T(8,128)}, f32[1024,128]{1,0:T(8,128)S(1)}, u32[]{:S(2)}, u32[]{:S(2)}) collective-permute-start(f32[1024,128]{1,0:T(8,128)} %get-tuple-element.21), channel_id=1, source_target_pairs={{8,24},{9,25},{10,26},{11,27}} | collective-permute-start | bytes 1572872 | tf_op jit(solution)/shard_map/ppermute | solution.py:368
  14.0 8.2 %collective-permute-start.2 = (f32[256,128]{1,0:T(8,128)}, f32[256,128]{1,0:T(8,128)S(1)}, u32[]{:S(2)}, u32[]{:S(2)}) collective-permute-start(f32[256,128]{1,0:T(8,128)} %get-tuple-element.25), channel_id=1, source_target_pairs={{0,24},{1,25},{2,26},{3,27},{4,28},{5,29},{6,30},{7,31}} | collective-permute-start | bytes 393224 | tf_op jit(solution)/shard_map/ppermute | solution.py:372
  17.2 7.1 %collective-permute-start.3 = (f32[256,128]{1,0:T(8,128)}, f32[256,128]{1,0:T(8,128)S(1)}, u32[]{:S(2)}, u32[]{:S(2)}) collective-permute-start(f32[256,128]{1,0:T(8,128)} %get-tuple-element.24), channel_id=1, source_target_pairs={{0,16},{1,17},{2,18},{3,19},{4,20},{5,21},{6,22},{7,23}} | collective-permute-start | bytes 393224 | tf_op jit(solution)/shard_map/ppermute | solution.py:372
  18.5 5.8 %collective-permute-start.4 = (f32[256,128]{1,0:T(8,128)S(1)}, f32[256,128]{1,0:T(8,128)}, u32[]{:S(2)}, u32[]{:S(2)}) collective-permute-start(f32[256,128]{1,0:T(8,128)S(1)} %get-tuple-element.23), channel_id=1, source_target_pairs={{0,8},{1,9},{2,10},{3,11},{4,12},{5,13},{6,14},{7,15}} | collective-permute-start | bytes 393224 | tf_op jit(solution)/shard_map/ppermute | solution.py:372
  27.5 211.7 %all-gather.7.cloned.1.call-start = ((), (), s32[]{:S(2)}) async-start(), calls=%async_computation.1 | async-start | bytes 11141120 | tf_op jit(solution)/shard_map/all_gather | solution.py:378
  30.7 83.1 %collective-permute-start.11 = (f32[1024,512]{1,0:T(8,128)}, f32[1024,512]{1,0:T(8,128)S(1)}, u32[]{:S(2)}, u32[]{:S(2)}) collective-permute-start(f32[1024,512]{1,0:T(8,128)} %dynamic-slice_bitcast_fusion.refs_3_), channel_id=1, source_target_pairs={{0,1},{1,2},{2,3},{4,5},{5,6},{6,7},{8,9},{9,10},{10,11},{12,13},{... | collective-permute-start | bytes 6291464 | tf_op jit(solution)/shard_map/ppermute | solution.py:346
  34.5 101.3 %collective-permute-start.12 = (f32[1024,512]{1,0:T(8,128)}, f32[1024,512]{1,0:T(8,128)}, u32[]{:S(2)}, u32[]{:S(2)}) collective-permute-start(f32[1024,512]{1,0:T(8,128)} %dynamic-slice_bitcast_fusion.refs_3_), channel_id=1, source_target_pairs={{1,0},{2,1},{3,2},{5,4},{6,5},{7,6},{9,8},{10,9},{11,10},{13,12},{... | collective-permute-start | bytes 6291464 | tf_op jit(solution)/shard_map/ppermute | solution.py:347
  35.8 5.1 %copy-start.2 = (f32[1024,128]{1,0:T(8,128)S(1)}, f32[1024,128]{1,0:T(8,128)}, u32[]{:S(2)}) copy-start(f32[1024,128]{1,0:T(8,128)} %shard_map.94) | copy-start | bytes 1572868
  37.7 9.7 %collective-permute-start.8 = (f32[256,128]{1,0:T(8,128)}, f32[256,128]{1,0:T(8,128)S(1)}, u32[]{:S(2)}, u32[]{:S(2)}) collective-permute-start(f32[256,128]{1,0:T(8,128)} %get-tuple-element.28), channel_id=1, source_target_pairs={{0,24},{1,25},{2,26},{3,27},{4,28},{5,29},{6,30},{7,31}} | collective-permute-start | bytes 393224 | tf_op jit(solution)/shard_map/ppermute | solution.py:372
  40.7 14.3 %collective-permute-start.5 = (f32[1024,128]{1,0:T(8,128)}, f32[1024,128]{1,0:T(8,128)S(1)}, u32[]{:S(2)}, u32[]{:S(2)}) collective-permute-start(f32[1024,128]{1,0:T(8,128)} %shard_map.95), channel_id=1, source_target_pairs={{0,4},{4,0},{1,5},{5,1},{2,6},{6,2},{3,7},{7,3},{8,12},{12,8},{9,1... | collective-permute-start | bytes 1572872 | tf_op jit(solution)/shard_map/ppermute | solution.py:367
  40.9 14.0 %collective-permute-start.7 = (f32[1024,128]{1,0:T(8,128)S(1)}, f32[1024,128]{1,0:T(8,128)S(1)}, u32[]{:S(2)}, u32[]{:S(2)}) collective-permute-start(f32[1024,128]{1,0:T(8,128)S(1)} %copy-done.2), channel_id=1, source_target_pairs={{8,24},{9,25},{10,26},{11,27}} | collective-permute-start | bytes 1572872 | tf_op jit(solution)/shard_map/ppermute | solution.py:368
  47.4 5.2 %collective-permute-start.9 = (f32[256,128]{1,0:T(8,128)S(1)}, f32[256,128]{1,0:T(8,128)S(1)}, u32[]{:S(2)}, u32[]{:S(2)}) collective-permute-start(f32[256,128]{1,0:T(8,128)S(1)} %get-tuple-element.27), channel_id=1, source_target_pairs={{0,16},{1,17},{2,18},{3,19},{4,20},{5,21},{6,22},{7,23}} | collective-permute-start | bytes 393224 | tf_op jit(solution)/shard_map/ppermute | solution.py:372
  52.6 2.3 collective-permute-start.10
  54.9 58.9 %copy-start.6 = (f32[1024,128]{1,0:T(8,128)}, f32[1024,128]{1,0:T(8,128)S(1)}, u32[]{:S(2)}) copy-start(f32[1024,128]{1,0:T(8,128)S(1)} %collective-permute-done.5) | copy-start | bytes 1572868
  56.6 80.0 %copy-start.9 = (s32[2,2,4,4]{3,2,1,0:T(4,128)S(1)}, s32[2,2,4,4]{3,2,1,0:T(4,128)}, u32[]{:S(2)}) copy-start(s32[2,2,4,4]{3,2,1,0:T(4,128)} %constant.44.clone) | copy-start | bytes 772
  113.8 22.1 %copy-start = (f32[1024,512]{1,0:T(8,128)}, f32[1024,512]{1,0:T(8,128)S(1)}, u32[]{:S(2)}) copy-start(f32[1024,512]{1,0:T(8,128)S(1)} %collective-permute-done.11.refs_1_.refs_0_) | copy-start | bytes 6291460
  163.7 25.5 %collective-permute-start.6 = (f32[4,256,256]{2,1,0:T(8,128)}, f32[4,256,256]{2,1,0:T(8,128)S(1)}, u32[]{:S(2)}, u32[]{:S(2)}) collective-permute-start(f32[4,256,256]{2,1,0:T(8,128)} %get-tuple-element.11), channel_id=1, source_target_pairs={{0,4},{4,0},{1,5},{5,1},{2,6},{6,2},{3,7},{7,3},{8,12},{12,8},{9,1... | collective-permute-start | bytes 3145736 | tf_op jit(solution)/shard_map/ppermute | solution.py:332
  239.2 50.0 %collective-permute-start.15 = (f32[1024,512]{1,0:T(8,128)}, f32[1024,512]{1,0:T(8,128)}, u32[]{:S(2)}, u32[]{:S(2)}) collective-permute-start(f32[1024,512]{1,0:T(8,128)} %shard_map.104.refs_0_), channel_id=1, source_target_pairs={{1,0},{2,1},{5,4},{6,5},{9,8},{10,9},{13,12},{14,13},{17,16},{18,1... | collective-permute-start | bytes 6291464 | tf_op jit(solution)/shard_map/ppermute | solution.py:347
  240.5 50.0 %collective-permute-start.17 = (f32[1024,512]{1,0:T(8,128)}, f32[1024,512]{1,0:T(8,128)}, u32[]{:S(2)}, u32[]{:S(2)}) collective-permute-start(f32[1024,512]{1,0:T(8,128)} %shard_map.105.refs_4_), channel_id=1, source_target_pairs={{1,2},{2,3},{5,6},{6,7},{9,10},{10,11},{13,14},{14,15},{17,18},{18... | collective-permute-start | bytes 6291464 | tf_op jit(solution)/shard_map/ppermute | solution.py:346
  242.5 50.0 %copy-start.8 = (s32[2]{0:T(128)S(1)}, s32[2]{0:T(128)}, u32[]{:S(2)}) copy-start(s32[2]{0:T(128)} %shard_map.97.order) | copy-start | bytes 28
  265.0 54.1 %collective-permute-start.13 = (f32[4,256,512]{2,1,0:T(8,128)}, f32[4,256,512]{2,1,0:T(8,128)}, u32[]{:S(2)}, u32[]{:S(2)}) collective-permute-start(f32[4,256,512]{2,1,0:T(8,128)} %get-tuple-element.16), channel_id=1, source_target_pairs={{0,4},{4,0},{1,5},{5,1},{2,6},{6,2},{3,7},{7,3},{8,12},{12,8},{9,1... | collective-permute-start | bytes 6291464 | tf_op jit(solution)/shard_map/ppermute | solution.py:332
  289.2 49.2 %collective-permute-start.16 = (f32[1024,512]{1,0:T(8,128)}, f32[1024,512]{1,0:T(8,128)}, u32[]{:S(2)}, u32[]{:S(2)}) collective-permute-start(f32[1024,512]{1,0:T(8,128)} %collective-permute-done.15.refs_1_), channel_id=1, source_target_pairs={{1,0},{5,4},{9,8},{13,12},{17,16},{21,20},{25,24},{29,28}} | collective-permute-start | bytes 6291464 | tf_op jit(solution)/shard_map/ppermute | solution.py:347
  290.4 47.9 %collective-permute-start.18 = (f32[1024,512]{1,0:T(8,128)}, f32[1024,512]{1,0:T(8,128)}, u32[]{:S(2)}, u32[]{:S(2)}) collective-permute-start(f32[1024,512]{1,0:T(8,128)} %collective-permute-done.17.refs_5_), channel_id=1, source_target_pairs={{2,3},{6,7},{10,11},{14,15},{18,19},{22,23},{26,27},{30,31}} | collective-permute-start | bytes 6291464 | tf_op jit(solution)/shard_map/ppermute | solution.py:346
  308.3 10.8 %copy-start.1 = (f32[4,256,512]{2,1,0:T(8,128)S(1)}, f32[4,256,512]{2,1,0:T(8,128)}, u32[]{:S(2)}) copy-start(f32[4,256,512]{2,1,0:T(8,128)} %shard_map.100.refs_1_) | copy-start | bytes 6291460
  346.9 80.4 %collective-permute-start.19 = (f32[2,512,512]{2,1,0:T(8,128)}, f32[2,512,512]{2,1,0:T(8,128)S(1)}, u32[]{:S(2)}, u32[]{:S(2)}) collective-permute-start(f32[2,512,512]{2,1,0:T(8,128)} %shard_map.107), channel_id=1, source_target_pairs={{0,4},{4,0},{1,5},{5,1},{2,6},{6,2},{3,7},{7,3},{8,12},{12,8},{9,1... | collective-permute-start | bytes 6291464 | tf_op jit(solution)/shard_map/ppermute | solution.py:332
  362.6 54.5 %copy-start.3 = (f32[4,256,256]{2,1,0:T(8,128)S(1)}, f32[4,256,256]{2,1,0:T(8,128)}, u32[]{:S(2)}) copy-start(f32[4,256,256]{2,1,0:T(8,128)} %add.44.refs_1_) | copy-start | bytes 3145732
  362.6 53.1 %collective-permute-start.14 = (f32[4,256,256]{2,1,0:T(8,128)}, f32[4,256,256]{2,1,0:T(8,128)S(1)}, u32[]{:S(2)}, u32[]{:S(2)}) collective-permute-start(f32[4,256,256]{2,1,0:T(8,128)} %shard_map.103), channel_id=1, source_target_pairs={{0,4},{4,0},{1,5},{5,1},{2,6},{6,2},{3,7},{7,3},{8,12},{12,8},{9,1... | collective-permute-start | bytes 3145736 | tf_op jit(solution)/shard_map/ppermute | solution.py:332
  (2 other events, 6.3 us)
Sparse Core Ops, SparseCore 0:
  27.6 121.9 all-gather.4
  151.9 87.1 all-gather.6

commit v4 on v3

--- a/solution.py
+++ b/solution.py
@@ -24,7 +24,7 @@
 
 class Layout:
     def __init__(self, rows, leaves, cols, half, width):
-        self.leaves, self.cols, self.half, self.width = leaves, cols, half, width
+        self.rows, self.leaves, self.cols, self.half, self.width = rows, leaves, cols, half, width
         self.part = half // leaves
         self.span = width * cols
         self.counts, self.holder, self.source = [], [], []
@@ -59,6 +59,7 @@
 
 def fetch_entry(lay, pat, tab, gathered, t, sems, k):
     leaf, col, sub = place_of(lay, pat, k)
+    lanes = pl.ds(pl.multiple_of(sub * BLK, BLK), BLK)
     for s in range(2):
         here = tab[s, leaf, 0] >= 0
 
@@ -68,15 +69,11 @@
                 entry = tab[s, leaf, j]
                 slot = entry // (lay.leaves + 1)
                 position = entry - slot * (lay.leaves + 1)
-                for which in range(len(gathered)):
-
-                    @pl.when(sub == which)
-                    def _():
-                        pltpu.make_async_copy(
-                            gathered[which].at[slot * lay.cols + col, position],
-                            t.at[k, s, pl.ds(j * lay.part, lay.part)],
-                            sems.at[k, s],
-                        ).start()
+                pltpu.make_async_copy(
+                    gathered.at[slot * lay.cols + col, position, :, lanes],
+                    t.at[k, s, pl.ds(j * lay.part, lay.part)],
+                    sems.at[k, s],
+                ).start()
 
         @pl.when(jnp.logical_not(here))
         def _():
@@ -102,11 +99,9 @@
     return dot(turned_high[s], high) + dot(turned_low[s], high) + dot(turned_high[s], low)
 
 
-def panel_kernel(lay, rows, pat, tab, order, *refs):
-    count = lay.width // BLK
-    gathered, p_ref = refs[:count], refs[count]
-    outs = refs[count + 1 : count + rows]
-    turned_high, turned_low, t, th, tl, image, sems = refs[count + rows :]
+def panel_kernel(lay, rows, pat, tab, order, gathered, p_ref, *refs):
+    outs = refs[: rows - 1]
+    turned_high, turned_low, t, th, tl, image, sems = refs[rows - 1 :]
     number = t.shape[0]
     each = number // 2 // rows
 
@@ -150,9 +145,7 @@
                     out[...] += back_product(turned_high, turned_low, th[kp, s], tl[kp, s], s).T
 
 
-def own_panel_kernel(lay, rows, pat, tab, order, *refs):
-    count = lay.width // BLK
-    gathered, (turned_high, turned_low, out_ref, t, sems) = refs[:count], refs[count:]
+def own_panel_kernel(lay, rows, pat, tab, order, gathered, turned_high, turned_low, out_ref, t, sems):
     each = t.shape[0] // 2 // rows
     first = order[rows - 1] * each
 
@@ -192,7 +185,7 @@
     result = pl.pallas_call(
         functools.partial(panel_kernel, lay, rows),
         out_shape=[block] * (rows - 1) + [turned] * 2,
-        in_specs=[SMEM] * 3 + [ANY] * len(gathered) + [VMEM],
+        in_specs=[SMEM] * 3 + [ANY, VMEM],
         out_specs=[VMEM] * (rows + 1),
         scratch_shapes=[
             pltpu.VMEM((number, 2, half, BLK), jnp.float32),
@@ -203,7 +196,7 @@
         ],
         compiler_params=pltpu.CompilerParams(vmem_limit_bytes=VMEM_BYTES),
         cost_estimate=estimate(18 * half * number * BLK * wide, 2 * half * number * BLK),
-    )(pattern, table, order, *gathered, normed)
+    )(pattern, table, order, gathered, normed)
     return result[: rows - 1], result[rows - 1 :]
 
 
@@ -213,7 +206,7 @@
     return pl.pallas_call(
         functools.partial(own_panel_kernel, lay, rows),
         out_shape=jax.ShapeDtypeStruct((number // 2 // rows, 2 * BLK, wide), jnp.float32),
-        in_specs=[SMEM] * 3 + [ANY] * len(gathered) + [VMEM] * 2,
+        in_specs=[SMEM] * 3 + [ANY, VMEM, VMEM],
         out_specs=VMEM,
         scratch_shapes=[
             pltpu.VMEM((number, 2, half, BLK), jnp.float32),
@@ -221,60 +214,81 @@
         ],
         compiler_params=pltpu.CompilerParams(vmem_limit_bytes=VMEM_BYTES),
         cost_estimate=estimate(6 * half * number * BLK * wide, half * number * BLK),
-    )(pattern, table, order, *gathered, *turned)
-
-
-def top_kernel(lay, rows, tab, info, g_ref, own_ref, *refs):
-    outs, own_turned = refs[:rows], refs[rows]
-    blocks = g_ref.shape[0]
-    parts = lay.leaves
-    each = blocks // 2 // rows
-    for s in range(2):
-
-        @pl.loop(0, parts)
-        def _(j):
-            high, low = halves(own_ref[s, j].T)
-            own_turned[s, j] = jnp.concatenate([high, low, high], axis=1)
-
-    for a in range(rows):
+    )(pattern, table, order, gathered, *turned)
+
+
+def top_kernel(lay, chunks, chunk, tab, dests, leaf_ref, g_ref, own_ref, *refs):
+    count = dests.shape[0]
+    outs, (own_turned, held, sems) = refs[:count], refs[count:]
+    parts, part = lay.leaves, lay.part
+    each = outs[0].shape[0]
+
+    def place(a, i):
+        block = (dests[a] * chunks + chunk) * each + i
+        leaf = block // lay.cols
+        return leaf, block - leaf * lay.cols
+
+    def wanted(leaf, s):
+        return jnp.logical_and(tab[s, leaf, 0] >= 0, tab[s, leaf_ref[0], 0] >= 0)
+
+    for a in range(count):
 
         @pl.loop(0, each)
         def _(i):
-            block = 2 * (info[a] * each + i)
-            leaf = block // lay.cols
-            col = block - leaf * lay.cols
-            out = outs[a].at[i]
-            out[...] = jnp.zeros(out.shape, out.dtype)
+            leaf, col = place(a, i)
             for s in range(2):
 
-                @pl.when(jnp.logical_and(tab[s, leaf, 0] >= 0, tab[s, info[rows], 0] >= 0))
+                @pl.when(wanted(leaf, s))
                 def _():
-                    total = None
                     for j in range(parts):
                         entry = tab[s, leaf, j]
                         slot = entry // (parts + 1)
                         position = entry - slot * (parts + 1)
-                        at = slot * lay.cols + col
-                        both = jnp.concatenate([g_ref[at, position], g_ref[at + 1, position]], axis=1)
-                        high, low = halves(both)
-                        term = dot(own_turned[s, j], jnp.concatenate([high, high, low], axis=0))
-                        total = term if total is None else total + term
+                        pltpu.make_async_copy(
+                            g_ref.at[slot * lay.cols + col, position],
+                            held.at[a, i, s, pl.ds(j * part, part)],
+                            sems.at[a, i, s],
+                        ).start()
+
+    for s in range(2):
+        high, low = halves(own_ref[s].T)
+        own_turned[s, 0] = high
+        own_turned[s, 1] = low
+
+    for a in range(count):
+
+        @pl.loop(0, each)
+        def _(i):
+            leaf, col = place(a, i)
+            out = outs[a].at[i]
+            out[...] = jnp.zeros(out.shape, out.dtype)
+            for s in range(2):
+
+                @pl.when(wanted(leaf, s))
+                def _():
+                    pltpu.make_async_copy(held.at[a, i, s], held.at[a, i, s], sems.at[a, i, s]).wait()
+                    high, low = halves(held[a, i, s])
+                    total = dot(own_turned[s, 0], high) + dot(own_turned[s, 1], high) + dot(own_turned[s, 0], low)
                     out[...] += total.T
 
 
-def top_product(lay, table, info, gathered, own):
-    blocks, rows = gathered.shape[0], info.shape[0] - 1
-    parts, part, width = lay.leaves, lay.part, lay.width
-    block = jax.ShapeDtypeStruct((blocks // 2 // rows, 2 * BLK, width), jnp.float32)
+def top_product(lay, table, dests, me_leaf, gathered, own, chunks, chunk):
+    count, width, half = dests.shape[0], lay.width, lay.half
+    each = gathered.shape[0] // lay.rows // chunks
+    block = jax.ShapeDtypeStruct((each, width, width), jnp.float32)
     return pl.pallas_call(
-        functools.partial(top_kernel, lay, rows),
-        out_shape=[block] * rows,
-        in_specs=[SMEM, SMEM, VMEM, VMEM],
-        out_specs=[VMEM] * rows,
-        scratch_shapes=[pltpu.VMEM((2, parts, width, 3 * part), jnp.bfloat16)],
+        functools.partial(top_kernel, lay, chunks, chunk),
+        out_shape=[block] * count,
+        in_specs=[SMEM] * 3 + [ANY, VMEM],
+        out_specs=[VMEM] * count,
+        scratch_shapes=[
+            pltpu.VMEM((2, 2, width, half), jnp.bfloat16),
+            pltpu.VMEM((count, each, 2, half, width), jnp.float32),
+            pltpu.SemaphoreType.DMA((count, each, 2)),
+        ],
         compiler_params=pltpu.CompilerParams(vmem_limit_bytes=VMEM_BYTES),
-        cost_estimate=estimate(12 * lay.half * blocks * BLK * width, gathered.size),
-    )(table, info, gathered, own)
+        cost_estimate=estimate(12 * half * count * each * width * width, 2 * half * count * each * width),
+    )(table, dests, me_leaf, gathered, own)
 
 
 def diagonal_kernel(cols, info, *refs):
@@ -326,11 +340,9 @@
     )(value, *earlier)
 
 
-def sum_over_rows(sent, own):
+def send_over_rows(sent):
     rows = lax.axis_size("row")
-    for a, value in enumerate(sent):
-        own = own + lax.ppermute(value, "row", [(i, (i + a + 1) % rows) for i in range(rows)])
-    return own
+    return [lax.ppermute(value, "row", [(i, (i + a + 1) % rows) for i in range(rows)]) for a, value in enumerate(sent)]
 
 
 def per_device(lay, top_inverse, pattern, panel, diag_inverse):
@@ -358,53 +370,47 @@
                 is_moved[r, slot] = True
                 pairs.append((leaf * rows + r, slot * rows + r))
     moved_here = jnp.asarray(is_moved)[me_row, me_leaf]
-    gathered, own, held = [], [], None
-    for sub in range(width // BLK):
-        lanes = slice(sub * BLK, (sub + 1) * BLK)
-        lower, upper = top_inverse[half:, lanes], top_inverse[:half, lanes]
-        if held is not None:
-            lower, upper = after(lower, held), after(upper, held)
-        swapped = lax.ppermute(upper, "row", [(r, rows - 1 - r) for r in range(rows)])
-        moved = lax.ppermute(lower, ("leaf", "row"), pairs) if pairs else lower
-        whole = jnp.where(me_leaf < second, swapped, jnp.where(moved_here, moved, lower))
-        extra = lower[:part]
-        for j in range(1, parts):
-            sent = lax.ppermute(lower[j * part : (j + 1) * part], "leaf", [(0, j)])
-            extra = jnp.where(me_leaf == j, sent, extra)
-        earlier = held
-        held = jnp.concatenate([whole.reshape(parts, part, BLK), extra[None]], axis=0)
-        if earlier is not None:
-            held = after(held, right[0], left[0])
-        gathered.append(lax.all_gather(held, ("leaf", "col"), axis=0, tiled=False))
-        own.append(jnp.stack([lower, swapped]))
-    own = jnp.concatenate(own, axis=2).reshape(2, parts, part, width)
-
-    right[0], left[0] = after(right[0], gathered[-1]), after(left[0], gathered[-1])
+    lower, upper = top_inverse[half:], top_inverse[:half]
+    swapped = lax.ppermute(upper, "row", [(r, rows - 1 - r) for r in range(rows)])
+    moved = lax.ppermute(lower, ("leaf", "row"), pairs) if pairs else lower
+    whole = jnp.where(me_leaf < second, swapped, jnp.where(moved_here, moved, lower))
+    extra = lower[:part]
+    for j in range(1, parts):
+        extra = jnp.where(me_leaf == j, lax.ppermute(lower[j * part : (j + 1) * part], "leaf", [(0, j)]), extra)
+    held = jnp.concatenate([whole.reshape(parts, part, width), extra[None]], axis=0)
+    gathered = lax.all_gather(after(held, right[0], left[0]), ("leaf", "col"), axis=0, tiled=False)
+    own = jnp.stack([lower, swapped])
+
+    right[0], left[0] = after(right[0], gathered), after(left[0], gathered)
     for step in range(1, cols - 1):
         right.append(hop(right[-1], step, 1))
         left.append(hop(left[-1], step, -1))
 
+    chunks = 2
     order = ((me_row + 1 + jnp.arange(rows)) % rows).astype(jnp.int32)
-    info = jnp.append(order, me_leaf.astype(jnp.int32))
-    tops = [top_product(lay, table, info, part_of, own) for part_of in gathered[:-1]]
-    tops = [sum_over_rows(top[:-1], top[-1]) for top in tops]
-    if tops:
-        order = after(order, tops[-1])
-
-    sent, turned = panel_product(lay, pattern[0], table, order, gathered, normed)
-    kept = own_panel_product(lay, pattern[0], table, order, gathered, turned)
-    sigma_panel = -sum_over_rows(sent, kept).reshape(-1, normed.shape[1])
-
-    *away, here = top_product(lay, table, after(info, kept), gathered[-1], own)
-    tops.append(sum_over_rows([after(value, sigma_panel) for value in away], here))
-    sigma_top = jnp.concatenate([top.reshape(-1, 1, BLK, width) for top in tops], axis=1).reshape(-1, width)
-
-    terms = [
-        diagonal_product(jnp.stack([order[a], me_col.astype(jnp.int32)]), rows, left, own_rows, right, sigma_panel)
-        for a in range(rows)
-    ]
-    update = sum_over_rows(terms[:-1], terms[-1])
+    leaf_here = me_leaf.astype(jnp.int32)[None]
+    top_args = (leaf_here, gathered, own, chunks)
+    early = top_product(lay, table, order[: rows - 1], *top_args, 0)
+    early_in = send_over_rows(early)
+    sent, turned = panel_product(lay, pattern[0], table, after(order, *early), gathered, normed)
+    sent_in = send_over_rows(sent)
+    kept = own_panel_product(lay, pattern[0], table, after(order, *early_in), gathered, turned)
+    sigma_panel = -sum(sent_in, kept).reshape(-1, normed.shape[1])
+    late = top_product(lay, table, after(order[: rows - 1], kept), *top_args, 1)
+    late_in = send_over_rows([after(value, sigma_panel) for value in late])
+
+    def diagonal(a, sigma):
+        return diagonal_product(jnp.stack([order[a], me_col.astype(jnp.int32)]), rows, left, own_rows, right, sigma)
+
+    terms = [diagonal(a, after(sigma_panel, *late)) for a in range(rows - 1)]
+    terms_in = send_over_rows([after(term, *late_in) for term in terms])
+    update = sum(terms_in, diagonal(rows - 1, after(sigma_panel, *terms)))
     sigma_diag = diag_inverse[0] - update.reshape(diag_inverse.shape[1:])
+
+    last = after(order[rows - 1 :], *terms)
+    tops = [top_product(lay, table, last, *top_args, chunk)[0] for chunk in range(chunks)]
+    tops = [sum(early_in, tops[0]), sum(late_in, tops[1])]
+    sigma_top = jnp.concatenate(tops, axis=0).reshape(-1, width)
     return (sigma_top, sigma_panel[None], sigma_diag[None])
 
 

time: 439 us -> 401 us (0.913); the launches traced: 438 us -> 393 us
  waiting for transfers between devices: 268 us -> 223 us
  starting transfers between devices: 39 us -> 32 us
  Pallas kernels: 82.1 us -> 87.4 us
    all_gather x2 -> x1, waiting for transfers between devices: 56.9 us -> 114 us  [per_device(): lax.all_gather(after(held, right[0], left[0]), ('leaf', 'col'), axis=0, t...]
    ppermute x3, waiting for transfers between devices: 57.2 us -> 1.19 us  [hop(): lax.ppermute(value, 'col', [(i, i + 1) for i in range(step, cols - 1)])]
    ppermute x3, waiting for transfers between devices: 54.2 us -> 20.8 us  [hop(): lax.ppermute(value, 'col', [(i, i - 1) for i in range(1, cols - step)])]
    ppermute x10 -> x7, waiting for transfers between devices: 99.5 us -> 86.9 us  [the longest x4 74.1 us: send_over_rows(): lax.ppermute(value, 'row', [(i, (i + a + 1) % rows) for i in range(rows)])]
    ppermute x10 -> x7, starting transfers between devices: 22.7 us -> 14.7 us  [the longest x4 9.02 us: send_over_rows(): lax.ppermute(value, 'row', [(i, (i + a + 1) % rows) for i in range(rows)])]
    unnamed x24 -> x33, local copies, waits for them, and re-layouts: 0.06 us -> 7.15 us
    pallas_call x2 -> x4, Pallas kernels: 28.2 us -> 31.3 us  [top_product(): pl.pallas_call(functools.partial(top_kernel, lay, chunks, chunk), out_sha...]
  transfers between devices with their start and end apart: 22 -> 16, of which waited for: 14 -> 9; matrix products, arithmetic and copies ran while one was open for 6% -> 6% of each run, Pallas kernels for 17% -> 22%
where the time goes in v4:
time: 401 us; the launch traced here: 393 us
  waiting for transfers between devices  223 us (56%)
  Pallas kernels  87.4 us (22%)
  starting transfers between devices  32 us (8%)
  other arithmetic  20.8 us (5%)
  between operations  15.1 us (4%)
  local copies, waits for them, and re-layouts  15 us (4%)
    all_gather x1, waiting for transfers between devices, per_device(): lax.all_gather(after(held, right[0], left[0]), ('leaf', 'col'), axis=0, t...  114 us
    ppermute x4, waiting for transfers between devices, send_over_rows(): lax.ppermute(value, 'row', [(i, (i + a + 1) % rows) for i in range(rows)])  74.1 us
    pallas_call x4, Pallas kernels, top_product(): pl.pallas_call(functools.partial(top_kernel, lay, chunks, chunk), out_sha...  31.3 us
    pallas_call x1, Pallas kernels, panel_product(): pl.pallas_call(functools.partial(panel_kernel, lay, rows), out_shape=[blo...  22.6 us
    ppermute x3, waiting for transfers between devices, hop(): lax.ppermute(value, 'col', [(i, i - 1) for i in range(1, cols - step)])  20.8 us
    pallas_call x2, Pallas kernels, diagonal_product(): pl.pallas_call(functools.partial(diagonal_kernel, cols), out_shape=jax.Sh...  17 us
    pallas_call x1, Pallas kernels, own_panel_product(): pl.pallas_call(functools.partial(own_panel_kernel, lay, rows), out_shape=...  14.2 us
    ppermute x3, waiting for transfers between devices, per_device(): lax.ppermute(lower[j * part:(j + 1) * part], 'leaf', [(0, j)])  12.8 us
  transfers between devices with their start and end apart: 16, of which 9 were waited for; matrix products, arithmetic and copies ran while one was open for 6% of the time, Pallas kernels for 22%

profile of v4, /device:TPU:0, one launch (start us, length us, event | category | flops | bytes accessed | tf_op | source)
XLA Modules:
  0.0 393.2 jit_solution(17998823005055558430)
XLA Ops:
  7.2 3.2 dynamic-slice_bitcast_fusion.refs_3_
  11.9 5.7 %collective-permute-start.6 = (f32[1024,512]{1,0:T(8,128)}, f32[1024,512]{1,0:T(8,128)S(1)}, u32[]{:S(2)}, u32[]{:S(2)}) collective-permute-start(f32[1024,512]{1,0:T(8,128)} %dynamic-slice_bitcast_fusion.refs_3_), channel_id=1, source_target_pairs={{0,1},{1,2},{2,3},{4,5},{5,6},{6,7},{8,9},{9,10},{10,11},{12,13},{... | collective-permute-start | bytes 6291464 | tf_op jit(solution)/shard_map/ppermute | solution.py:358
  19.0 2.0 collective-permute-start.1
  21.0 1.6 collective-permute-start.2
  23.4 1.7 collective-permute-start.3
  25.0 6.7 %collective-permute-done.3 = f32[256,256]{1,0:T(8,128)S(1)} collective-permute-done((f32[256,256]{1,0:T(8,128)S(1)}, f32[256,256]{1,0:T(8,128)S(1)}, u32[]{:S(2)}, u32[]{:S(2)}) %collective-permute-start.3) | collective-permute-done | bytes 262176 | tf_op jit(solution)/shard_map/ppermute | solution.py:379
  31.8 2.0 collective-permute-start.4
  33.8 6.1 %collective-permute-done.4 = f32[256,256]{1,0:T(8,128)} collective-permute-done((f32[256,256]{1,0:T(8,128)S(1)}, f32[256,256]{1,0:T(8,128)}, u32[]{:S(2)}, u32[]{:S(2)}) %collective-permute-start.4) | collective-permute-done | bytes 262176 | tf_op jit(solution)/shard_map/ppermute | solution.py:379
  39.8 2.0 collective-permute-start.5
  44.8 3.0 slice_bitcast_fusion
  49.0 12.5 %collective-permute-done.refs_2_.refs_0_ = f32[1024,512]{1,0:T(8,128)} collective-permute-done((f32[1024,512]{1,0:T(8,128)}, f32[1024,512]{1,0:T(8,128)}, u32[]{:S(2)}, u32[]{:S(2)}) %collective-permute-start) | collective-permute-done | bytes 2097184 | tf_op jit(solution)/shard_map/ppermute | solution.py:359
  65.7 2.7 pad_maximum_fusion.own_ref
  68.4 114.0 %all-gather.3.cloned.1.call-done = f32[80,256,256]{2,1,0:T(8,128)} async-done(((f32[5,256,256]{2,1,0:T(8,128)}), f32[80,256,256]{2,1,0:T(8,128)}) %all-gather.3.cloned.1.call-update) | async-done | bytes 20971536 | tf_op jit(solution)/shard_map/all_gather | solution.py:381
  183.6 2.1 collective-permute-start.9
  185.7 7.3 %shard_map.97.refs_1_ = f32[4,256,256]{2,1,0:T(8,128)} custom-call(s32[2,4,4]{2,1,0:T(4,128)} %dynamic-slice_bitcast_fusion.1.tab, s32[1]{0:T(128)} %get-tuple-element.16.dests.refs_0_, s32[1]{0:T(128)} %bitcast.9.leaf_ref, f32[16,5,256,256]{3,2,1,0:T(8,128)} %bitcast.25, f32[2,1024,256]{2,1,0:T(8,128)} %pad_maximum_fusion.own_ref), custom_call_target="tpu_custom_call" | custom-call | flops 3221225472 | bytes 8388608 | tf_op jit(solution)/shard_map/pallas_call | solution.py:279
  193.0 22.6 %shard_map.100 = (f32[4,256,512]{2,1,0:T(8,128)}, bf16[2,512,1024]{2,1,0:T(8,128)(2,1)}, bf16[2,512,1024]{2,1,0:T(8,128)(2,1)}) custom-call(s32[16]{0:T(128)} %bitcast.40, s32[2,4,4]{2,1,0:T(4,128)} %dynamic-slice_bitcast_fusion.1.tab, s32[2]{0:T(128)} %shard_map.99.order, f32[16,5,256,256]{3,2,1,0:T(8,128)} %bitcast.26, f32[2048,512]{1,0:T(8,128)} %bitcast.39), custom_call_target="tpu_custom_call" | custom-call | flops 19327352832 | bytes 16777216 | tf_op jit(solution)/shard_map/pallas_call | solution.py:185
  215.6 8.3 %collective-permute-start.12 = (f32[4,256,512]{2,1,0:T(8,128)}, f32[4,256,512]{2,1,0:T(8,128)}, u32[]{:S(2)}, u32[]{:S(2)}) collective-permute-start(f32[4,256,512]{2,1,0:T(8,128)} %get-tuple-element.8), channel_id=1, source_target_pairs={{0,4},{4,0},{1,5},{5,1},{2,6},{6,2},{3,7},{7,3},{8,12},{12,8},{9,1... | collective-permute-start | bytes 6291464 | tf_op jit(solution)/shard_map/ppermute | solution.py:345
  224.0 8.3 %collective-permute-done.7.refs_1_ = f32[1024,512]{1,0:T(8,128)} collective-permute-done((f32[1024,512]{1,0:T(8,128)}, f32[1024,512]{1,0:T(8,128)}, u32[]{:S(2)}, u32[]{:S(2)}) %collective-permute-start.7) | collective-permute-done | bytes 2097184 | tf_op jit(solution)/shard_map/ppermute | solution.py:359
  233.6 2.0 collective-permute-start.10
  237.0 53.1 %collective-permute-done.11.refs_1_ = f32[4,256,256]{2,1,0:T(8,128)S(1)} collective-permute-done((f32[4,256,256]{2,1,0:T(8,128)S(1)}, f32[4,256,256]{2,1,0:T(8,128)S(1)}, u32[]{:S(2)}, u32[]{:S(2)}) %collective-permute-start.11) | collective-permute-done | bytes 1048608 | tf_op jit(solution)/shard_map/ppermute | solution.py:345
  291.0 14.2 %shard_map.101.refs_1_ = f32[4,256,512]{2,1,0:T(8,128)} custom-call(s32[16]{0:T(128)} %bitcast.41, s32[2,4,4]{2,1,0:T(4,128)} %dynamic-slice_bitcast_fusion.1.tab, s32[2]{0:T(128)} %shard_map.98.order, f32[16,5,256,256]{3,2,1,0:T(8,128)} %bitcast.27, bf16[2,512,1024]{2,1,0:T(8,128)(2,1)} %get-tuple-element.6.turned_high, ...), custom_call_target="tpu_custom_call" | custom-call | flops 6442450944 | bytes 8388608 | tf_op jit(solution)/shard_map/pallas_call | solution.py:206
  306.5 4.5 %shard_map.103.refs_1_.refs_0_ = f32[4,256,256]{2,1,0:T(8,128)} custom-call(s32[2,4,4]{2,1,0:T(4,128)} %dynamic-slice_bitcast_fusion.1.tab, s32[1]{0:T(128)} %shard_map.102.dests, s32[1]{0:T(128)} %bitcast.9.leaf_ref, f32[16,5,256,256]{3,2,1,0:T(8,128)} %bitcast.28, f32[2,1024,256]{2,1,0:T(8,128)} %pad_maximum_fusion.own_ref), custom_call_target="tpu_custom_call" | custom-call | flops 3221225472 | bytes 8388608 | tf_op jit(solution)/shard_map/pallas_call | solution.py:279
  311.0 2.2 add_negate_fusion
  318.3 8.5 %shard_map.105.refs_1_.refs_0_ = f32[2,512,512]{2,1,0:T(8,128)} custom-call(s32[2]{0:T(128)} %pad_add_fusion.info, f32[1024,512]{1,0:T(8,128)} %shard_map.95.refs_0_, f32[1024,512]{1,0:T(8,128)} %collective-permute-done.7.refs_1_, f32[1024,512]{1,0:T(8,128)} %collective-permute-done.8.refs_2_, f32[1024,512]{1,0:T(8,128)} %dynamic-slice_bitcast_fusion.refs_3_, ...), custom_call_target="tpu_custom_call" | custom-call | flops 3221225472 | bytes 6291456 | tf_op jit(solution)/shard_map/pallas_call | solution.py:321
  327.9 9.7 %collective-permute-done.13.refs_1_ = f32[4,256,256]{2,1,0:T(8,128)S(1)} collective-permute-done((f32[4,256,256]{2,1,0:T(8,128)}, f32[4,256,256]{2,1,0:T(8,128)S(1)}, u32[]{:S(2)}, u32[]{:S(2)}) %collective-permute-start.13) | collective-permute-done | bytes 1048608 | tf_op jit(solution)/shard_map/ppermute | solution.py:345
  338.8 9.7 %shard_map.108 = f32[4,256,256]{2,1,0:T(8,128)} custom-call(s32[2,4,4]{2,1,0:T(4,128)} %dynamic-slice_bitcast_fusion.1.tab, s32[1]{0:T(128)} %shard_map.106.dests, s32[1]{0:T(128)} %bitcast.9.leaf_ref, f32[16,5,256,256]{3,2,1,0:T(8,128)} %bitcast.29, f32[2,1024,256]{2,1,0:T(8,128)} %pad_maximum_fusion.own_ref), custom_call_target="tpu_custom_call" | custom-call | flops 3221225472 | bytes 8388608 | tf_op jit(solution)/shard_map/pallas_call | solution.py:279
  349.9 9.8 %shard_map.107 = f32[4,256,256]{2,1,0:T(8,128)} custom-call(s32[2,4,4]{2,1,0:T(4,128)} %dynamic-slice_bitcast_fusion.1.tab, s32[1]{0:T(128)} %shard_map.106.dests, s32[1]{0:T(128)} %bitcast.9.leaf_ref, f32[16,5,256,256]{3,2,1,0:T(8,128)} %bitcast.30, f32[2,1024,256]{2,1,0:T(8,128)} %pad_maximum_fusion.own_ref), custom_call_target="tpu_custom_call" | custom-call | flops 3221225472 | bytes 8388608 | tf_op jit(solution)/shard_map/pallas_call | solution.py:279
  361.1 1.5 pad_maximum_fusion.1
  362.6 8.5 %shard_map.111 = f32[2,512,512]{2,1,0:T(8,128)} custom-call(s32[2]{0:T(128)} %pad_add_fusion.1.info, f32[1024,512]{1,0:T(8,128)} %shard_map.95.refs_0_, f32[1024,512]{1,0:T(8,128)} %collective-permute-done.7.refs_1_, f32[1024,512]{1,0:T(8,128)} %collective-permute-done.8.refs_2_, f32[1024,512]{1,0:T(8,128)} %dynamic-slice_bitcast_fusion.refs_3_, ...), custom_call_target="tpu_custom_call" | custom-call | flops 3221225472 | bytes 6291456 | tf_op jit(solution)/shard_map/pallas_call | solution.py:321
  371.1 11.3 %collective-permute-done.14 = f32[2,512,512]{2,1,0:T(8,128)S(1)} collective-permute-done((f32[2,512,512]{2,1,0:T(8,128)}, f32[2,512,512]{2,1,0:T(8,128)S(1)}, u32[]{:S(2)}, u32[]{:S(2)}) %collective-permute-start.14) | collective-permute-done | bytes 2097184 | tf_op jit(solution)/shard_map/ppermute | solution.py:345
  382.4 2.1 add.48
  384.5 1.8 bitcast_subtract_fusion
  (73 shorter events, 27.7 us)
Async XLA Ops:
  7.2 175.2 %all-gather.3.cloned.1.call-start = ((), (), s32[]{:S(2)}) async-start(), calls=%async_computation | async-start | bytes 22282240 | tf_op jit(solution)/shard_map/all_gather | solution.py:381
  7.2 10.4 %copy-start.4 = (f32[2048,256]{1,0:T(8,128)S(1)}, f32[2048,256]{1,0:T(8,128)}, u32[]{:S(2)}) copy-start(f32[2048,256]{1,0:T(8,128)} %param.7) | copy-start | bytes 6291460
  10.5 31.3 %copy-start.14 = (s32[2]{0:T(128)S(1)}, s32[2]{0:T(128)}, u32[]{:S(2)}) copy-start(s32[2]{0:T(128)} %constant.45.clone) | copy-start | bytes 28
  10.5 32.7 %copy-start.13 = (pred[2,4]{1,0:T(4,128)(4,1)S(1)}, pred[2,4]{1,0:T(4,128)(4,1)}, u32[]{:S(2)}) copy-start(pred[2,4]{1,0:T(4,128)(4,1)} %constant.46.clone) | copy-start | bytes 28
  10.5 51.0 %collective-permute-start = (f32[1024,512]{1,0:T(8,128)}, f32[1024,512]{1,0:T(8,128)}, u32[]{:S(2)}, u32[]{:S(2)}) collective-permute-start(f32[1024,512]{1,0:T(8,128)} %dynamic-slice_bitcast_fusion.refs_3_), channel_id=1, source_target_pairs={{1,0},{2,1},{3,2},{5,4},{6,5},{7,6},{9,8},{10,9},{11,10},{13,12},{... | collective-permute-start | bytes 6291464 | tf_op jit(solution)/shard_map/ppermute | solution.py:359
  11.9 50.8 %collective-permute-start.6 = (f32[1024,512]{1,0:T(8,128)}, f32[1024,512]{1,0:T(8,128)S(1)}, u32[]{:S(2)}, u32[]{:S(2)}) collective-permute-start(f32[1024,512]{1,0:T(8,128)} %dynamic-slice_bitcast_fusion.refs_3_), channel_id=1, source_target_pairs={{0,1},{1,2},{2,3},{4,5},{5,6},{6,7},{8,9},{9,10},{10,11},{12,13},{... | collective-permute-start | bytes 6291464 | tf_op jit(solution)/shard_map/ppermute | solution.py:358
  19.0 25.8 %collective-permute-start.1 = (f32[1024,256]{1,0:T(8,128)}, f32[1024,256]{1,0:T(8,128)S(1)}, u32[]{:S(2)}, u32[]{:S(2)}) collective-permute-start(f32[1024,256]{1,0:T(8,128)} %get-tuple-element.12), channel_id=1, source_target_pairs={{0,4},{4,0},{1,5},{5,1},{2,6},{6,2},{3,7},{7,3},{8,12},{12,8},{9,1... | collective-permute-start | bytes 3145736 | tf_op jit(solution)/shard_map/ppermute | solution.py:374
  21.0 23.8 %collective-permute-start.2 = (f32[1024,256]{1,0:T(8,128)}, f32[1024,256]{1,0:T(8,128)}, u32[]{:S(2)}, u32[]{:S(2)}) collective-permute-start(f32[1024,256]{1,0:T(8,128)} %get-tuple-element.11), channel_id=1, source_target_pairs={{8,24},{9,25},{10,26},{11,27}} | collective-permute-start | bytes 3145736 | tf_op jit(solution)/shard_map/ppermute | solution.py:375
  23.4 8.4 %collective-permute-start.3 = (f32[256,256]{1,0:T(8,128)S(1)}, f32[256,256]{1,0:T(8,128)S(1)}, u32[]{:S(2)}, u32[]{:S(2)}) collective-permute-start(f32[256,256]{1,0:T(8,128)S(1)} %get-tuple-element.15), channel_id=1, source_target_pairs={{0,24},{1,25},{2,26},{3,27},{4,28},{5,29},{6,30},{7,31}} | collective-permute-start | bytes 786440 | tf_op jit(solution)/shard_map/ppermute | solution.py:379
  31.8 8.0 %collective-permute-start.4 = (f32[256,256]{1,0:T(8,128)S(1)}, f32[256,256]{1,0:T(8,128)}, u32[]{:S(2)}, u32[]{:S(2)}) collective-permute-start(f32[256,256]{1,0:T(8,128)S(1)} %get-tuple-element.14), channel_id=1, source_target_pairs={{0,16},{1,17},{2,18},{3,19},{4,20},{5,21},{6,22},{7,23}} | collective-permute-start | bytes 786440 | tf_op jit(solution)/shard_map/ppermute | solution.py:379
  39.8 4.0 %collective-permute-start.5 = (f32[256,256]{1,0:T(8,128)}, f32[256,256]{1,0:T(8,128)}, u32[]{:S(2)}, u32[]{:S(2)}) collective-permute-start(f32[256,256]{1,0:T(8,128)} %get-tuple-element.13), channel_id=1, source_target_pairs={{0,8},{1,9},{2,10},{3,11},{4,12},{5,13},{6,14},{7,15}} | collective-permute-start | bytes 786440 | tf_op jit(solution)/shard_map/ppermute | solution.py:379
  49.0 15.5 %copy-start.12 = (s32[2,2,4,4]{3,2,1,0:T(4,128)S(1)}, s32[2,2,4,4]{3,2,1,0:T(4,128)}, u32[]{:S(2)}) copy-start(s32[2,2,4,4]{3,2,1,0:T(4,128)} %constant.44.clone) | copy-start | bytes 772
  62.6 1.3 copy-start.2
  64.0 4.4 %copy-start.11 = (s32[2]{0:T(128)}, s32[2]{0:T(128)S(1)}, u32[]{:S(2)}) copy-start(s32[2]{0:T(128)S(1)} %and_select_fusion.refs_0_) | copy-start | bytes 28
  182.4 50.0 %collective-permute-start.7 = (f32[1024,512]{1,0:T(8,128)}, f32[1024,512]{1,0:T(8,128)}, u32[]{:S(2)}, u32[]{:S(2)}) collective-permute-start(f32[1024,512]{1,0:T(8,128)} %shard_map.95.refs_0_), channel_id=1, source_target_pairs={{1,0},{2,1},{5,4},{6,5},{9,8},{10,9},{13,12},{14,13},{17,16},{18,1... | collective-permute-start | bytes 6291464 | tf_op jit(solution)/shard_map/ppermute | solution.py:359
  183.6 50.0 %collective-permute-start.9 = (f32[1024,512]{1,0:T(8,128)}, f32[1024,512]{1,0:T(8,128)}, u32[]{:S(2)}, u32[]{:S(2)}) collective-permute-start(f32[1024,512]{1,0:T(8,128)} %shard_map.96.refs_4_), channel_id=1, source_target_pairs={{1,2},{2,3},{5,6},{6,7},{9,10},{10,11},{13,14},{14,15},{17,18},{18... | collective-permute-start | bytes 6291464 | tf_op jit(solution)/shard_map/ppermute | solution.py:358
  193.0 30.9 %copy-start.9 = (f32[4,256,256]{2,1,0:T(8,128)S(1)}, f32[4,256,256]{2,1,0:T(8,128)}, u32[]{:S(2)}) copy-start(f32[4,256,256]{2,1,0:T(8,128)} %shard_map.97.refs_1_) | copy-start | bytes 3145732
  215.6 95.4 %collective-permute-start.12 = (f32[4,256,512]{2,1,0:T(8,128)}, f32[4,256,512]{2,1,0:T(8,128)}, u32[]{:S(2)}, u32[]{:S(2)}) collective-permute-start(f32[4,256,512]{2,1,0:T(8,128)} %get-tuple-element.8), channel_id=1, source_target_pairs={{0,4},{4,0},{1,5},{5,1},{2,6},{6,2},{3,7},{7,3},{8,12},{12,8},{9,1... | collective-permute-start | bytes 6291464 | tf_op jit(solution)/shard_map/ppermute | solution.py:345
  223.9 66.1 %collective-permute-start.11 = (f32[4,256,256]{2,1,0:T(8,128)S(1)}, f32[4,256,256]{2,1,0:T(8,128)S(1)}, u32[]{:S(2)}, u32[]{:S(2)}) collective-permute-start(f32[4,256,256]{2,1,0:T(8,128)S(1)} %copy-done.9), channel_id=1, source_target_pairs={{0,4},{4,0},{1,5},{5,1},{2,6},{6,2},{3,7},{7,3},{8,12},{12,8},{9,1... | collective-permute-start | bytes 3145736 | tf_op jit(solution)/shard_map/ppermute | solution.py:345
  232.3 85.9 %collective-permute-start.8 = (f32[1024,512]{1,0:T(8,128)}, f32[1024,512]{1,0:T(8,128)}, u32[]{:S(2)}, u32[]{:S(2)}) collective-permute-start(f32[1024,512]{1,0:T(8,128)} %collective-permute-done.7.refs_1_), channel_id=1, source_target_pairs={{1,0},{5,4},{9,8},{13,12},{17,16},{21,20},{25,24},{29,28}} | collective-permute-start | bytes 6291464 | tf_op jit(solution)/shard_map/ppermute | solution.py:359
  233.6 84.6 %collective-permute-start.10 = (f32[1024,512]{1,0:T(8,128)}, f32[1024,512]{1,0:T(8,128)}, u32[]{:S(2)}, u32[]{:S(2)}) collective-permute-start(f32[1024,512]{1,0:T(8,128)} %collective-permute-done.9.refs_5_), channel_id=1, source_target_pairs={{2,3},{6,7},{10,11},{14,15},{18,19},{22,23},{26,27},{30,31}} | collective-permute-start | bytes 6291464 | tf_op jit(solution)/shard_map/ppermute | solution.py:358
  290.1 1.0 copy-start.7
  306.5 4.5 %copy-start.3 = (f32[4,256,512]{2,1,0:T(8,128)S(1)}, f32[4,256,512]{2,1,0:T(8,128)}, u32[]{:S(2)}) copy-start(f32[4,256,512]{2,1,0:T(8,128)} %shard_map.101.refs_1_) | copy-start | bytes 6291460
  313.2 2.0 copy-start
  315.2 1.7 copy-start.1
  315.2 22.3 %collective-permute-start.13 = (f32[4,256,256]{2,1,0:T(8,128)}, f32[4,256,256]{2,1,0:T(8,128)S(1)}, u32[]{:S(2)}, u32[]{:S(2)}) collective-permute-start(f32[4,256,256]{2,1,0:T(8,128)} %shard_map.109), channel_id=1, source_target_pairs={{0,4},{4,0},{1,5},{5,1},{2,6},{6,2},{3,7},{7,3},{8,12},{12,8},{9,1... | collective-permute-start | bytes 3145736 | tf_op jit(solution)/shard_map/ppermute | solution.py:345
  337.5 1.0 copy-start.5
  338.5 10.0 %copy-start.6 = (f32[4,256,256]{2,1,0:T(8,128)S(1)}, f32[4,256,256]{2,1,0:T(8,128)}, u32[]{:S(2)}) copy-start(f32[4,256,256]{2,1,0:T(8,128)} %copy-done.5) | copy-start | bytes 3145732
  338.5 43.9 %collective-permute-start.14 = (f32[2,512,512]{2,1,0:T(8,128)}, f32[2,512,512]{2,1,0:T(8,128)S(1)}, u32[]{:S(2)}, u32[]{:S(2)}) collective-permute-start(f32[2,512,512]{2,1,0:T(8,128)} %shard_map.112), channel_id=1, source_target_pairs={{0,4},{4,0},{1,5},{5,1},{2,6},{6,2},{3,7},{7,3},{8,12},{12,8},{9,1... | collective-permute-start | bytes 6291464 | tf_op jit(solution)/shard_map/ppermute | solution.py:345
  349.9 9.8 %copy-start.8 = (f32[4,256,256]{2,1,0:T(8,128)S(1)}, f32[4,256,256]{2,1,0:T(8,128)}, u32[]{:S(2)}) copy-start(f32[4,256,256]{2,1,0:T(8,128)} %copy-done.7) | copy-start | bytes 3145732
  371.1 13.4 %copy-start.10 = (f32[1,1024,512]{2,1,0:T(8,128)S(1)}, f32[1,1024,512]{2,1,0:T(8,128)}, u32[]{:S(2)}) copy-start(f32[1,1024,512]{2,1,0:T(8,128)} %param.10) | copy-start | bytes 6291460
Sparse Core Ops, SparseCore 0:
  64.1 118.2 all-gather.2

commit v5 on v4

--- a/solution.py
+++ b/solution.py
@@ -213,7 +213,7 @@
             pltpu.SemaphoreType.DMA((number, 2)),
         ],
         compiler_params=pltpu.CompilerParams(vmem_limit_bytes=VMEM_BYTES),
-        cost_estimate=estimate(6 * half * number * BLK * wide, half * number * BLK),
+        cost_estimate=estimate(24 * half * number * BLK * wide, half * number * BLK),
     )(pattern, table, order, gathered, *turned)
 
 
@@ -291,15 +291,15 @@
     )(table, dests, me_leaf, gathered, own)
 
 
-def diagonal_kernel(cols, info, *refs):
-    lefts, own, rights = refs[: cols - 1], refs[cols - 1], refs[cols : 2 * cols - 1]
-    sigma, out_ref, held, sems = refs[2 * cols - 1 :]
+def diagonal_kernel(reach, info, *refs):
+    lefts, own, rights = refs[:reach], refs[reach], refs[reach + 1 : 2 * reach + 1]
+    sigma, out_ref, held, sems = refs[2 * reach + 1 :]
     each = out_ref.shape[0]
     sources = {0: own}
-    for t in range(1, cols):
+    for t in range(1, reach + 1):
         sources[t], sources[-t] = lefts[t - 1], rights[t - 1]
     for i in range(each):
-        away = info[0] * each + i - info[1]
+        away = info[i] - info[each]
         for step, source in sources.items():
 
             @pl.when(away == step)
@@ -314,19 +314,18 @@
         out_ref[i] = total.T
 
 
-def diagonal_product(info, rows, lefts, own, rights, sigma):
-    cols = len(lefts) + 1
-    each = cols // rows
+def diagonal_product(blocks, me_col, lefts, own, rights, sigma):
+    each, reach = blocks.shape[0], len(lefts)
     depth, wide = sigma.shape
     return pl.pallas_call(
-        functools.partial(diagonal_kernel, cols),
+        functools.partial(diagonal_kernel, reach),
         out_shape=jax.ShapeDtypeStruct((each, wide, wide), jnp.float32),
-        in_specs=[SMEM] + [ANY] * (2 * cols - 1) + [VMEM],
+        in_specs=[SMEM] + [ANY] * (2 * reach + 1) + [VMEM],
         out_specs=VMEM,
         scratch_shapes=[pltpu.VMEM((each, depth, wide), jnp.float32), pltpu.SemaphoreType.DMA((each,))],
         compiler_params=pltpu.CompilerParams(vmem_limit_bytes=VMEM_BYTES),
         cost_estimate=estimate(6 * each * depth * wide * wide, (each + 1) * depth * wide),
-    )(info, *lefts, own, *rights, sigma)
+    )(jnp.append(blocks, me_col).astype(jnp.int32), *lefts, own, *rights, sigma)
 
 
 def after(value, *earlier):
@@ -357,8 +356,6 @@
         if way > 0:
             return lax.ppermute(value, "col", [(i, i + 1) for i in range(step, cols - 1)])
         return lax.ppermute(value, "col", [(i, i - 1) for i in range(1, cols - step)])
-
-    right, left = [hop(own_rows, 0, 1)], [hop(own_rows, 0, -1)]
 
     table = jnp.asarray(lay.table)[me_row]
     second = jnp.asarray([count[1] for count in lay.counts], jnp.int32)[me_row]
@@ -374,19 +371,23 @@
     swapped = lax.ppermute(upper, "row", [(r, rows - 1 - r) for r in range(rows)])
     moved = lax.ppermute(lower, ("leaf", "row"), pairs) if pairs else lower
     whole = jnp.where(me_leaf < second, swapped, jnp.where(moved_here, moved, lower))
-    extra = lower[:part]
-    for j in range(1, parts):
-        extra = jnp.where(me_leaf == j, lax.ppermute(lower[j * part : (j + 1) * part], "leaf", [(0, j)]), extra)
+    both = lower[: 2 * part]
+    for chip in range(2, leaves, 2):
+        both = jnp.where(me_leaf == chip, lax.ppermute(lower[chip * part : (chip + 2) * part], "leaf", [(0, chip)]), both)
+    other = lax.ppermute(both[part:], "leaf", [(chip, chip + 1) for chip in range(0, leaves, 2)])
+    extra = jnp.where(me_leaf % 2 == 0, both[:part], other)
     held = jnp.concatenate([whole.reshape(parts, part, width), extra[None]], axis=0)
-    gathered = lax.all_gather(after(held, right[0], left[0]), ("leaf", "col"), axis=0, tiled=False)
+    gathered = lax.all_gather(held, ("leaf", "col"), axis=0, tiled=False)
     own = jnp.stack([lower, swapped])
 
-    right[0], left[0] = after(right[0], gathered), after(left[0], gathered)
-    for step in range(1, cols - 1):
-        right.append(hop(right[-1], step, 1))
-        left.append(hop(left[-1], step, -1))
-
-    chunks = 2
+    start = after(own_rows, gathered)
+    right, left = [hop(start, 0, 1)], [hop(start, 0, -1)]
+
+    def hop_on(step, *earlier):
+        right.append(hop(after(right[-1], *earlier), step, 1))
+        left.append(hop(after(left[-1], *earlier), step, -1))
+
+    chunks, each = 2, cols // rows
     order = ((me_row + 1 + jnp.arange(rows)) % rows).astype(jnp.int32)
     leaf_here = me_leaf.astype(jnp.int32)[None]
     top_args = (leaf_here, gathered, own, chunks)
@@ -394,18 +395,33 @@
     early_in = send_over_rows(early)
     sent, turned = panel_product(lay, pattern[0], table, after(order, *early), gathered, normed)
     sent_in = send_over_rows(sent)
+    for step in range(1, cols // 2):
+        hop_on(step, *sent)
     kept = own_panel_product(lay, pattern[0], table, after(order, *early_in), gathered, turned)
     sigma_panel = -sum(sent_in, kept).reshape(-1, normed.shape[1])
     late = top_product(lay, table, after(order[: rows - 1], kept), *top_args, 1)
+    for step in range(cols // 2, cols - 1):
+        hop_on(step, sigma_panel, *late)
     late_in = send_over_rows([after(value, sigma_panel) for value in late])
 
-    def diagonal(a, sigma):
-        return diagonal_product(jnp.stack([order[a], me_col.astype(jnp.int32)]), rows, left, own_rows, right, sigma)
-
-    terms = [diagonal(a, after(sigma_panel, *late)) for a in range(rows - 1)]
-    terms_in = send_over_rows([after(term, *late_in) for term in terms])
-    update = sum(terms_in, diagonal(rows - 1, after(sigma_panel, *terms)))
-    sigma_diag = diag_inverse[0] - update.reshape(diag_inverse.shape[1:])
+    near = [[sorted(range(d * each, d * each + each), key=lambda block: abs(block - c)) for c in range(cols)] for d in range(rows)]
+    near = np.asarray(near, np.int32)
+    reach = np.abs(near - np.arange(cols)[None, :, None]).max(axis=(0, 1))
+    near_here = jnp.asarray(near)[:, me_col]
+    ready, terms_in, terms = after(sigma_panel, *late), [], []
+    for i in range(each):
+        pieces = (left[: reach[i]], own_rows, right[: reach[i]])
+        term = [diagonal_product(near_here[order[a]][i : i + 1], me_col, *pieces, ready) for a in range(rows - 1)]
+        terms_in.append(send_over_rows(term))
+        terms += term
+        ready = after(sigma_panel, *terms)
+    mine = me_row * each + jnp.arange(each)
+    update = list(diagonal_product(mine, me_col, left, own_rows, right, ready))
+    for block in range(each):
+        for i in range(each):
+            for value in terms_in[i]:
+                update[block] += jnp.where(near_here[me_row, i] == mine[block], value[0], 0.0)
+    sigma_diag = diag_inverse[0] - jnp.concatenate(update, axis=0)
 
     last = after(order[rows - 1 :], *terms)
     tops = [top_product(lay, table, last, *top_args, chunk)[0] for chunk in range(chunks)]

time: 401 us -> 366 us (0.913); the launches traced: 393 us -> 363 us
  waiting for transfers between devices: 223 us -> 161 us
  local copies, waits for them, and re-layouts: 15 us -> 31.6 us
  Pallas kernels: 87.4 us -> 95 us
  between operations: 15.1 us -> 21.7 us
    ppermute x4 -> x5, waiting for transfers between devices: 74.1 us -> 12.9 us  [send_over_rows(): lax.ppermute(value, 'row', [(i, (i + a + 1) % rows) for i in range(rows)])]
    ppermute x1, waiting for transfers between devices: 0.01 us -> 12.2 us  [per_device(): lax.ppermute(upper, 'row', [(r, rows - 1 - r) for r in range(rows)])]
    unnamed x33 -> x41, local copies, waits for them, and re-layouts: 7.15 us -> 19.3 us
    ppermute x3 -> x2, waiting for transfers between devices: 12.8 us -> 1.06 us  [the longest x1 1.05 us: per_device(): lax.ppermute(lower[chip * part:(chip + 2) * part], 'leaf', [(0, chip)])]
    ppermute x3, waiting for transfers between devices: 20.8 us -> 28.3 us  [hop(): lax.ppermute(value, 'col', [(i, i - 1) for i in range(1, cols - step)])]
    all_gather x1, waiting for transfers between devices: 114 us -> 107 us  [per_device(): gathered = lax.all_gather(held, ('leaf', 'col'), axis=0, tiled=False)]
    pallas_call x1, Pallas kernels: 22.6 us -> 26.6 us  [panel_product(): pl.pallas_call(functools.partial(panel_kernel, lay, rows), out_shape=[blo...]
    pallas_call x2 -> x3, Pallas kernels: 17 us -> 20.9 us  [diagonal_product(): pl.pallas_call(functools.partial(diagonal_kernel, reach), out_shape=jax.S...]
  transfers between devices with their start and end apart: 16 -> 16, of which waited for: 9 -> 7; matrix products, arithmetic and copies ran while one was open for 6% -> 11% of each run, Pallas kernels for 22% -> 26%
where the time goes in v5:
time: 366 us; the launch traced here: 363 us
  waiting for transfers between devices  161 us (44%)
  Pallas kernels  95 us (26%)
  starting transfers between devices  32.9 us (9%)
  local copies, waits for them, and re-layouts  31.6 us (9%)
  between operations  21.7 us (6%)
  other arithmetic  20.4 us (6%)
    all_gather x1, waiting for transfers between devices, per_device(): gathered = lax.all_gather(held, ('leaf', 'col'), axis=0, tiled=False)  107 us
    pallas_call x4, Pallas kernels, top_product(): pl.pallas_call(functools.partial(top_kernel, lay, chunks, chunk), out_sha...  31.2 us
    ppermute x3, waiting for transfers between devices, hop(): lax.ppermute(value, 'col', [(i, i - 1) for i in range(1, cols - step)])  28.3 us
    pallas_call x1, Pallas kernels, panel_product(): pl.pallas_call(functools.partial(panel_kernel, lay, rows), out_shape=[blo...  26.6 us
    pallas_call x3, Pallas kernels, diagonal_product(): pl.pallas_call(functools.partial(diagonal_kernel, reach), out_shape=jax.S...  20.9 us
    unnamed x41, local copies, waits for them, and re-layouts  19.3 us
    pallas_call x1, Pallas kernels, own_panel_product(): pl.pallas_call(functools.partial(own_panel_kernel, lay, rows), out_shape=...  14.2 us
    ppermute x5, waiting for transfers between devices, send_over_rows(): lax.ppermute(value, 'row', [(i, (i + a + 1) % rows) for i in range(rows)])  12.9 us
  transfers between devices with their start and end apart: 16, of which 7 were waited for; matrix products, arithmetic and copies ran while one was open for 11% of the time, Pallas kernels for 26%

profile of v5, /device:TPU:0, one launch (start us, length us, event | category | flops | bytes accessed | tf_op | source)
XLA Modules:
  0.0 362.9 jit_solution(4693338369641241623)
XLA Ops:
  7.2 1.9 slice.55
  9.1 5.8 %collective-permute-start.2 = (f32[512,256]{1,0:T(8,128)}, f32[512,256]{1,0:T(8,128)}, u32[]{:S(2)}, u32[]{:S(2)}) collective-permute-start(f32[512,256]{1,0:T(8,128)} %slice.55), channel_id=1, source_target_pairs={{0,16},{1,17},{2,18},{3,19},{4,20},{5,21},{6,22},{7,23}} | collective-permute-start | bytes 1572872 | tf_op jit(solution)/shard_map/ppermute | solution.py:376
  14.8 3.0 fusion.4
  19.4 1.6 collective-permute-start.1
  23.0 2.0 collective-permute-start.3
  27.8 12.2 %collective-permute-done = f32[1024,256]{1,0:T(8,128)S(1)} collective-permute-done((f32[1024,256]{1,0:T(8,128)}, f32[1024,256]{1,0:T(8,128)S(1)}, u32[]{:S(2)}, u32[]{:S(2)}) %collective-permute-start) | collective-permute-done | bytes 1048608 | tf_op jit(solution)/shard_map/ppermute | solution.py:371
  40.0 1.8 slice_bitcast_fusion
  45.3 1.8 dynamic-slice_bitcast_fusion.refs_2_.refs_3_
  52.5 106.9 %all-gather.3.cloned.1.call-done = f32[80,256,256]{2,1,0:T(8,128)} async-done(((f32[5,256,256]{2,1,0:T(8,128)}), f32[80,256,256]{2,1,0:T(8,128)}) %all-gather.3.cloned.1.call-update) | async-done | bytes 20971536 | tf_op jit(solution)/shard_map/all_gather | solution.py:380
  160.6 6.0 %collective-permute-start.6 = (f32[1024,512]{1,0:T(8,128)}, f32[1024,512]{1,0:T(8,128)}, u32[]{:S(2)}, u32[]{:S(2)}) collective-permute-start(f32[1024,512]{1,0:T(8,128)} %shard_map.103), channel_id=1, source_target_pairs={{0,1},{1,2},{2,3},{4,5},{5,6},{6,7},{8,9},{9,10},{10,11},{12,13},{... | collective-permute-start | bytes 6291464 | tf_op jit(solution)/shard_map/ppermute | solution.py:357
  166.6 7.1 %shard_map.104.refs_1_ = f32[4,256,256]{2,1,0:T(8,128)} custom-call(s32[2,4,4]{2,1,0:T(4,128)} %dynamic-slice_bitcast_fusion.1.tab, s32[1]{0:T(128)} %get-tuple-element.21.dests.refs_0_, s32[1]{0:T(128)} %bitcast.11.leaf_ref, f32[16,5,256,256]{3,2,1,0:T(8,128)} %bitcast.28, f32[2,1024,256]{2,1,0:T(8,128)} %pad_maximum_fusion.own_ref), custom_call_target="tpu_custom_call" | custom-call | flops 3221225472 | bytes 8388608 | tf_op jit(solution)/shard_map/pallas_call | solution.py:279
  173.8 4.1 %collective-permute-start.8 = (f32[4,256,256]{2,1,0:T(8,128)}, f32[4,256,256]{2,1,0:T(8,128)S(1)}, u32[]{:S(2)}, u32[]{:S(2)}) collective-permute-start(f32[4,256,256]{2,1,0:T(8,128)} %shard_map.104.refs_1_), channel_id=1, source_target_pairs={{0,4},{4,0},{1,5},{5,1},{2,6},{6,2},{3,7},{7,3},{8,12},{12,8},{9,1... | collective-permute-start | bytes 3145736 | tf_op jit(solution)/shard_map/ppermute | solution.py:344
  177.9 26.6 %shard_map.106 = (f32[4,256,512]{2,1,0:T(8,128)}, bf16[2,512,1024]{2,1,0:T(8,128)(2,1)}, bf16[2,512,1024]{2,1,0:T(8,128)(2,1)}) custom-call(s32[16]{0:T(128)} %bitcast.45, s32[2,4,4]{2,1,0:T(4,128)} %dynamic-slice_bitcast_fusion.1.tab, s32[2]{0:T(128)} %shard_map.105.order, f32[16,5,256,256]{3,2,1,0:T(8,128)} %bitcast.29, f32[2048,512]{1,0:T(8,128)} %bitcast.44), custom_call_target="tpu_custom_call" | custom-call | flops 19327352832 | bytes 16777216 | tf_op jit(solution)/shard_map/pallas_call | solution.py:185
  205.6 3.6 collective-permute-done.4.refs_0_
  212.5 3.1 copy.27.refs_0_
  215.6 2.0 collective-permute-start.7
  217.6 14.2 %shard_map.110.refs_1_ = f32[4,256,512]{2,1,0:T(8,128)} custom-call(s32[16]{0:T(128)} %bitcast.46, s32[2,4,4]{2,1,0:T(4,128)} %dynamic-slice_bitcast_fusion.1.tab, s32[2]{0:T(128)} %shard_map.109.order, f32[16,5,256,256]{3,2,1,0:T(8,128)} %bitcast.30, bf16[2,512,1024]{2,1,0:T(8,128)(2,1)} %get-tuple-element.7.turned_high, ...), custom_call_target="tpu_custom_call" | custom-call | flops 25769803776 | bytes 8388608 | tf_op jit(solution)/shard_map/pallas_call | solution.py:206
  232.8 4.4 %shard_map.112.refs_1_.refs_2_.refs_0_ = f32[4,256,256]{2,1,0:T(8,128)} custom-call(s32[2,4,4]{2,1,0:T(4,128)} %dynamic-slice_bitcast_fusion.1.tab, s32[1]{0:T(128)} %shard_map.111.dests, s32[1]{0:T(128)} %bitcast.11.leaf_ref, f32[16,5,256,256]{3,2,1,0:T(8,128)} %bitcast.31, f32[2,1024,256]{2,1,0:T(8,128)} %pad_maximum_fusion.own_ref), custom_call_target="tpu_custom_call" | custom-call | flops 3221225472 | bytes 8388608 | tf_op jit(solution)/shard_map/pallas_call | solution.py:279
  237.2 12.9 %collective-permute-done.9 = f32[4,256,512]{2,1,0:T(8,128)} collective-permute-done((f32[4,256,512]{2,1,0:T(8,128)}, f32[4,256,512]{2,1,0:T(8,128)}, u32[]{:S(2)}, u32[]{:S(2)}) %collective-permute-start.9) | collective-permute-done | bytes 2097184 | tf_op jit(solution)/shard_map/ppermute | solution.py:344
  250.1 3.4 add_negate_fusion
  253.5 6.8 %collective-permute-done.5.refs_1_ = f32[1024,512]{1,0:T(8,128)S(1)} collective-permute-done((f32[1024,512]{1,0:T(8,128)}, f32[1024,512]{1,0:T(8,128)S(1)}, u32[]{:S(2)}, u32[]{:S(2)}) %collective-permute-start.5) | collective-permute-done | bytes 2097184 | tf_op jit(solution)/shard_map/ppermute | solution.py:358
  263.7 3.1 copy.32.refs_0_
  266.8 2.1 collective-permute-start.11
  285.9 6.2 %shard_map.114.refs_1_ = f32[1,512,512]{2,1,0:T(8,128)} custom-call(s32[2]{0:T(128)} %pad_add_fusion.info, f32[1024,512]{1,0:T(8,128)} %copy-done.3, f32[1024,512]{1,0:T(8,128)} %copy-done.4, f32[1024,512]{1,0:T(8,128)} %copy-done.2, f32[1024,512]{1,0:T(8,128)} %collective-permute-done.6.refs_3_.refs_4_, f32[1024,512]{1,0:T(8,128)} %collective-permute-done.7.refs_4_.refs_5_, ...), custom_call_target="tpu_custom_call" | custom-call | flops 1610612736 | bytes 4194304 | tf_op jit(solution)/shard_map/pallas_call | solution.py:320
  292.8 17.9 %collective-permute-done.10.refs_2_ = f32[1024,512]{1,0:T(8,128)} collective-permute-done((f32[1024,512]{1,0:T(8,128)}, f32[1024,512]{1,0:T(8,128)}, u32[]{:S(2)}, u32[]{:S(2)}) %collective-permute-start.10) | collective-permute-done | bytes 2097184 | tf_op jit(solution)/shard_map/ppermute | solution.py:358
  310.7 6.2 %shard_map.118.refs_2_ = f32[1,512,512]{2,1,0:T(8,128)} custom-call(s32[2]{0:T(128)} %pad_add_fusion.1.info, f32[1024,512]{1,0:T(8,128)} %copy-done.3, f32[1024,512]{1,0:T(8,128)} %copy-done.4, f32[1024,512]{1,0:T(8,128)} %collective-permute-done.10.refs_2_, f32[1024,512]{1,0:T(8,128)} %copy-done.2, f32[1024,512]{1,0:T(8,128)} %collective-permute-done.6.refs_3_.refs_4_, ...), custom_call_target="tpu_custom_call" | custom-call | flops 1610612736 | bytes 4194304 | tf_op jit(solution)/shard_map/pallas_call | solution.py:320
  316.9 1.6 collective-permute-start.14
  319.5 10.0 %shard_map.120 = f32[4,256,256]{2,1,0:T(8,128)} custom-call(s32[2,4,4]{2,1,0:T(4,128)} %dynamic-slice_bitcast_fusion.1.tab, s32[1]{0:T(128)} %shard_map.119.dests, s32[1]{0:T(128)} %bitcast.11.leaf_ref, f32[16,5,256,256]{3,2,1,0:T(8,128)} %bitcast.32, f32[2,1024,256]{2,1,0:T(8,128)} %pad_maximum_fusion.own_ref), custom_call_target="tpu_custom_call" | custom-call | flops 3221225472 | bytes 8388608 | tf_op jit(solution)/shard_map/pallas_call | solution.py:279
  330.9 9.7 %shard_map.121 = f32[4,256,256]{2,1,0:T(8,128)} custom-call(s32[2,4,4]{2,1,0:T(4,128)} %dynamic-slice_bitcast_fusion.1.tab, s32[1]{0:T(128)} %shard_map.119.dests, s32[1]{0:T(128)} %bitcast.11.leaf_ref, f32[16,5,256,256]{3,2,1,0:T(8,128)} %bitcast.33, f32[2,1024,256]{2,1,0:T(8,128)} %pad_maximum_fusion.own_ref), custom_call_target="tpu_custom_call" | custom-call | flops 3221225472 | bytes 8388608 | tf_op jit(solution)/shard_map/pallas_call | solution.py:279
  343.5 8.6 %shard_map.124 = f32[2,512,512]{2,1,0:T(8,128)} custom-call(s32[3]{0:T(128)} %pad_add_fusion.2.info, f32[1024,512]{1,0:T(8,128)} %copy-done.3, f32[1024,512]{1,0:T(8,128)} %copy-done.4, f32[1024,512]{1,0:T(8,128)} %collective-permute-done.10.refs_2_, f32[1024,512]{1,0:T(8,128)} %copy-done.2, f32[1024,512]{1,0:T(8,128)} %collective-permute-done.6.refs_3_.refs_4_, ...), custom_call_target="tpu_custom_call" | custom-call | flops 3221225472 | bytes 6291456 | tf_op jit(solution)/shard_map/pallas_call | solution.py:320
  352.1 2.2 fusion.1
  354.3 1.8 maximum_subtract_fusion
  (92 shorter events, 41.0 us)
Async XLA Ops:
  7.2 152.2 %all-gather.3.cloned.1.call-start = ((), (), s32[]{:S(2)}) async-start(), calls=%async_computation | async-start | bytes 22282240 | tf_op jit(solution)/shard_map/all_gather | solution.py:380
  9.1 13.0 %copy-start.6 = (f32[2048,256]{1,0:T(8,128)S(1)}, f32[2048,256]{1,0:T(8,128)}, u32[]{:S(2)}) copy-start(f32[2048,256]{1,0:T(8,128)} %param.8) | copy-start | bytes 6291460
  9.1 13.0 %collective-permute-start.2 = (f32[512,256]{1,0:T(8,128)}, f32[512,256]{1,0:T(8,128)}, u32[]{:S(2)}, u32[]{:S(2)}) collective-permute-start(f32[512,256]{1,0:T(8,128)} %slice.55), channel_id=1, source_target_pairs={{0,16},{1,17},{2,18},{3,19},{4,20},{5,21},{6,22},{7,23}} | collective-permute-start | bytes 1572872 | tf_op jit(solution)/shard_map/ppermute | solution.py:376
  17.8 7.1 %copy-start.15 = (s32[2]{0:T(128)S(1)}, s32[2]{0:T(128)}, u32[]{:S(2)}) copy-start(s32[2]{0:T(128)} %constant.106.clone) | copy-start | bytes 28
  17.8 8.3 %copy-start.14 = (pred[2,4]{1,0:T(4,128)(4,1)S(1)}, pred[2,4]{1,0:T(4,128)(4,1)}, u32[]{:S(2)}) copy-start(pred[2,4]{1,0:T(4,128)(4,1)} %constant.107.clone) | copy-start | bytes 28
  17.8 22.2 %collective-permute-start = (f32[1024,256]{1,0:T(8,128)}, f32[1024,256]{1,0:T(8,128)S(1)}, u32[]{:S(2)}, u32[]{:S(2)}) collective-permute-start(f32[1024,256]{1,0:T(8,128)} %get-tuple-element.14), channel_id=1, source_target_pairs={{0,4},{4,0},{1,5},{5,1},{2,6},{6,2},{3,7},{7,3},{8,12},{12,8},{9,1... | collective-permute-start | bytes 3145736 | tf_op jit(solution)/shard_map/ppermute | solution.py:371
  19.4 20.6 %collective-permute-start.1 = (f32[1024,256]{1,0:T(8,128)}, f32[1024,256]{1,0:T(8,128)}, u32[]{:S(2)}, u32[]{:S(2)}) collective-permute-start(f32[1024,256]{1,0:T(8,128)} %get-tuple-element.13), channel_id=1, source_target_pairs={{8,24},{9,25},{10,26},{11,27}} | collective-permute-start | bytes 3145736 | tf_op jit(solution)/shard_map/ppermute | solution.py:372
  22.1 0.8 copy-start.11
  23.0 3.9 %collective-permute-start.3 = (f32[256,256]{1,0:T(8,128)S(1)}, f32[256,256]{1,0:T(8,128)}, u32[]{:S(2)}, u32[]{:S(2)}) collective-permute-start(f32[256,256]{1,0:T(8,128)S(1)} %slice.64), channel_id=1, source_target_pairs={{0,8},{16,24},{1,9},{17,25},{2,10},{18,26},{3,11},{19,27},{4,12},{... | collective-permute-start | bytes 786440 | tf_op jit(solution)/shard_map/ppermute | solution.py:377
  43.0 4.1 %copy-start.12 = (s32[2]{0:T(128)}, s32[2]{0:T(128)S(1)}, u32[]{:S(2)}) copy-start(s32[2]{0:T(128)S(1)} %and_select_fusion.refs_0_) | copy-start | bytes 28
  47.1 1.4 copy-start.2
  48.5 1.9 copy-start.13
  48.5 2.5 copy-start.9
  159.3 49.9 %collective-permute-start.4 = (f32[1024,512]{1,0:T(8,128)}, f32[1024,512]{1,0:T(8,128)S(1)}, u32[]{:S(2)}, u32[]{:S(2)}) collective-permute-start(f32[1024,512]{1,0:T(8,128)} %shard_map.103), channel_id=1, source_target_pairs={{1,0},{2,1},{3,2},{5,4},{6,5},{7,6},{9,8},{10,9},{11,10},{13,12},{... | collective-permute-start | bytes 6291464 | tf_op jit(solution)/shard_map/ppermute | solution.py:358
  160.6 51.9 %collective-permute-start.6 = (f32[1024,512]{1,0:T(8,128)}, f32[1024,512]{1,0:T(8,128)}, u32[]{:S(2)}, u32[]{:S(2)}) collective-permute-start(f32[1024,512]{1,0:T(8,128)} %shard_map.103), channel_id=1, source_target_pairs={{0,1},{1,2},{2,3},{4,5},{5,6},{6,7},{8,9},{9,10},{10,11},{12,13},{... | collective-permute-start | bytes 6291464 | tf_op jit(solution)/shard_map/ppermute | solution.py:357
  173.8 30.9 %collective-permute-start.8 = (f32[4,256,256]{2,1,0:T(8,128)}, f32[4,256,256]{2,1,0:T(8,128)S(1)}, u32[]{:S(2)}, u32[]{:S(2)}) collective-permute-start(f32[4,256,256]{2,1,0:T(8,128)} %shard_map.104.refs_1_), channel_id=1, source_target_pairs={{0,4},{4,0},{1,5},{5,1},{2,6},{6,2},{3,7},{7,3},{8,12},{12,8},{9,1... | collective-permute-start | bytes 3145736 | tf_op jit(solution)/shard_map/ppermute | solution.py:344
  204.4 45.7 %collective-permute-start.9 = (f32[4,256,512]{2,1,0:T(8,128)}, f32[4,256,512]{2,1,0:T(8,128)}, u32[]{:S(2)}, u32[]{:S(2)}) collective-permute-start(f32[4,256,512]{2,1,0:T(8,128)} %get-tuple-element.6.refs_1_), channel_id=1, source_target_pairs={{0,4},{4,0},{1,5},{5,1},{2,6},{6,2},{3,7},{7,3},{8,12},{12,8},{9,1... | collective-permute-start | bytes 6291464 | tf_op jit(solution)/shard_map/ppermute | solution.py:344
  204.6 1.0 copy-start.7
  209.2 2.0 copy-start.3
  211.2 49.1 %collective-permute-start.5 = (f32[1024,512]{1,0:T(8,128)}, f32[1024,512]{1,0:T(8,128)S(1)}, u32[]{:S(2)}, u32[]{:S(2)}) collective-permute-start(f32[1024,512]{1,0:T(8,128)} %shard_map.107), channel_id=1, source_target_pairs={{1,0},{2,1},{5,4},{6,5},{9,8},{10,9},{13,12},{14,13},{17,16},{18,1... | collective-permute-start | bytes 6291464 | tf_op jit(solution)/shard_map/ppermute | solution.py:358
  215.6 48.1 %collective-permute-start.7 = (f32[1024,512]{1,0:T(8,128)}, f32[1024,512]{1,0:T(8,128)}, u32[]{:S(2)}, u32[]{:S(2)}) collective-permute-start(f32[1024,512]{1,0:T(8,128)} %shard_map.108), channel_id=1, source_target_pairs={{1,2},{2,3},{5,6},{6,7},{9,10},{10,11},{13,14},{14,15},{17,18},{18... | collective-permute-start | bytes 6291464 | tf_op jit(solution)/shard_map/ppermute | solution.py:357
  232.8 17.3 %copy-start.5 = (f32[4,256,512]{2,1,0:T(8,128)S(1)}, f32[4,256,512]{2,1,0:T(8,128)}, u32[]{:S(2)}) copy-start(f32[4,256,512]{2,1,0:T(8,128)} %shard_map.110.refs_1_) | copy-start | bytes 6291460
  260.4 2.0 copy-start.4
  262.4 48.3 %collective-permute-start.10 = (f32[1024,512]{1,0:T(8,128)}, f32[1024,512]{1,0:T(8,128)}, u32[]{:S(2)}, u32[]{:S(2)}) collective-permute-start(f32[1024,512]{1,0:T(8,128)} %shard_map.115), channel_id=1, source_target_pairs={{1,0},{5,4},{9,8},{13,12},{17,16},{21,20},{25,24},{29,28}} | collective-permute-start | bytes 6291464 | tf_op jit(solution)/shard_map/ppermute | solution.py:358
  266.8 4.7 %copy-start = (f32[4,256,512]{2,1,0:T(8,128)S(1)}, f32[4,256,512]{2,1,0:T(8,128)}, u32[]{:S(2)}) copy-start(f32[4,256,512]{2,1,0:T(8,128)} %add_negate_fusion) | copy-start | bytes 6291460
  266.8 43.9 %collective-permute-start.11 = (f32[1024,512]{1,0:T(8,128)}, f32[1024,512]{1,0:T(8,128)}, u32[]{:S(2)}, u32[]{:S(2)}) collective-permute-start(f32[1024,512]{1,0:T(8,128)} %shard_map.116), channel_id=1, source_target_pairs={{2,3},{6,7},{10,11},{14,15},{18,19},{22,23},{26,27},{30,31}} | collective-permute-start | bytes 6291464 | tf_op jit(solution)/shard_map/ppermute | solution.py:357
  272.8 10.4 %copy-start.1 = (f32[4,256,512]{2,1,0:T(8,128)S(1)}, f32[4,256,512]{2,1,0:T(8,128)}, u32[]{:S(2)}) copy-start(f32[4,256,512]{2,1,0:T(8,128)} %add_negate_fusion) | copy-start | bytes 6291460
  272.8 67.7 %collective-permute-start.12 = (f32[4,256,256]{2,1,0:T(8,128)}, f32[4,256,256]{2,1,0:T(8,128)S(1)}, u32[]{:S(2)}, u32[]{:S(2)}) collective-permute-start(f32[4,256,256]{2,1,0:T(8,128)} %shard_map.122), channel_id=1, source_target_pairs={{0,4},{4,0},{1,5},{5,1},{2,6},{6,2},{3,7},{7,3},{8,12},{12,8},{9,1... | collective-permute-start | bytes 3145736 | tf_op jit(solution)/shard_map/ppermute | solution.py:344
  292.1 60.0 %collective-permute-start.13 = (f32[1,512,512]{2,1,0:T(8,128)}, f32[1,512,512]{2,1,0:T(8,128)S(1)}, u32[]{:S(2)}, u32[]{:S(2)}) collective-permute-start(f32[1,512,512]{2,1,0:T(8,128)} %shard_map.114.refs_1_), channel_id=1, source_target_pairs={{0,4},{4,0},{1,5},{5,1},{2,6},{6,2},{3,7},{7,3},{8,12},{12,8},{9,1... | collective-permute-start | bytes 3145736 | tf_op jit(solution)/shard_map/ppermute | solution.py:344
  316.9 35.2 %collective-permute-start.14 = (f32[1,512,512]{2,1,0:T(8,128)}, f32[1,512,512]{2,1,0:T(8,128)S(1)}, u32[]{:S(2)}, u32[]{:S(2)}) collective-permute-start(f32[1,512,512]{2,1,0:T(8,128)} %shard_map.118.refs_2_), channel_id=1, source_target_pairs={{0,4},{4,0},{1,5},{5,1},{2,6},{6,2},{3,7},{7,3},{8,12},{12,8},{9,1... | collective-permute-start | bytes 3145736 | tf_op jit(solution)/shard_map/ppermute | solution.py:344
  319.5 10.0 %copy-start.8 = (f32[4,256,256]{2,1,0:T(8,128)S(1)}, f32[4,256,256]{2,1,0:T(8,128)}, u32[]{:S(2)}) copy-start(f32[4,256,256]{2,1,0:T(8,128)} %copy-done.7) | copy-start | bytes 3145732
  352.0 2.2 copy-start.10
Sparse Core Ops, SparseCore 0:
  43.1 116.1 all-gather.2

commit v6 on v5

--- a/solution.py
+++ b/solution.py
@@ -99,9 +99,9 @@
     return dot(turned_high[s], high) + dot(turned_low[s], high) + dot(turned_high[s], low)
 
 
-def panel_kernel(lay, rows, pat, tab, order, gathered, p_ref, *refs):
-    outs = refs[: rows - 1]
-    turned_high, turned_low, t, th, tl, image, sems = refs[rows - 1 :]
+def panel_kernel(lay, rows, tokens, pat, tab, order, gathered, p_ref, *refs):
+    outs = refs[tokens : tokens + rows - 1]
+    turned_high, turned_low, t, th, tl, image, sems = refs[tokens + rows - 1 :]
     number = t.shape[0]
     each = number // 2 // rows
 
@@ -145,7 +145,8 @@
                     out[...] += back_product(turned_high, turned_low, th[kp, s], tl[kp, s], s).T
 
 
-def own_panel_kernel(lay, rows, pat, tab, order, gathered, turned_high, turned_low, out_ref, t, sems):
+def own_panel_kernel(lay, rows, tokens, pat, tab, order, gathered, turned_high, turned_low, *refs):
+    out_ref, t, sems = refs[tokens:]
     each = t.shape[0] // 2 // rows
     first = order[rows - 1] * each
 
@@ -176,16 +177,16 @@
     return pl.CostEstimate(flops=flops, bytes_accessed=4 * values, transcendentals=0)
 
 
-def panel_product(lay, pattern, table, order, gathered, normed):
+def panel_product(lay, pattern, table, order, gathered, normed, tokens):
     number, wide, rows = pattern.shape[0], normed.shape[1], order.shape[0]
     half = lay.half
     pairs = number // 2
     block = jax.ShapeDtypeStruct((pairs // rows, 2 * BLK, wide), jnp.float32)
     turned = jax.ShapeDtypeStruct((2, wide, half), jnp.bfloat16)
     result = pl.pallas_call(
-        functools.partial(panel_kernel, lay, rows),
+        functools.partial(panel_kernel, lay, rows, len(tokens)),
         out_shape=[block] * (rows - 1) + [turned] * 2,
-        in_specs=[SMEM] * 3 + [ANY, VMEM],
+        in_specs=[SMEM] * 3 + [ANY, VMEM] + [ANY] * len(tokens),
         out_specs=[VMEM] * (rows + 1),
         scratch_shapes=[
             pltpu.VMEM((number, 2, half, BLK), jnp.float32),
@@ -196,17 +197,17 @@
         ],
         compiler_params=pltpu.CompilerParams(vmem_limit_bytes=VMEM_BYTES),
         cost_estimate=estimate(18 * half * number * BLK * wide, 2 * half * number * BLK),
-    )(pattern, table, order, gathered, normed)
+    )(pattern, table, order, gathered, normed, *tokens)
     return result[: rows - 1], result[rows - 1 :]
 
 
-def own_panel_product(lay, pattern, table, order, gathered, turned):
+def own_panel_product(lay, pattern, table, order, gathered, turned, tokens):
     number, wide, rows = pattern.shape[0], turned[0].shape[1], order.shape[0]
     half = lay.half
     return pl.pallas_call(
-        functools.partial(own_panel_kernel, lay, rows),
+        functools.partial(own_panel_kernel, lay, rows, len(tokens)),
         out_shape=jax.ShapeDtypeStruct((number // 2 // rows, 2 * BLK, wide), jnp.float32),
-        in_specs=[SMEM] * 3 + [ANY, VMEM, VMEM],
+        in_specs=[SMEM] * 3 + [ANY, VMEM, VMEM] + [ANY] * len(tokens),
         out_specs=VMEM,
         scratch_shapes=[
             pltpu.VMEM((number, 2, half, BLK), jnp.float32),
@@ -214,12 +215,12 @@
         ],
         compiler_params=pltpu.CompilerParams(vmem_limit_bytes=VMEM_BYTES),
         cost_estimate=estimate(24 * half * number * BLK * wide, half * number * BLK),
-    )(pattern, table, order, gathered, *turned)
-
-
-def top_kernel(lay, chunks, chunk, tab, dests, leaf_ref, g_ref, own_ref, *refs):
+    )(pattern, table, order, gathered, *turned, *tokens)
+
+
+def top_kernel(lay, chunks, chunk, tokens, tab, dests, leaf_ref, g_ref, own_ref, *refs):
     count = dests.shape[0]
-    outs, (own_turned, held, sems) = refs[:count], refs[count:]
+    outs, (own_turned, held, sems) = refs[tokens : tokens + count], refs[tokens + count :]
     parts, part = lay.leaves, lay.part
     each = outs[0].shape[0]
 
@@ -272,14 +273,14 @@
                     out[...] += total.T
 
 
-def top_product(lay, table, dests, me_leaf, gathered, own, chunks, chunk):
+def top_product(lay, table, dests, me_leaf, gathered, own, chunks, chunk, tokens=()):
     count, width, half = dests.shape[0], lay.width, lay.half
     each = gathered.shape[0] // lay.rows // chunks
     block = jax.ShapeDtypeStruct((each, width, width), jnp.float32)
     return pl.pallas_call(
-        functools.partial(top_kernel, lay, chunks, chunk),
+        functools.partial(top_kernel, lay, chunks, chunk, len(tokens)),
         out_shape=[block] * count,
-        in_specs=[SMEM] * 3 + [ANY, VMEM],
+        in_specs=[SMEM] * 3 + [ANY, VMEM] + [ANY] * len(tokens),
         out_specs=[VMEM] * count,
         scratch_shapes=[
             pltpu.VMEM((2, 2, width, half), jnp.bfloat16),
@@ -288,23 +289,21 @@
         ],
         compiler_params=pltpu.CompilerParams(vmem_limit_bytes=VMEM_BYTES),
         cost_estimate=estimate(12 * half * count * each * width * width, 2 * half * count * each * width),
-    )(table, dests, me_leaf, gathered, own)
-
-
-def diagonal_kernel(reach, info, *refs):
-    lefts, own, rights = refs[:reach], refs[reach], refs[reach + 1 : 2 * reach + 1]
-    sigma, out_ref, held, sems = refs[2 * reach + 1 :]
+    )(table, dests, me_leaf, gathered, own, *tokens)
+
+
+def diagonal_kernel(steps, tokens, info, *refs):
+    sources, refs = list(zip(steps, refs)), refs[len(steps) :]
+    sigma, (out_ref, held, sems) = refs[0], refs[1 + tokens :]
     each = out_ref.shape[0]
-    sources = {0: own}
-    for t in range(1, reach + 1):
-        sources[t], sources[-t] = lefts[t - 1], rights[t - 1]
     for i in range(each):
         away = info[i] - info[each]
-        for step, source in sources.items():
+        for (step, run), source in sources:
 
             @pl.when(away == step)
             def _():
-                pltpu.make_async_copy(source, held.at[i], sems.at[i]).start()
+                rows = pl.ds(run * source.shape[0], source.shape[0])
+                pltpu.make_async_copy(source, held.at[i, rows], sems.at[i]).start()
 
     turned_high, turned_low = halves(sigma[...].T)
     for i in range(each):
@@ -314,18 +313,18 @@
         out_ref[i] = total.T
 
 
-def diagonal_product(blocks, me_col, lefts, own, rights, sigma):
-    each, reach = blocks.shape[0], len(lefts)
+def diagonal_product(blocks, me_col, pieces, sigma, tokens):
+    each = blocks.shape[0]
     depth, wide = sigma.shape
     return pl.pallas_call(
-        functools.partial(diagonal_kernel, reach),
+        functools.partial(diagonal_kernel, tuple(pieces), len(tokens)),
         out_shape=jax.ShapeDtypeStruct((each, wide, wide), jnp.float32),
-        in_specs=[SMEM] + [ANY] * (2 * reach + 1) + [VMEM],
+        in_specs=[SMEM] + [ANY] * len(pieces) + [VMEM] + [ANY] * len(tokens),
         out_specs=VMEM,
         scratch_shapes=[pltpu.VMEM((each, depth, wide), jnp.float32), pltpu.SemaphoreType.DMA((each,))],
         compiler_params=pltpu.CompilerParams(vmem_limit_bytes=VMEM_BYTES),
         cost_estimate=estimate(6 * each * depth * wide * wide, (each + 1) * depth * wide),
-    )(jnp.append(blocks, me_col).astype(jnp.int32), *lefts, own, *rights, sigma)
+    )(jnp.append(blocks, me_col).astype(jnp.int32), *pieces.values(), sigma, *tokens)
 
 
 def after(value, *earlier):
@@ -350,12 +349,21 @@
     half, width, parts, part = lay.half, lay.width, lay.leaves, lay.part
     normed = panel[0]
 
-    own_rows = lax.dynamic_slice_in_dim(normed, me_row * (normed.shape[0] // rows), normed.shape[0] // rows, 0)
-
-    def hop(value, step, way):
-        if way > 0:
-            return lax.ppermute(value, "col", [(i, i + 1) for i in range(step, cols - 1)])
-        return lax.ppermute(value, "col", [(i, i - 1) for i in range(1, cols - step)])
+    count = normed.shape[0] // rows
+    own_rows = lax.dynamic_slice_in_dim(normed, me_row * count, count, 0)
+    runs = 2
+    pieces = {(0, run): own_rows[run * count // runs : (run + 1) * count // runs] for run in range(runs)}
+
+    def hop(run, step, *earlier):
+        if earlier:
+            for key in sorted({(step, run), (-step, run)}):
+                pieces[key] = after(pieces[key], *earlier)
+        for way in (1, -1):
+            at = [i for i in range(cols) if 0 <= i - way * step < cols and 0 <= i + way < cols]
+            moved_on = lax.ppermute(pieces[-way * step, run], "col", [(i, i + way) for i in at])
+            pieces[-way * (step + 1), run] = moved_on
+
+    hop(0, 0)
 
     table = jnp.asarray(lay.table)[me_row]
     second = jnp.asarray([count[1] for count in lay.counts], jnp.int32)[me_row]
@@ -377,15 +385,10 @@
     other = lax.ppermute(both[part:], "leaf", [(chip, chip + 1) for chip in range(0, leaves, 2)])
     extra = jnp.where(me_leaf % 2 == 0, both[:part], other)
     held = jnp.concatenate([whole.reshape(parts, part, width), extra[None]], axis=0)
-    gathered = lax.all_gather(held, ("leaf", "col"), axis=0, tiled=False)
+    gathered = lax.all_gather(after(held, pieces[1, 0], pieces[-1, 0]), ("leaf", "col"), axis=0, tiled=False)
     own = jnp.stack([lower, swapped])
-
-    start = after(own_rows, gathered)
-    right, left = [hop(start, 0, 1)], [hop(start, 0, -1)]
-
-    def hop_on(step, *earlier):
-        right.append(hop(after(right[-1], *earlier), step, 1))
-        left.append(hop(after(left[-1], *earlier), step, -1))
+    hop(1, 0, gathered)
+    hop(0, 1, gathered)
 
     chunks, each = 2, cols // rows
     order = ((me_row + 1 + jnp.arange(rows)) % rows).astype(jnp.int32)
@@ -393,40 +396,50 @@
     top_args = (leaf_here, gathered, own, chunks)
     early = top_product(lay, table, order[: rows - 1], *top_args, 0)
     early_in = send_over_rows(early)
-    sent, turned = panel_product(lay, pattern[0], table, after(order, *early), gathered, normed)
+    sent, turned = panel_product(lay, pattern[0], table, order, gathered, normed, early)
+    if cols > 2:
+        sent = [after(value, pieces[2, 0], pieces[-2, 0]) for value in sent]
     sent_in = send_over_rows(sent)
-    for step in range(1, cols // 2):
-        hop_on(step, *sent)
-    kept = own_panel_product(lay, pattern[0], table, after(order, *early_in), gathered, turned)
+    middle = cols // 2
+    for step in range(1, middle):
+        hop(1, step, *sent)
+        if step + 1 < cols - 1:
+            hop(0, step + 1, *sent)
+    kept = own_panel_product(lay, pattern[0], table, order, gathered, turned, early_in)
+    late = top_product(lay, table, order[: rows - 1], *top_args, 1, [kept])
     sigma_panel = -sum(sent_in, kept).reshape(-1, normed.shape[1])
-    late = top_product(lay, table, after(order[: rows - 1], kept), *top_args, 1)
-    for step in range(cols // 2, cols - 1):
-        hop_on(step, sigma_panel, *late)
-    late_in = send_over_rows([after(value, sigma_panel) for value in late])
+    late = [after(value, sigma_panel) for value in late]
+    late_in = send_over_rows(late)
+    for step in range(middle, cols - 1):
+        hop(1, step, sigma_panel)
+        if step + 1 < cols - 1:
+            hop(0, step + 1, sigma_panel)
 
     near = [[sorted(range(d * each, d * each + each), key=lambda block: abs(block - c)) for c in range(cols)] for d in range(rows)]
     near = np.asarray(near, np.int32)
     reach = np.abs(near - np.arange(cols)[None, :, None]).max(axis=(0, 1))
     near_here = jnp.asarray(near)[:, me_col]
-    ready, terms_in, terms = after(sigma_panel, *late), [], []
+    terms_in, tokens = [], late
     for i in range(each):
-        pieces = (left[: reach[i]], own_rows, right[: reach[i]])
-        term = [diagonal_product(near_here[order[a]][i : i + 1], me_col, *pieces, ready) for a in range(rows - 1)]
+        there = {key: piece for key, piece in pieces.items() if abs(key[0]) <= reach[i]}
+        term = [
+            diagonal_product(near_here[order[a]][i : i + 1], me_col, there, sigma_panel, tokens)
+            for a in range(rows - 1)
+        ]
         terms_in.append(send_over_rows(term))
-        terms += term
-        ready = after(sigma_panel, *terms)
+        if i == 0:
+            tops = list(top_product(lay, table, order[rows - 1 :], *top_args, 1, term))
+        tokens = tops + late_in
+    tops = list(top_product(lay, table, order[rows - 1 :], *top_args, 0, term)) + tops
     mine = me_row * each + jnp.arange(each)
-    update = list(diagonal_product(mine, me_col, left, own_rows, right, ready))
+    update = list(diagonal_product(mine, me_col, pieces, sigma_panel, term))
     for block in range(each):
         for i in range(each):
             for value in terms_in[i]:
                 update[block] += jnp.where(near_here[me_row, i] == mine[block], value[0], 0.0)
     sigma_diag = diag_inverse[0] - jnp.concatenate(update, axis=0)
 
-    last = after(order[rows - 1 :], *terms)
-    tops = [top_product(lay, table, last, *top_args, chunk)[0] for chunk in range(chunks)]
-    tops = [sum(early_in, tops[0]), sum(late_in, tops[1])]
-    sigma_top = jnp.concatenate(tops, axis=0).reshape(-1, width)
+    sigma_top = jnp.concatenate([sum(early_in, tops[0]), sum(late_in, tops[1])], axis=0).reshape(-1, width)
     return (sigma_top, sigma_panel[None], sigma_diag[None])
 
 

time: 366 us -> 357 us (0.975)
  local copies, waits for them, and re-layouts: 31.6 us -> 20.3 us
  starting transfers between devices: 32.9 us -> 40.4 us
  Pallas kernels: 95 us -> 88.8 us
  other arithmetic: 20.4 us -> 24.7 us
    ppermute x5, waiting for transfers between devices: 12.9 us -> 26.2 us  [send_over_rows(): lax.ppermute(value, 'row', [(i, (i + a + 1) % rows) for i in range(rows)])]
    unnamed x41 -> x36, local copies, waits for them, and re-layouts: 19.3 us -> 7.09 us
    ppermute x6 -> x12, waiting for transfers between devices: 28.3 us -> 19.2 us  [hop(): lax.ppermute(pieces[-way * step, run], 'col', [(i, i + way) for i in at])]
    ppermute x1, waiting for transfers between devices: 12.2 us -> 3.58 us  [per_device(): lax.ppermute(upper, 'row', [(r, rows - 1 - r) for r in range(rows)])]
    ppermute x6 -> x12, starting transfers between devices: 13.9 us -> 20.8 us  [hop(): lax.ppermute(pieces[-way * step, run], 'col', [(i, i + way) for i in at])]
    pallas_call x9, Pallas kernels: 92.8 us -> 88.7 us  [the longest x4 31.3 us: top_product(): pl.pallas_call(functools.partial(top_kernel, lay, chunks, chunk, len(toke...]
    all_gather x1, waiting for transfers between devices: 107 us -> 111 us  [per_device(): lax.all_gather(after(held, pieces[1, 0], pieces[-1, 0]), ('leaf', 'col'),...]
  transfers between devices with their start and end apart: 16 -> 22, of which waited for: 7 -> 8; matrix products, arithmetic and copies ran while one was open for 11% -> 9% of each run, Pallas kernels for 26% -> 25%
where the time goes in v6:
time: 357 us; the launch traced here: 356 us
  waiting for transfers between devices  160 us (45%)
  Pallas kernels  88.8 us (25%)
  starting transfers between devices  40.4 us (11%)
  other arithmetic  24.7 us (7%)
  between operations  21.6 us (6%)
  local copies, waits for them, and re-layouts  20.3 us (6%)
    all_gather x1, waiting for transfers between devices, per_device(): lax.all_gather(after(held, pieces[1, 0], pieces[-1, 0]), ('leaf', 'col'),...  111 us
    pallas_call x4, Pallas kernels, top_product(): pl.pallas_call(functools.partial(top_kernel, lay, chunks, chunk, len(toke...  31.3 us
    ppermute x5, waiting for transfers between devices, send_over_rows(): lax.ppermute(value, 'row', [(i, (i + a + 1) % rows) for i in range(rows)])  26.2 us
    pallas_call x1, Pallas kernels, panel_product(): pl.pallas_call(functools.partial(panel_kernel, lay, rows, len(tokens)), o...  22.5 us
    ppermute x12, starting transfers between devices, hop(): lax.ppermute(pieces[-way * step, run], 'col', [(i, i + way) for i in at])  20.8 us
    pallas_call x3, Pallas kernels, diagonal_product(): pl.pallas_call(functools.partial(diagonal_kernel, tuple(pieces), len(toke...  20.7 us
    ppermute x12, waiting for transfers between devices, hop(): lax.ppermute(pieces[-way * step, run], 'col', [(i, i + way) for i in at])  19.2 us
    pallas_call x1, Pallas kernels, own_panel_product(): pl.pallas_call(functools.partial(own_panel_kernel, lay, rows, len(tokens)...  14.2 us
  transfers between devices with their start and end apart: 22, of which 8 were waited for; matrix products, arithmetic and copies ran while one was open for 9% of the time, Pallas kernels for 25%

profile of v6, /device:TPU:0, one launch (start us, length us, event | category | flops | bytes accessed | tf_op | source)
XLA Modules:
  0.0 355.8 jit_solution(4439494312404471607)
XLA Ops:
  7.2 1.9 slice.65
  9.1 5.6 %collective-permute-start.2 = (f32[512,256]{1,0:T(8,128)}, f32[512,256]{1,0:T(8,128)}, u32[]{:S(2)}, u32[]{:S(2)}) collective-permute-start(f32[512,256]{1,0:T(8,128)} %slice.65), channel_id=1, source_target_pairs={{0,16},{1,17},{2,18},{3,19},{4,20},{5,21},{6,22},{7,23}} | collective-permute-start | bytes 1572872 | tf_op jit(solution)/shard_map/ppermute | solution.py:384
  14.7 3.0 fusion.4
  19.2 1.7 collective-permute-start.1
  20.9 2.7 dynamic-slice_bitcast_fusion
  25.1 4.6 %collective-permute-start.5 = (f32[512,512]{1,0:T(8,128)S(1)}, f32[512,512]{1,0:T(8,128)S(1)}, u32[]{:S(2)}, u32[]{:S(2)}) collective-permute-start(f32[512,512]{1,0:T(8,128)S(1)} %get-tuple-element.12.refs_0_), channel_id=1, source_target_pairs={{0,1},{1,2},{2,3},{4,5},{5,6},{6,7},{8,9},{9,10},{10,11},{12,13},{... | collective-permute-start | bytes 3145736 | tf_op jit(solution)/shard_map/ppermute | solution.py:363
  31.6 2.0 collective-permute-start.3
  36.4 3.6 %collective-permute-done = f32[1024,256]{1,0:T(8,128)} collective-permute-done((f32[1024,256]{1,0:T(8,128)}, f32[1024,256]{1,0:T(8,128)}, u32[]{:S(2)}, u32[]{:S(2)}) %collective-permute-start) | collective-permute-done | bytes 1048608 | tf_op jit(solution)/shard_map/ppermute | solution.py:379
  40.0 3.3 slice_bitcast_fusion
  44.4 5.6 %collective-permute-done.4.refs_1_.refs_0_ = f32[512,512]{1,0:T(8,128)S(1)} collective-permute-done((f32[512,512]{1,0:T(8,128)S(1)}, f32[512,512]{1,0:T(8,128)S(1)}, u32[]{:S(2)}, u32[]{:S(2)}) %collective-permute-start.4) | collective-permute-done | bytes 1048608 | tf_op jit(solution)/shard_map/ppermute | solution.py:363
  53.5 3.0 pad_maximum_fusion.own_ref
  56.5 111.0 %all-gather.3.cloned.1.call-done = f32[80,256,256]{2,1,0:T(8,128)} async-done(((f32[5,256,256]{2,1,0:T(8,128)}), f32[80,256,256]{2,1,0:T(8,128)}) %all-gather.3.cloned.1.call-update) | async-done | bytes 20971536 | tf_op jit(solution)/shard_map/all_gather | solution.py:388
  167.4 4.4 %collective-permute-start.6 = (f32[512,512]{1,0:T(8,128)}, f32[512,512]{1,0:T(8,128)}, u32[]{:S(2)}, u32[]{:S(2)}) collective-permute-start(f32[512,512]{1,0:T(8,128)} %shard_map.104.refs_1_), channel_id=1, source_target_pairs={{0,1},{1,2},{2,3},{4,5},{5,6},{6,7},{8,9},{9,10},{10,11},{12,13},{... | collective-permute-start | bytes 3145736 | tf_op jit(solution)/shard_map/ppermute | solution.py:363
  175.1 7.2 %shard_map.107.refs_0_ = f32[4,256,256]{2,1,0:T(8,128)} custom-call(s32[2,4,4]{2,1,0:T(4,128)} %dynamic-slice_bitcast_fusion.2.tab, s32[1]{0:T(128)} %get-tuple-element.23.dests, s32[1]{0:T(128)} %bitcast.1.leaf_ref, f32[16,5,256,256]{3,2,1,0:T(8,128)} %bitcast.32, f32[2,1024,256]{2,1,0:T(8,128)} %pad_maximum_fusion.own_ref), custom_call_target="tpu_custom_call" | custom-call | flops 3221225472 | bytes 8388608 | tf_op jit(solution)/shard_map/pallas_call | solution.py:280
  182.3 4.1 %collective-permute-start.11 = (f32[4,256,256]{2,1,0:T(8,128)}, f32[4,256,256]{2,1,0:T(8,128)}, u32[]{:S(2)}, u32[]{:S(2)}) collective-permute-start(f32[4,256,256]{2,1,0:T(8,128)} %shard_map.107.refs_0_), channel_id=1, source_target_pairs={{0,4},{4,0},{1,5},{5,1},{2,6},{6,2},{3,7},{7,3},{8,12},{12,8},{9,1... | collective-permute-start | bytes 3145736 | tf_op jit(solution)/shard_map/ppermute | solution.py:343
  186.4 22.5 %shard_map.108 = (f32[4,256,512]{2,1,0:T(8,128)}, bf16[2,512,1024]{2,1,0:T(8,128)(2,1)}, bf16[2,512,1024]{2,1,0:T(8,128)(2,1)}) custom-call(s32[16]{0:T(128)} %bitcast.48, s32[2,4,4]{2,1,0:T(4,128)} %dynamic-slice_bitcast_fusion.2.tab, s32[2]{0:T(128)} %copy-done.15, f32[16,5,256,256]{3,2,1,0:T(8,128)} %bitcast.33, f32[2048,512]{1,0:T(8,128)} %bitcast.47, ...), custom_call_target="tpu_custom_call" | custom-call | flops 19327352832 | bytes 16777216 | tf_op jit(solution)/shard_map/pallas_call | solution.py:186
  209.0 11.4 %collective-permute-done.7.refs_1_.refs_0_ = f32[512,512]{1,0:T(8,128)S(1)} collective-permute-done((f32[512,512]{1,0:T(8,128)}, f32[512,512]{1,0:T(8,128)S(1)}, u32[]{:S(2)}, u32[]{:S(2)}) %collective-permute-start.7) | collective-permute-done | bytes 1048608 | tf_op jit(solution)/shard_map/ppermute | solution.py:363
  221.7 1.8 collective-permute-start.12
  228.8 14.2 %shard_map.114.refs_0_ = f32[4,256,512]{2,1,0:T(8,128)} custom-call(s32[16]{0:T(128)} %bitcast.49, s32[2,4,4]{2,1,0:T(4,128)} %dynamic-slice_bitcast_fusion.2.tab, s32[2]{0:T(128)} %copy-done.15, f32[16,5,256,256]{3,2,1,0:T(8,128)} %bitcast.34, bf16[2,512,1024]{2,1,0:T(8,128)(2,1)} %get-tuple-element.7.turned_high, ...), custom_call_target="tpu_custom_call" | custom-call | flops 25769803776 | bytes 8388608 | tf_op jit(solution)/shard_map/pallas_call | solution.py:207
  243.0 4.4 %shard_map.117.refs_0_ = f32[4,256,256]{2,1,0:T(8,128)} custom-call(s32[2,4,4]{2,1,0:T(4,128)} %dynamic-slice_bitcast_fusion.2.tab, s32[1]{0:T(128)} %get-tuple-element.23.dests, s32[1]{0:T(128)} %bitcast.1.leaf_ref, f32[16,5,256,256]{3,2,1,0:T(8,128)} %bitcast.35, f32[2,1024,256]{2,1,0:T(8,128)} %pad_maximum_fusion.own_ref, f32[4,256,512]{2,1,0:T(8,128)} %shard_map.114.refs_0_), custom_call_target="tpu_custom_call" | custom-call | flops 3221225472 | bytes 8388608 | tf_op jit(solution)/shard_map/pallas_call | solution.py:280
  247.4 20.6 %collective-permute-done.12 = f32[4,256,512]{2,1,0:T(8,128)} collective-permute-done((f32[4,256,512]{2,1,0:T(8,128)}, f32[4,256,512]{2,1,0:T(8,128)}, u32[]{:S(2)}, u32[]{:S(2)}) %collective-permute-start.12) | collective-permute-done | bytes 2097184 | tf_op jit(solution)/shard_map/ppermute | solution.py:343
  268.0 3.4 add_negate_fusion
  271.4 1.7 collective-permute-start.18
  283.6 6.1 %shard_map.119.refs_0_ = f32[1,512,512]{2,1,0:T(8,128)} custom-call(s32[2]{0:T(128)} %pad_add_fusion.1.info, f32[512,512]{1,0:T(8,128)} %copy-done.4, f32[512,512]{1,0:T(8,128)} %shard_map.104.refs_1_, f32[512,512]{1,0:T(8,128)} %shard_map.105.refs_2_, f32[512,512]{1,0:T(8,128)} %shard_map.106.refs_3_, f32[512,512]{1,0:T(8,128)} %shard_map.110.refs_4_, ...), custom_call_target="tpu_custom_call" | custom-call | flops 1610612736 | bytes 4194304 | tf_op jit(solution)/shard_map/pallas_call | solution.py:319
  289.8 10.0 %shard_map.120.refs_15_ = f32[4,256,256]{2,1,0:T(8,128)} custom-call(s32[2,4,4]{2,1,0:T(4,128)} %dynamic-slice_bitcast_fusion.2.tab, s32[1]{0:T(128)} %get-tuple-element.24.dests, s32[1]{0:T(128)} %bitcast.1.leaf_ref, f32[16,5,256,256]{3,2,1,0:T(8,128)} %bitcast.36, f32[2,1024,256]{2,1,0:T(8,128)} %pad_maximum_fusion.own_ref, f32[1,512,512]{2,1,0:T(8,128)} %shard_map.119.refs_0_), custom_call_target="tpu_custom_call" | custom-call | flops 3221225472 | bytes 8388608 | tf_op jit(solution)/shard_map/pallas_call | solution.py:280
  302.0 6.1 %shard_map.121.refs_0_.refs_15_ = f32[1,512,512]{2,1,0:T(8,128)} custom-call(s32[2]{0:T(128)} %pad_add_fusion.info, f32[512,512]{1,0:T(8,128)} %copy-done.4, f32[512,512]{1,0:T(8,128)} %shard_map.104.refs_1_, f32[512,512]{1,0:T(8,128)} %shard_map.105.refs_2_, f32[512,512]{1,0:T(8,128)} %shard_map.106.refs_3_, f32[512,512]{1,0:T(8,128)} %shard_map.110.refs_4_, ...), custom_call_target="tpu_custom_call" | custom-call | flops 1610612736 | bytes 4194304 | tf_op jit(solution)/shard_map/pallas_call | solution.py:319
  317.8 9.8 %shard_map.122 = f32[4,256,256]{2,1,0:T(8,128)} custom-call(s32[2,4,4]{2,1,0:T(4,128)} %dynamic-slice_bitcast_fusion.2.tab, s32[1]{0:T(128)} %get-tuple-element.24.dests, s32[1]{0:T(128)} %bitcast.1.leaf_ref, f32[16,5,256,256]{3,2,1,0:T(8,128)} %bitcast.37, f32[2,1024,256]{2,1,0:T(8,128)} %pad_maximum_fusion.own_ref, f32[1,512,512]{2,1,0:T(8,128)} %shard_map.121.refs_0_.refs_15_), custom_call_target="tpu_custom_call" | custom-call | flops 3221225472 | bytes 8388608 | tf_op jit(solution)/shard_map/pallas_call | solution.py:280
  327.5 1.7 add.92
  330.7 8.5 %shard_map.123 = f32[2,512,512]{2,1,0:T(8,128)} custom-call(s32[3]{0:T(128)} %pad_add_fusion.2.info, f32[512,512]{1,0:T(8,128)} %copy-done.4, f32[512,512]{1,0:T(8,128)} %shard_map.104.refs_1_, f32[512,512]{1,0:T(8,128)} %shard_map.105.refs_2_, f32[512,512]{1,0:T(8,128)} %shard_map.106.refs_3_, f32[512,512]{1,0:T(8,128)} %shard_map.110.refs_4_, ...), custom_call_target="tpu_custom_call" | custom-call | flops 3221225472 | bytes 6291456 | tf_op jit(solution)/shard_map/pallas_call | solution.py:319
  339.2 5.6 %collective-permute-done.20 = f32[1,512,512]{2,1,0:T(8,128)S(1)} collective-permute-done((f32[1,512,512]{2,1,0:T(8,128)}, f32[1,512,512]{2,1,0:T(8,128)S(1)}, u32[]{:S(2)}, u32[]{:S(2)}) %collective-permute-start.20) | collective-permute-done | bytes 1048608 | tf_op jit(solution)/shard_map/ppermute | solution.py:343
  344.8 2.4 fusion.1
  347.2 1.8 maximum_subtract_fusion
  (98 shorter events, 38.7 us)
Async XLA Ops:
  7.2 160.3 %all-gather.3.cloned.1.call-start = ((), (), s32[]{:S(2)}) async-start(), calls=%async_computation | async-start | bytes 22282240 | tf_op jit(solution)/shard_map/all_gather | solution.py:388
  9.1 20.6 %collective-permute-start.2 = (f32[512,256]{1,0:T(8,128)}, f32[512,256]{1,0:T(8,128)}, u32[]{:S(2)}, u32[]{:S(2)}) collective-permute-start(f32[512,256]{1,0:T(8,128)} %slice.65), channel_id=1, source_target_pairs={{0,16},{1,17},{2,18},{3,19},{4,20},{5,21},{6,22},{7,23}} | collective-permute-start | bytes 1572872 | tf_op jit(solution)/shard_map/ppermute | solution.py:384
  17.7 22.3 %collective-permute-start = (f32[1024,256]{1,0:T(8,128)}, f32[1024,256]{1,0:T(8,128)}, u32[]{:S(2)}, u32[]{:S(2)}) collective-permute-start(f32[1024,256]{1,0:T(8,128)} %get-tuple-element.16), channel_id=1, source_target_pairs={{0,4},{4,0},{1,5},{5,1},{2,6},{6,2},{3,7},{7,3},{8,12},{12,8},{9,1... | collective-permute-start | bytes 3145736 | tf_op jit(solution)/shard_map/ppermute | solution.py:379
  19.2 20.7 %collective-permute-start.1 = (f32[1024,256]{1,0:T(8,128)}, f32[1024,256]{1,0:T(8,128)}, u32[]{:S(2)}, u32[]{:S(2)}) collective-permute-start(f32[1024,256]{1,0:T(8,128)} %get-tuple-element.15), channel_id=1, source_target_pairs={{8,24},{9,25},{10,26},{11,27}} | collective-permute-start | bytes 3145736 | tf_op jit(solution)/shard_map/ppermute | solution.py:380
  23.6 19.6 %copy-start.4 = (f32[512,512]{1,0:T(8,128)}, f32[512,512]{1,0:T(8,128)S(1)}, u32[]{:S(2)}) copy-start(f32[512,512]{1,0:T(8,128)S(1)} %get-tuple-element.12.refs_0_) | copy-start | bytes 3145732
  23.6 10.0 %copy-start.17 = (s32[2]{0:T(128)S(1)}, s32[2]{0:T(128)}, u32[]{:S(2)}) copy-start(s32[2]{0:T(128)} %constant.106.clone) | copy-start | bytes 28
  23.7 11.2 %copy-start.16 = (pred[2,4]{1,0:T(4,128)(4,1)S(1)}, pred[2,4]{1,0:T(4,128)(4,1)}, u32[]{:S(2)}) copy-start(pred[2,4]{1,0:T(4,128)(4,1)} %constant.107.clone) | copy-start | bytes 28
  23.7 26.4 %collective-permute-start.4 = (f32[512,512]{1,0:T(8,128)S(1)}, f32[512,512]{1,0:T(8,128)S(1)}, u32[]{:S(2)}, u32[]{:S(2)}) collective-permute-start(f32[512,512]{1,0:T(8,128)S(1)} %get-tuple-element.12.refs_0_), channel_id=1, source_target_pairs={{1,0},{2,1},{3,2},{5,4},{6,5},{7,6},{9,8},{10,9},{11,10},{13,12},{... | collective-permute-start | bytes 3145736 | tf_op jit(solution)/shard_map/ppermute | solution.py:363
  25.1 26.1 %collective-permute-start.5 = (f32[512,512]{1,0:T(8,128)S(1)}, f32[512,512]{1,0:T(8,128)S(1)}, u32[]{:S(2)}, u32[]{:S(2)}) collective-permute-start(f32[512,512]{1,0:T(8,128)S(1)} %get-tuple-element.12.refs_0_), channel_id=1, source_target_pairs={{0,1},{1,2},{2,3},{4,5},{5,6},{6,7},{8,9},{9,10},{10,11},{12,13},{... | collective-permute-start | bytes 3145736 | tf_op jit(solution)/shard_map/ppermute | solution.py:363
  31.6 3.8 %collective-permute-start.3 = (f32[256,256]{1,0:T(8,128)S(1)}, f32[256,256]{1,0:T(8,128)}, u32[]{:S(2)}, u32[]{:S(2)}) collective-permute-start(f32[256,256]{1,0:T(8,128)S(1)} %slice.81), channel_id=1, source_target_pairs={{0,8},{16,24},{1,9},{17,25},{2,10},{18,26},{3,11},{19,27},{4,12},{... | collective-permute-start | bytes 786440 | tf_op jit(solution)/shard_map/ppermute | solution.py:385
  44.4 7.8 %copy-start.14 = (s32[2,2,4,4]{3,2,1,0:T(4,128)S(1)}, s32[2,2,4,4]{3,2,1,0:T(4,128)}, u32[]{:S(2)}) copy-start(s32[2,2,4,4]{3,2,1,0:T(4,128)} %constant.105.clone) | copy-start | bytes 772
  52.2 4.2 %copy-start.15 = (s32[2]{0:T(128)}, s32[2]{0:T(128)S(1)}, u32[]{:S(2)}) copy-start(s32[2]{0:T(128)S(1)} %and_select_fusion.order) | copy-start | bytes 28
  167.4 56.1 %collective-permute-start.6 = (f32[512,512]{1,0:T(8,128)}, f32[512,512]{1,0:T(8,128)}, u32[]{:S(2)}, u32[]{:S(2)}) collective-permute-start(f32[512,512]{1,0:T(8,128)} %shard_map.104.refs_1_), channel_id=1, source_target_pairs={{0,1},{1,2},{2,3},{4,5},{5,6},{6,7},{8,9},{9,10},{10,11},{12,13},{... | collective-permute-start | bytes 3145736 | tf_op jit(solution)/shard_map/ppermute | solution.py:363
  171.8 52.5 %collective-permute-start.9 = (f32[512,512]{1,0:T(8,128)}, f32[512,512]{1,0:T(8,128)S(1)}, u32[]{:S(2)}, u32[]{:S(2)}) collective-permute-start(f32[512,512]{1,0:T(8,128)} %shard_map.104.refs_1_), channel_id=1, source_target_pairs={{1,0},{2,1},{3,2},{5,4},{6,5},{7,6},{9,8},{10,9},{11,10},{13,12},{... | collective-permute-start | bytes 3145736 | tf_op jit(solution)/shard_map/ppermute | solution.py:363
  173.1 47.2 %collective-permute-start.7 = (f32[512,512]{1,0:T(8,128)}, f32[512,512]{1,0:T(8,128)S(1)}, u32[]{:S(2)}, u32[]{:S(2)}) collective-permute-start(f32[512,512]{1,0:T(8,128)} %shard_map.106.refs_3_), channel_id=1, source_target_pairs={{1,0},{2,1},{5,4},{6,5},{9,8},{10,9},{13,12},{14,13},{17,16},{18,1... | collective-permute-start | bytes 3145736 | tf_op jit(solution)/shard_map/ppermute | solution.py:363
  174.4 45.9 %collective-permute-start.8 = (f32[512,512]{1,0:T(8,128)}, f32[512,512]{1,0:T(8,128)S(1)}, u32[]{:S(2)}, u32[]{:S(2)}) collective-permute-start(f32[512,512]{1,0:T(8,128)} %shard_map.105.refs_2_), channel_id=1, source_target_pairs={{1,2},{2,3},{5,6},{6,7},{9,10},{10,11},{13,14},{14,15},{17,18},{18... | collective-permute-start | bytes 3145736 | tf_op jit(solution)/shard_map/ppermute | solution.py:363
  182.3 44.9 %collective-permute-start.11 = (f32[4,256,256]{2,1,0:T(8,128)}, f32[4,256,256]{2,1,0:T(8,128)}, u32[]{:S(2)}, u32[]{:S(2)}) collective-permute-start(f32[4,256,256]{2,1,0:T(8,128)} %shard_map.107.refs_0_), channel_id=1, source_target_pairs={{0,4},{4,0},{1,5},{5,1},{2,6},{6,2},{3,7},{7,3},{8,12},{12,8},{9,1... | collective-permute-start | bytes 3145736 | tf_op jit(solution)/shard_map/ppermute | solution.py:343
  220.3 1.3 copy-start.3
  221.7 46.3 %collective-permute-start.12 = (f32[4,256,512]{2,1,0:T(8,128)}, f32[4,256,512]{2,1,0:T(8,128)}, u32[]{:S(2)}, u32[]{:S(2)}) collective-permute-start(f32[4,256,512]{2,1,0:T(8,128)} %shard_map.109.refs_1_), channel_id=1, source_target_pairs={{0,4},{4,0},{1,5},{5,1},{2,6},{6,2},{3,7},{7,3},{8,12},{12,8},{9,1... | collective-permute-start | bytes 6291464 | tf_op jit(solution)/shard_map/ppermute | solution.py:343
  223.5 49.6 %collective-permute-start.10 = (f32[512,512]{1,0:T(8,128)}, f32[512,512]{1,0:T(8,128)S(1)}, u32[]{:S(2)}, u32[]{:S(2)}) collective-permute-start(f32[512,512]{1,0:T(8,128)} %shard_map.110.refs_4_), channel_id=1, source_target_pairs={{1,2},{2,3},{5,6},{6,7},{9,10},{10,11},{13,14},{14,15},{17,18},{18... | collective-permute-start | bytes 3145736 | tf_op jit(solution)/shard_map/ppermute | solution.py:363
  225.2 50.5 %collective-permute-start.13 = (f32[512,512]{1,0:T(8,128)}, f32[512,512]{1,0:T(8,128)S(1)}, u32[]{:S(2)}, u32[]{:S(2)}) collective-permute-start(f32[512,512]{1,0:T(8,128)} %shard_map.111.refs_5_), channel_id=1, source_target_pairs={{1,0},{2,1},{5,4},{6,5},{9,8},{10,9},{13,12},{14,13},{17,16},{18,1... | collective-permute-start | bytes 3145736 | tf_op jit(solution)/shard_map/ppermute | solution.py:363
  226.5 73.3 %collective-permute-start.14 = (f32[512,512]{1,0:T(8,128)}, f32[512,512]{1,0:T(8,128)S(1)}, u32[]{:S(2)}, u32[]{:S(2)}) collective-permute-start(f32[512,512]{1,0:T(8,128)} %shard_map.112.refs_6_), channel_id=1, source_target_pairs={{2,3},{6,7},{10,11},{14,15},{18,19},{22,23},{26,27},{30,31}} | collective-permute-start | bytes 3145736 | tf_op jit(solution)/shard_map/ppermute | solution.py:363
  227.3 72.6 %collective-permute-start.15 = (f32[512,512]{1,0:T(8,128)}, f32[512,512]{1,0:T(8,128)}, u32[]{:S(2)}, u32[]{:S(2)}) collective-permute-start(f32[512,512]{1,0:T(8,128)} %shard_map.113.refs_7_), channel_id=1, source_target_pairs={{1,0},{5,4},{9,8},{13,12},{17,16},{21,20},{25,24},{29,28}} | collective-permute-start | bytes 3145736 | tf_op jit(solution)/shard_map/ppermute | solution.py:363
  243.0 25.0 %copy-start.9 = (f32[4,256,512]{2,1,0:T(8,128)S(1)}, f32[4,256,512]{2,1,0:T(8,128)}, u32[]{:S(2)}) copy-start(f32[4,256,512]{2,1,0:T(8,128)} %shard_map.114.refs_0_) | copy-start | bytes 6291460
  271.4 28.5 %collective-permute-start.18 = (f32[4,256,256]{2,1,0:T(8,128)}, f32[4,256,256]{2,1,0:T(8,128)}, u32[]{:S(2)}, u32[]{:S(2)}) collective-permute-start(f32[4,256,256]{2,1,0:T(8,128)} %shard_map.118.refs_11_), channel_id=1, source_target_pairs={{0,4},{4,0},{1,5},{5,1},{2,6},{6,2},{3,7},{7,3},{8,12},{12,8},{9,1... | collective-permute-start | bytes 3145736 | tf_op jit(solution)/shard_map/ppermute | solution.py:343
  274.1 25.8 %collective-permute-start.16 = (f32[512,512]{1,0:T(8,128)}, f32[512,512]{1,0:T(8,128)}, u32[]{:S(2)}, u32[]{:S(2)}) collective-permute-start(f32[512,512]{1,0:T(8,128)} %shard_map.115.refs_8_), channel_id=1, source_target_pairs={{2,3},{6,7},{10,11},{14,15},{18,19},{22,23},{26,27},{30,31}} | collective-permute-start | bytes 3145736 | tf_op jit(solution)/shard_map/ppermute | solution.py:363
  276.8 24.3 %collective-permute-start.17 = (f32[512,512]{1,0:T(8,128)}, f32[512,512]{1,0:T(8,128)S(1)}, u32[]{:S(2)}, u32[]{:S(2)}) collective-permute-start(f32[512,512]{1,0:T(8,128)} %shard_map.116.refs_9_), channel_id=1, source_target_pairs={{1,0},{5,4},{9,8},{13,12},{17,16},{21,20},{25,24},{29,28}} | collective-permute-start | bytes 3145736 | tf_op jit(solution)/shard_map/ppermute | solution.py:363
  299.8 16.6 %copy-start.8 = (f32[4,256,256]{2,1,0:T(8,128)S(1)}, f32[4,256,256]{2,1,0:T(8,128)}, u32[]{:S(2)}) copy-start(f32[4,256,256]{2,1,0:T(8,128)} %shard_map.120.refs_15_) | copy-start | bytes 3145732
  299.8 1.2 copy-start.10
  299.8 39.4 %collective-permute-start.19 = (f32[1,512,512]{2,1,0:T(8,128)}, f32[1,512,512]{2,1,0:T(8,128)}, u32[]{:S(2)}, u32[]{:S(2)}) collective-permute-start(f32[1,512,512]{2,1,0:T(8,128)} %shard_map.119.refs_0_), channel_id=1, source_target_pairs={{0,4},{4,0},{1,5},{5,1},{2,6},{6,2},{3,7},{7,3},{8,12},{12,8},{9,1... | collective-permute-start | bytes 3145736 | tf_op jit(solution)/shard_map/ppermute | solution.py:343
  308.1 36.6 %collective-permute-start.20 = (f32[1,512,512]{2,1,0:T(8,128)}, f32[1,512,512]{2,1,0:T(8,128)S(1)}, u32[]{:S(2)}, u32[]{:S(2)}) collective-permute-start(f32[1,512,512]{2,1,0:T(8,128)} %shard_map.121.refs_0_.refs_15_), channel_id=1, source_target_pairs={{0,4},{4,0},{1,5},{5,1},{2,6},{6,2},{3,7},{7,3},{8,12},{12,8},{9,1... | collective-permute-start | bytes 3145736 | tf_op jit(solution)/shard_map/ppermute | solution.py:343
  339.2 8.0 %copy-start.12 = (f32[1,1024,512]{2,1,0:T(8,128)S(1)}, f32[1,1024,512]{2,1,0:T(8,128)}, u32[]{:S(2)}) copy-start(f32[1,1024,512]{2,1,0:T(8,128)} %param.11) | copy-start | bytes 6291460
  (8 other events, 7.9 us)
Sparse Core Ops, SparseCore 0:
  52.3 115.0 all-gather.2

commit v7 on v6

--- a/solution.py
+++ b/solution.py
@@ -111,20 +111,31 @@
 
     image[...] = jnp.zeros_like(image)
 
-    @pl.loop(0, number // 2)
-    def _(kp):
-        span = pl.ds(pl.multiple_of(kp * 2 * BLK, 2 * BLK), 2 * BLK)
+    group = 2 if number % 4 == 0 else 1
+
+    @pl.loop(0, number // 2 // group)
+    def _(step):
+        deep = 2 * group * BLK
+        span = pl.ds(pl.multiple_of(step * deep, deep), deep)
         p_high, p_low = halves(p_ref[span, :])
         stacked = jnp.concatenate([p_high, p_low, p_high], axis=0)
+        pairs = [step * group + m for m in range(group)]
         for s in range(2):
-            wait_pair(lay, pat, tab, t, sems, kp, s)
-
-            @pl.when(any_valid(lay, pat, tab, kp, s))
+            found = False
+            for kp in pairs:
+                wait_pair(lay, pat, tab, t, sems, kp, s)
+                found = jnp.logical_or(found, any_valid(lay, pat, tab, kp, s))
+
+            @pl.when(found)
             def _():
-                high, low = halves(jnp.concatenate([t[2 * kp, s], t[2 * kp + 1, s]], axis=1))
-                th[kp, s] = high
-                tl[kp, s] = low
-                image[s] += dot(jnp.concatenate([high, high, low], axis=1), stacked)
+                highs, lows = [], []
+                for kp in pairs:
+                    high, low = halves(jnp.concatenate([t[2 * kp, s], t[2 * kp + 1, s]], axis=1))
+                    th[kp, s] = high
+                    tl[kp, s] = low
+                    highs.append(high)
+                    lows.append(low)
+                image[s] += dot(jnp.concatenate(highs + highs + lows, axis=1), stacked)
 
     for s in range(2):
         high, low = halves(image[s].T)
@@ -292,12 +303,12 @@
     )(table, dests, me_leaf, gathered, own, *tokens)
 
 
-def diagonal_kernel(steps, tokens, info, *refs):
+def diagonal_kernel(steps, first, tokens, info, *refs):
     sources, refs = list(zip(steps, refs)), refs[len(steps) :]
     sigma, (out_ref, held, sems) = refs[0], refs[1 + tokens :]
     each = out_ref.shape[0]
     for i in range(each):
-        away = info[i] - info[each]
+        away = info[1 + first + i] - info[0]
         for (step, run), source in sources:
 
             @pl.when(away == step)
@@ -313,18 +324,17 @@
         out_ref[i] = total.T
 
 
-def diagonal_product(blocks, me_col, pieces, sigma, tokens):
-    each = blocks.shape[0]
+def diagonal_product(info, first, each, pieces, sigma, tokens):
     depth, wide = sigma.shape
     return pl.pallas_call(
-        functools.partial(diagonal_kernel, tuple(pieces), len(tokens)),
+        functools.partial(diagonal_kernel, tuple(pieces), first, len(tokens)),
         out_shape=jax.ShapeDtypeStruct((each, wide, wide), jnp.float32),
         in_specs=[SMEM] + [ANY] * len(pieces) + [VMEM] + [ANY] * len(tokens),
         out_specs=VMEM,
         scratch_shapes=[pltpu.VMEM((each, depth, wide), jnp.float32), pltpu.SemaphoreType.DMA((each,))],
         compiler_params=pltpu.CompilerParams(vmem_limit_bytes=VMEM_BYTES),
         cost_estimate=estimate(6 * each * depth * wide * wide, (each + 1) * depth * wide),
-    )(jnp.append(blocks, me_col).astype(jnp.int32), *pieces.values(), sigma, *tokens)
+    )(info, *pieces.values(), sigma, *tokens)
 
 
 def after(value, *earlier):
@@ -388,17 +398,22 @@
     gathered = lax.all_gather(after(held, pieces[1, 0], pieces[-1, 0]), ("leaf", "col"), axis=0, tiled=False)
     own = jnp.stack([lower, swapped])
     hop(1, 0, gathered)
-    hop(0, 1, gathered)
 
     chunks, each = 2, cols // rows
     order = ((me_row + 1 + jnp.arange(rows)) % rows).astype(jnp.int32)
+    near = [[sorted(range(d * each, d * each + each), key=lambda block: abs(block - c)) for c in range(cols)] for d in range(rows)]
+    near = np.asarray(near, np.int32)
+    reach = np.abs(near - np.arange(cols)[None, :, None]).max(axis=(0, 1))
+    near_here = jnp.asarray(near)[:, me_col]
+    wanted = near_here[order[: rows - 1]].reshape(-1)
+    info = jnp.concatenate([me_col[None], wanted, me_row * each + jnp.arange(each)]).astype(jnp.int32)
     leaf_here = me_leaf.astype(jnp.int32)[None]
     top_args = (leaf_here, gathered, own, chunks)
-    early = top_product(lay, table, order[: rows - 1], *top_args, 0)
+    early = top_product(lay, table, order[: rows - 1], *top_args, 0, [info])
     early_in = send_over_rows(early)
+    if cols > 2:
+        hop(0, 1, *early)
     sent, turned = panel_product(lay, pattern[0], table, order, gathered, normed, early)
-    if cols > 2:
-        sent = [after(value, pieces[2, 0], pieces[-2, 0]) for value in sent]
     sent_in = send_over_rows(sent)
     middle = cols // 2
     for step in range(1, middle):
@@ -415,29 +430,23 @@
         if step + 1 < cols - 1:
             hop(0, step + 1, sigma_panel)
 
-    near = [[sorted(range(d * each, d * each + each), key=lambda block: abs(block - c)) for c in range(cols)] for d in range(rows)]
-    near = np.asarray(near, np.int32)
-    reach = np.abs(near - np.arange(cols)[None, :, None]).max(axis=(0, 1))
-    near_here = jnp.asarray(near)[:, me_col]
     terms_in, tokens = [], late
     for i in range(each):
         there = {key: piece for key, piece in pieces.items() if abs(key[0]) <= reach[i]}
-        term = [
-            diagonal_product(near_here[order[a]][i : i + 1], me_col, there, sigma_panel, tokens)
-            for a in range(rows - 1)
-        ]
+        term = [diagonal_product(info, a * each + i, 1, there, sigma_panel, tokens) for a in range(rows - 1)]
         terms_in.append(send_over_rows(term))
-        if i == 0:
-            tops = list(top_product(lay, table, order[rows - 1 :], *top_args, 1, term))
-        tokens = tops + late_in
-    tops = list(top_product(lay, table, order[rows - 1 :], *top_args, 0, term)) + tops
-    mine = me_row * each + jnp.arange(each)
-    update = list(diagonal_product(mine, me_col, pieces, sigma_panel, term))
+        tokens = term + late_in
+    mine = diagonal_product(info, (rows - 1) * each, each, pieces, sigma_panel, term)
+    rest = diag_inverse[0] - mine.reshape(diag_inverse.shape[1:])
+    tops = [top_product(lay, table, order[rows - 1 :], *top_args, chunk, [mine])[0] for chunk in range(chunks)]
+    update = []
     for block in range(each):
+        total = 0.0
         for i in range(each):
             for value in terms_in[i]:
-                update[block] += jnp.where(near_here[me_row, i] == mine[block], value[0], 0.0)
-    sigma_diag = diag_inverse[0] - jnp.concatenate(update, axis=0)
+                total += jnp.where(near_here[me_row, i] == me_row * each + block, value[0], 0.0)
+        update.append(total)
+    sigma_diag = rest - jnp.concatenate(update, axis=0)
 
     sigma_top = jnp.concatenate([sum(early_in, tops[0]), sum(late_in, tops[1])], axis=0).reshape(-1, width)
     return (sigma_top, sigma_panel[None], sigma_diag[None])

time: 357 us -> 345 us (0.966)
  waiting for transfers between devices: 160 us -> 151 us
  other arithmetic: 24.7 us -> 20.8 us
    ppermute x5, waiting for transfers between devices: 26.2 us -> 14.8 us  [send_over_rows(): lax.ppermute(value, 'row', [(i, (i + a + 1) % rows) for i in range(rows)])]
    ppermute x12, waiting for transfers between devices: 19.2 us -> 24.8 us  [hop(): lax.ppermute(pieces[-way * step, run], 'col', [(i, i + way) for i in at])]
  transfers between devices with their start and end apart: 22 -> 22, of which waited for: 8 -> 8; matrix products, arithmetic and copies ran while one was open for 9% -> 8% of each run, Pallas kernels for 25% -> 26%
where the time goes in v7:
time: 345 us; the launch traced here: 341 us
  waiting for transfers between devices  151 us (44%)
  Pallas kernels  87.7 us (25%)
  starting transfers between devices  43.7 us (13%)
  other arithmetic  20.8 us (6%)
  between operations  19.5 us (6%)
  local copies, waits for them, and re-layouts  18.1 us (5%)
    all_gather x1, waiting for transfers between devices, per_device(): lax.all_gather(after(held, pieces[1, 0], pieces[-1, 0]), ('leaf', 'col'),...  108 us
    pallas_call x4, Pallas kernels, top_product(): pl.pallas_call(functools.partial(top_kernel, lay, chunks, chunk, len(toke...  31.2 us
    ppermute x12, waiting for transfers between devices, hop(): lax.ppermute(pieces[-way * step, run], 'col', [(i, i + way) for i in at])  24.8 us
    pallas_call x1, Pallas kernels, panel_product(): pl.pallas_call(functools.partial(panel_kernel, lay, rows, len(tokens)), o...  21.5 us
    ppermute x12, starting transfers between devices, hop(): lax.ppermute(pieces[-way * step, run], 'col', [(i, i + way) for i in at])  20.8 us
    pallas_call x3, Pallas kernels, diagonal_product(): pl.pallas_call(functools.partial(diagonal_kernel, tuple(pieces), first, l...  20.7 us
    ppermute x5, waiting for transfers between devices, send_over_rows(): lax.ppermute(value, 'row', [(i, (i + a + 1) % rows) for i in range(rows)])  14.8 us
    pallas_call x1, Pallas kernels, own_panel_product(): pl.pallas_call(functools.partial(own_panel_kernel, lay, rows, len(tokens)...  14.2 us
  transfers between devices with their start and end apart: 22, of which 8 were waited for; matrix products, arithmetic and copies ran while one was open for 8% of the time, Pallas kernels for 26%

profile of v7, /device:TPU:0, one launch (start us, length us, event | category | flops | bytes accessed | tf_op | source)
XLA Modules:
  0.0 340.9 jit_solution(570012965314784494)
XLA Ops:
  7.2 1.9 slice.44
  9.1 5.7 %collective-permute-start.2 = (f32[512,256]{1,0:T(8,128)}, f32[512,256]{1,0:T(8,128)}, u32[]{:S(2)}, u32[]{:S(2)}) collective-permute-start(f32[512,256]{1,0:T(8,128)} %slice.44), channel_id=1, source_target_pairs={{0,16},{1,17},{2,18},{3,19},{4,20},{5,21},{6,22},{7,23}} | collective-permute-start | bytes 1572872 | tf_op jit(solution)/shard_map/ppermute | solution.py:394
  14.7 3.0 fusion.3
  19.2 1.7 collective-permute-start.1
  20.9 2.7 dynamic-slice_bitcast_fusion
  25.0 4.6 %collective-permute-start.5 = (f32[512,512]{1,0:T(8,128)S(1)}, f32[512,512]{1,0:T(8,128)S(1)}, u32[]{:S(2)}, u32[]{:S(2)}) collective-permute-start(f32[512,512]{1,0:T(8,128)S(1)} %get-tuple-element.21.refs_0_), channel_id=1, source_target_pairs={{0,1},{1,2},{2,3},{4,5},{5,6},{6,7},{8,9},{9,10},{10,11},{12,13},{... | collective-permute-start | bytes 3145736 | tf_op jit(solution)/shard_map/ppermute | solution.py:373
  31.6 2.0 collective-permute-start.3
  36.3 3.7 %collective-permute-done = f32[1024,256]{1,0:T(8,128)} collective-permute-done((f32[1024,256]{1,0:T(8,128)}, f32[1024,256]{1,0:T(8,128)}, u32[]{:S(2)}, u32[]{:S(2)}) %collective-permute-start) | collective-permute-done | bytes 1048608 | tf_op jit(solution)/shard_map/ppermute | solution.py:389
  40.0 3.3 slice_bitcast_fusion
  44.5 5.5 %collective-permute-done.4.refs_1_.refs_0_ = f32[512,512]{1,0:T(8,128)S(1)} collective-permute-done((f32[512,512]{1,0:T(8,128)S(1)}, f32[512,512]{1,0:T(8,128)S(1)}, u32[]{:S(2)}, u32[]{:S(2)}) %collective-permute-start.4) | collective-permute-done | bytes 1048608 | tf_op jit(solution)/shard_map/ppermute | solution.py:373
  56.5 3.0 pad_maximum_fusion.own_ref
  59.5 107.9 %all-gather.3.cloned.1.call-done = f32[80,256,256]{2,1,0:T(8,128)} async-done(((f32[5,256,256]{2,1,0:T(8,128)}), f32[80,256,256]{2,1,0:T(8,128)}) %all-gather.3.cloned.1.call-update) | async-done | bytes 20971536 | tf_op jit(solution)/shard_map/all_gather | solution.py:398
  167.4 3.4 %collective-permute-start.6 = (f32[512,512]{1,0:T(8,128)}, f32[512,512]{1,0:T(8,128)S(1)}, u32[]{:S(2)}, u32[]{:S(2)}) collective-permute-start(f32[512,512]{1,0:T(8,128)} %shard_map.104.refs_1_), channel_id=1, source_target_pairs={{0,1},{1,2},{2,3},{4,5},{5,6},{6,7},{8,9},{9,10},{10,11},{12,13},{... | collective-permute-start | bytes 3145736 | tf_op jit(solution)/shard_map/ppermute | solution.py:373
  172.1 7.2 %shard_map.105.refs_1_.refs_0_ = f32[4,256,256]{2,1,0:T(8,128)} custom-call(s32[2,4,4]{2,1,0:T(4,128)} %dynamic-slice_bitcast_fusion.2.tab, s32[1]{0:T(128)} %get-tuple-element.30.dests, s32[1]{0:T(128)} %bitcast.1.leaf_ref, f32[16,5,256,256]{3,2,1,0:T(8,128)} %bitcast.33, f32[2,1024,256]{2,1,0:T(8,128)} %pad_maximum_fusion.own_ref, s32[5]{0:T(128)} %pad_add_fusion.refs_0_.info), custom_call_target="tpu_custom_call" | custom-call | flops 3221225472 | bytes 8388608 | tf_op jit(solution)/shard_map/pallas_call | solution.py:291
  179.3 4.1 %collective-permute-start.11 = (f32[4,256,256]{2,1,0:T(8,128)}, f32[4,256,256]{2,1,0:T(8,128)}, u32[]{:S(2)}, u32[]{:S(2)}) collective-permute-start(f32[4,256,256]{2,1,0:T(8,128)} %shard_map.105.refs_1_.refs_0_), channel_id=1, source_target_pairs={{0,4},{4,0},{1,5},{5,1},{2,6},{6,2},{3,7},{7,3},{8,12},{12,8},{9,1... | collective-permute-start | bytes 3145736 | tf_op jit(solution)/shard_map/ppermute | solution.py:353
  186.3 21.5 %shard_map.108 = (f32[4,256,512]{2,1,0:T(8,128)}, bf16[2,512,1024]{2,1,0:T(8,128)(2,1)}, bf16[2,512,1024]{2,1,0:T(8,128)(2,1)}) custom-call(s32[16]{0:T(128)} %bitcast.50, s32[2,4,4]{2,1,0:T(4,128)} %dynamic-slice_bitcast_fusion.2.tab, s32[2]{0:T(128)} %copy-done.16, f32[16,5,256,256]{3,2,1,0:T(8,128)} %bitcast.34, f32[2048,512]{1,0:T(8,128)} %bitcast.49, ...), custom_call_target="tpu_custom_call" | custom-call | flops 19327352832 | bytes 16777216 | tf_op jit(solution)/shard_map/pallas_call | solution.py:197
  207.9 4.3 %collective-permute-start.12 = (f32[4,256,512]{2,1,0:T(8,128)}, f32[4,256,512]{2,1,0:T(8,128)}, u32[]{:S(2)}, u32[]{:S(2)}) collective-permute-start(f32[4,256,512]{2,1,0:T(8,128)} %get-tuple-element.6.refs_1_), channel_id=1, source_target_pairs={{0,4},{4,0},{1,5},{5,1},{2,6},{6,2},{3,7},{7,3},{8,12},{12,8},{9,1... | collective-permute-start | bytes 6291464 | tf_op jit(solution)/shard_map/ppermute | solution.py:353
  214.6 4.8 %collective-permute-done.9.refs_0_ = f32[512,512]{1,0:T(8,128)S(1)} collective-permute-done((f32[512,512]{1,0:T(8,128)}, f32[512,512]{1,0:T(8,128)S(1)}, u32[]{:S(2)}, u32[]{:S(2)}) %collective-permute-start.9) | collective-permute-done | bytes 1048608 | tf_op jit(solution)/shard_map/ppermute | solution.py:373
  222.5 14.2 %shard_map.113.refs_0_ = f32[4,256,512]{2,1,0:T(8,128)} custom-call(s32[16]{0:T(128)} %bitcast.51, s32[2,4,4]{2,1,0:T(4,128)} %dynamic-slice_bitcast_fusion.2.tab, s32[2]{0:T(128)} %copy-done.16, f32[16,5,256,256]{3,2,1,0:T(8,128)} %bitcast.35, bf16[2,512,1024]{2,1,0:T(8,128)(2,1)} %get-tuple-element.7.turned_high, ...), custom_call_target="tpu_custom_call" | custom-call | flops 25769803776 | bytes 8388608 | tf_op jit(solution)/shard_map/pallas_call | solution.py:218
  236.7 4.4 %shard_map.116.refs_0_ = f32[4,256,256]{2,1,0:T(8,128)} custom-call(s32[2,4,4]{2,1,0:T(4,128)} %dynamic-slice_bitcast_fusion.2.tab, s32[1]{0:T(128)} %get-tuple-element.30.dests, s32[1]{0:T(128)} %bitcast.1.leaf_ref, f32[16,5,256,256]{3,2,1,0:T(8,128)} %bitcast.36, f32[2,1024,256]{2,1,0:T(8,128)} %pad_maximum_fusion.own_ref, f32[4,256,512]{2,1,0:T(8,128)} %shard_map.113.refs_0_), custom_call_target="tpu_custom_call" | custom-call | flops 3221225472 | bytes 8388608 | tf_op jit(solution)/shard_map/pallas_call | solution.py:291
  241.1 14.0 %collective-permute-done.12 = f32[4,256,512]{2,1,0:T(8,128)} collective-permute-done((f32[4,256,512]{2,1,0:T(8,128)}, f32[4,256,512]{2,1,0:T(8,128)}, u32[]{:S(2)}, u32[]{:S(2)}) %collective-permute-start.12) | collective-permute-done | bytes 2097184 | tf_op jit(solution)/shard_map/ppermute | solution.py:353
  255.1 3.4 add_negate_fusion
  262.5 1.7 collective-permute-start.18
  268.3 6.1 %shard_map.118.refs_15_ = f32[1,512,512]{2,1,0:T(8,128)} custom-call(s32[5]{0:T(128)} %pad_add_fusion.refs_0_.info, f32[512,512]{1,0:T(8,128)} %copy-done.3, f32[512,512]{1,0:T(8,128)} %shard_map.104.refs_1_, f32[512,512]{1,0:T(8,128)} %shard_map.106.refs_2_, f32[512,512]{1,0:T(8,128)} %shard_map.107.refs_3_, f32[512,512]{1,0:T(8,128)} %shard_map.109.refs_4_, ...), custom_call_target="tpu_custom_call" | custom-call | flops 1610612736 | bytes 4194304 | tf_op jit(solution)/shard_map/pallas_call | solution.py:329
  274.9 13.3 %collective-permute-done.17.refs_13_ = f32[512,512]{1,0:T(8,128)S(1)} collective-permute-done((f32[512,512]{1,0:T(8,128)}, f32[512,512]{1,0:T(8,128)S(1)}, u32[]{:S(2)}, u32[]{:S(2)}) %collective-permute-start.17) | collective-permute-done | bytes 1048608 | tf_op jit(solution)/shard_map/ppermute | solution.py:373
  289.1 6.1 %shard_map.119.refs_15_ = f32[1,512,512]{2,1,0:T(8,128)} custom-call(s32[5]{0:T(128)} %pad_add_fusion.refs_0_.info, f32[512,512]{1,0:T(8,128)} %copy-done.3, f32[512,512]{1,0:T(8,128)} %shard_map.104.refs_1_, f32[512,512]{1,0:T(8,128)} %shard_map.106.refs_2_, f32[512,512]{1,0:T(8,128)} %shard_map.107.refs_3_, f32[512,512]{1,0:T(8,128)} %shard_map.109.refs_4_, ...), custom_call_target="tpu_custom_call" | custom-call | flops 1610612736 | bytes 4194304 | tf_op jit(solution)/shard_map/pallas_call | solution.py:329
  296.8 8.5 %shard_map.120.refs_0_ = f32[2,512,512]{2,1,0:T(8,128)} custom-call(s32[5]{0:T(128)} %pad_add_fusion.refs_0_.info, f32[512,512]{1,0:T(8,128)} %copy-done.3, f32[512,512]{1,0:T(8,128)} %shard_map.104.refs_1_, f32[512,512]{1,0:T(8,128)} %shard_map.106.refs_2_, f32[512,512]{1,0:T(8,128)} %shard_map.107.refs_3_, f32[512,512]{1,0:T(8,128)} %shard_map.109.refs_4_, ...), custom_call_target="tpu_custom_call" | custom-call | flops 3221225472 | bytes 6291456 | tf_op jit(solution)/shard_map/pallas_call | solution.py:329
  305.3 9.9 %shard_map.122 = f32[4,256,256]{2,1,0:T(8,128)} custom-call(s32[2,4,4]{2,1,0:T(4,128)} %dynamic-slice_bitcast_fusion.2.tab, s32[1]{0:T(128)} %get-tuple-element.31.dests, s32[1]{0:T(128)} %bitcast.1.leaf_ref, f32[16,5,256,256]{3,2,1,0:T(8,128)} %bitcast.37, f32[2,1024,256]{2,1,0:T(8,128)} %pad_maximum_fusion.own_ref, f32[2,512,512]{2,1,0:T(8,128)} %shard_map.120.refs_0_), custom_call_target="tpu_custom_call" | custom-call | flops 3221225472 | bytes 8388608 | tf_op jit(solution)/shard_map/pallas_call | solution.py:291
  315.2 1.7 add.87
  316.9 9.7 %shard_map.121 = f32[4,256,256]{2,1,0:T(8,128)} custom-call(s32[2,4,4]{2,1,0:T(4,128)} %dynamic-slice_bitcast_fusion.2.tab, s32[1]{0:T(128)} %get-tuple-element.31.dests, s32[1]{0:T(128)} %bitcast.1.leaf_ref, f32[16,5,256,256]{3,2,1,0:T(8,128)} %bitcast.38, f32[2,1024,256]{2,1,0:T(8,128)} %pad_maximum_fusion.own_ref, f32[2,512,512]{2,1,0:T(8,128)} %shard_map.120.refs_0_), custom_call_target="tpu_custom_call" | custom-call | flops 3221225472 | bytes 8388608 | tf_op jit(solution)/shard_map/pallas_call | solution.py:291
  326.6 1.7 add.86
  332.0 2.1 maximum_subtract_fusion
  (95 shorter events, 34.5 us)
Async XLA Ops:
  7.2 160.2 %all-gather.3.cloned.1.call-start = ((), (), s32[]{:S(2)}) async-start(), calls=%async_computation | async-start | bytes 22282240 | tf_op jit(solution)/shard_map/all_gather | solution.py:398
  9.1 20.6 %collective-permute-start.2 = (f32[512,256]{1,0:T(8,128)}, f32[512,256]{1,0:T(8,128)}, u32[]{:S(2)}, u32[]{:S(2)}) collective-permute-start(f32[512,256]{1,0:T(8,128)} %slice.44), channel_id=1, source_target_pairs={{0,16},{1,17},{2,18},{3,19},{4,20},{5,21},{6,22},{7,23}} | collective-permute-start | bytes 1572872 | tf_op jit(solution)/shard_map/ppermute | solution.py:394
  17.7 22.3 %collective-permute-start = (f32[1024,256]{1,0:T(8,128)}, f32[1024,256]{1,0:T(8,128)}, u32[]{:S(2)}, u32[]{:S(2)}) collective-permute-start(f32[1024,256]{1,0:T(8,128)} %get-tuple-element.27), channel_id=1, source_target_pairs={{0,4},{4,0},{1,5},{5,1},{2,6},{6,2},{3,7},{7,3},{8,12},{12,8},{9,1... | collective-permute-start | bytes 3145736 | tf_op jit(solution)/shard_map/ppermute | solution.py:389
  19.2 20.7 %collective-permute-start.1 = (f32[1024,256]{1,0:T(8,128)}, f32[1024,256]{1,0:T(8,128)}, u32[]{:S(2)}, u32[]{:S(2)}) collective-permute-start(f32[1024,256]{1,0:T(8,128)} %get-tuple-element.26), channel_id=1, source_target_pairs={{8,24},{9,25},{10,26},{11,27}} | collective-permute-start | bytes 3145736 | tf_op jit(solution)/shard_map/ppermute | solution.py:390
  23.6 19.7 %copy-start.3 = (f32[512,512]{1,0:T(8,128)}, f32[512,512]{1,0:T(8,128)S(1)}, u32[]{:S(2)}) copy-start(f32[512,512]{1,0:T(8,128)S(1)} %get-tuple-element.21.refs_0_) | copy-start | bytes 3145732
  23.6 10.0 %copy-start.18 = (s32[2]{0:T(128)S(1)}, s32[2]{0:T(128)}, u32[]{:S(2)}) copy-start(s32[2]{0:T(128)} %constant.94.clone) | copy-start | bytes 28
  23.6 11.1 %copy-start.17 = (pred[2,4]{1,0:T(4,128)(4,1)S(1)}, pred[2,4]{1,0:T(4,128)(4,1)}, u32[]{:S(2)}) copy-start(pred[2,4]{1,0:T(4,128)(4,1)} %constant.95.clone) | copy-start | bytes 28
  23.6 26.4 %collective-permute-start.4 = (f32[512,512]{1,0:T(8,128)S(1)}, f32[512,512]{1,0:T(8,128)S(1)}, u32[]{:S(2)}, u32[]{:S(2)}) collective-permute-start(f32[512,512]{1,0:T(8,128)S(1)} %get-tuple-element.21.refs_0_), channel_id=1, source_target_pairs={{1,0},{2,1},{3,2},{5,4},{6,5},{7,6},{9,8},{10,9},{11,10},{13,12},{... | collective-permute-start | bytes 3145736 | tf_op jit(solution)/shard_map/ppermute | solution.py:373
  25.0 26.1 %collective-permute-start.5 = (f32[512,512]{1,0:T(8,128)S(1)}, f32[512,512]{1,0:T(8,128)S(1)}, u32[]{:S(2)}, u32[]{:S(2)}) collective-permute-start(f32[512,512]{1,0:T(8,128)S(1)} %get-tuple-element.21.refs_0_), channel_id=1, source_target_pairs={{0,1},{1,2},{2,3},{4,5},{5,6},{6,7},{8,9},{9,10},{10,11},{12,13},{... | collective-permute-start | bytes 3145736 | tf_op jit(solution)/shard_map/ppermute | solution.py:373
  31.6 3.7 %collective-permute-start.3 = (f32[256,256]{1,0:T(8,128)S(1)}, f32[256,256]{1,0:T(8,128)}, u32[]{:S(2)}, u32[]{:S(2)}) collective-permute-start(f32[256,256]{1,0:T(8,128)S(1)} %slice.61), channel_id=1, source_target_pairs={{0,8},{16,24},{1,9},{17,25},{2,10},{18,26},{3,11},{19,27},{4,12},{... | collective-permute-start | bytes 786440 | tf_op jit(solution)/shard_map/ppermute | solution.py:395
  44.4 11.5 %copy-start.15 = (s32[2,2,4,4]{3,2,1,0:T(4,128)S(1)}, s32[2,2,4,4]{3,2,1,0:T(4,128)}, u32[]{:S(2)}) copy-start(s32[2,2,4,4]{3,2,1,0:T(4,128)} %constant.93.clone) | copy-start | bytes 772
  52.2 7.3 %copy-start.16 = (s32[2]{0:T(128)}, s32[2]{0:T(128)S(1)}, u32[]{:S(2)}) copy-start(s32[2]{0:T(128)S(1)} %and_select_fusion.order) | copy-start | bytes 28
  167.4 40.5 %collective-permute-start.6 = (f32[512,512]{1,0:T(8,128)}, f32[512,512]{1,0:T(8,128)S(1)}, u32[]{:S(2)}, u32[]{:S(2)}) collective-permute-start(f32[512,512]{1,0:T(8,128)} %shard_map.104.refs_1_), channel_id=1, source_target_pairs={{0,1},{1,2},{2,3},{4,5},{5,6},{6,7},{8,9},{9,10},{10,11},{12,13},{... | collective-permute-start | bytes 3145736 | tf_op jit(solution)/shard_map/ppermute | solution.py:373
  170.8 41.4 %collective-permute-start.7 = (f32[512,512]{1,0:T(8,128)}, f32[512,512]{1,0:T(8,128)S(1)}, u32[]{:S(2)}, u32[]{:S(2)}) collective-permute-start(f32[512,512]{1,0:T(8,128)} %shard_map.104.refs_1_), channel_id=1, source_target_pairs={{1,0},{2,1},{3,2},{5,4},{6,5},{7,6},{9,8},{10,9},{11,10},{13,12},{... | collective-permute-start | bytes 3145736 | tf_op jit(solution)/shard_map/ppermute | solution.py:373
  179.3 41.7 %collective-permute-start.11 = (f32[4,256,256]{2,1,0:T(8,128)}, f32[4,256,256]{2,1,0:T(8,128)}, u32[]{:S(2)}, u32[]{:S(2)}) collective-permute-start(f32[4,256,256]{2,1,0:T(8,128)} %shard_map.105.refs_1_.refs_0_), channel_id=1, source_target_pairs={{0,4},{4,0},{1,5},{5,1},{2,6},{6,2},{3,7},{7,3},{8,12},{12,8},{9,1... | collective-permute-start | bytes 3145736 | tf_op jit(solution)/shard_map/ppermute | solution.py:353
  183.4 29.8 %collective-permute-start.8 = (f32[512,512]{1,0:T(8,128)}, f32[512,512]{1,0:T(8,128)}, u32[]{:S(2)}, u32[]{:S(2)}) collective-permute-start(f32[512,512]{1,0:T(8,128)} %shard_map.106.refs_2_), channel_id=1, source_target_pairs={{1,2},{2,3},{5,6},{6,7},{9,10},{10,11},{13,14},{14,15},{17,18},{18... | collective-permute-start | bytes 3145736 | tf_op jit(solution)/shard_map/ppermute | solution.py:373
  185.1 34.3 %collective-permute-start.9 = (f32[512,512]{1,0:T(8,128)}, f32[512,512]{1,0:T(8,128)S(1)}, u32[]{:S(2)}, u32[]{:S(2)}) collective-permute-start(f32[512,512]{1,0:T(8,128)} %shard_map.107.refs_3_), channel_id=1, source_target_pairs={{1,0},{2,1},{5,4},{6,5},{9,8},{10,9},{13,12},{14,13},{17,16},{18,1... | collective-permute-start | bytes 3145736 | tf_op jit(solution)/shard_map/ppermute | solution.py:373
  207.9 4.3 %copy-start.8 = (f32[512,512]{1,0:T(8,128)}, f32[512,512]{1,0:T(8,128)S(1)}, u32[]{:S(2)}) copy-start(f32[512,512]{1,0:T(8,128)S(1)} %collective-permute-done.6.refs_0_) | copy-start | bytes 3145732
  207.9 47.2 %collective-permute-start.12 = (f32[4,256,512]{2,1,0:T(8,128)}, f32[4,256,512]{2,1,0:T(8,128)}, u32[]{:S(2)}, u32[]{:S(2)}) collective-permute-start(f32[4,256,512]{2,1,0:T(8,128)} %get-tuple-element.6.refs_1_), channel_id=1, source_target_pairs={{0,4},{4,0},{1,5},{5,1},{2,6},{6,2},{3,7},{7,3},{8,12},{12,8},{9,1... | collective-permute-start | bytes 6291464 | tf_op jit(solution)/shard_map/ppermute | solution.py:353
  212.2 46.3 %collective-permute-start.10 = (f32[512,512]{1,0:T(8,128)}, f32[512,512]{1,0:T(8,128)S(1)}, u32[]{:S(2)}, u32[]{:S(2)}) collective-permute-start(f32[512,512]{1,0:T(8,128)} %shard_map.109.refs_4_), channel_id=1, source_target_pairs={{1,2},{2,3},{5,6},{6,7},{9,10},{10,11},{13,14},{14,15},{17,18},{18... | collective-permute-start | bytes 3145736 | tf_op jit(solution)/shard_map/ppermute | solution.py:373
  213.3 46.9 %collective-permute-start.13 = (f32[512,512]{1,0:T(8,128)}, f32[512,512]{1,0:T(8,128)S(1)}, u32[]{:S(2)}, u32[]{:S(2)}) collective-permute-start(f32[512,512]{1,0:T(8,128)} %shard_map.110.refs_5_), channel_id=1, source_target_pairs={{1,0},{2,1},{5,4},{6,5},{9,8},{10,9},{13,12},{14,13},{17,16},{18,1... | collective-permute-start | bytes 3145736 | tf_op jit(solution)/shard_map/ppermute | solution.py:373
  219.4 55.0 %collective-permute-start.14 = (f32[512,512]{1,0:T(8,128)}, f32[512,512]{1,0:T(8,128)}, u32[]{:S(2)}, u32[]{:S(2)}) collective-permute-start(f32[512,512]{1,0:T(8,128)} %shard_map.111.refs_6_), channel_id=1, source_target_pairs={{2,3},{6,7},{10,11},{14,15},{18,19},{22,23},{26,27},{30,31}} | collective-permute-start | bytes 3145736 | tf_op jit(solution)/shard_map/ppermute | solution.py:373
  221.0 53.8 %collective-permute-start.15 = (f32[512,512]{1,0:T(8,128)}, f32[512,512]{1,0:T(8,128)S(1)}, u32[]{:S(2)}, u32[]{:S(2)}) collective-permute-start(f32[512,512]{1,0:T(8,128)} %shard_map.112.refs_7_), channel_id=1, source_target_pairs={{1,0},{5,4},{9,8},{13,12},{17,16},{21,20},{25,24},{29,28}} | collective-permute-start | bytes 3145736 | tf_op jit(solution)/shard_map/ppermute | solution.py:373
  236.7 18.4 %copy-start.9 = (f32[4,256,512]{2,1,0:T(8,128)S(1)}, f32[4,256,512]{2,1,0:T(8,128)}, u32[]{:S(2)}) copy-start(f32[4,256,512]{2,1,0:T(8,128)} %shard_map.113.refs_0_) | copy-start | bytes 6291460
  259.5 15.4 %collective-permute-start.16 = (f32[512,512]{1,0:T(8,128)}, f32[512,512]{1,0:T(8,128)S(1)}, u32[]{:S(2)}, u32[]{:S(2)}) collective-permute-start(f32[512,512]{1,0:T(8,128)} %shard_map.114.refs_8_), channel_id=1, source_target_pairs={{2,3},{6,7},{10,11},{14,15},{18,19},{22,23},{26,27},{30,31}} | collective-permute-start | bytes 3145736 | tf_op jit(solution)/shard_map/ppermute | solution.py:373
  261.2 27.0 %collective-permute-start.17 = (f32[512,512]{1,0:T(8,128)}, f32[512,512]{1,0:T(8,128)S(1)}, u32[]{:S(2)}, u32[]{:S(2)}) collective-permute-start(f32[512,512]{1,0:T(8,128)} %shard_map.115.refs_9_), channel_id=1, source_target_pairs={{1,0},{5,4},{9,8},{13,12},{17,16},{21,20},{25,24},{29,28}} | collective-permute-start | bytes 3145736 | tf_op jit(solution)/shard_map/ppermute | solution.py:373
  262.5 26.5 %collective-permute-start.18 = (f32[4,256,256]{2,1,0:T(8,128)}, f32[4,256,256]{2,1,0:T(8,128)}, u32[]{:S(2)}, u32[]{:S(2)}) collective-permute-start(f32[4,256,256]{2,1,0:T(8,128)} %shard_map.117.refs_11_), channel_id=1, source_target_pairs={{0,4},{4,0},{1,5},{5,1},{2,6},{6,2},{3,7},{7,3},{8,12},{12,8},{9,1... | collective-permute-start | bytes 3145736 | tf_op jit(solution)/shard_map/ppermute | solution.py:353
  274.4 55.4 %collective-permute-start.19 = (f32[1,512,512]{2,1,0:T(8,128)}, f32[1,512,512]{2,1,0:T(8,128)S(1)}, u32[]{:S(2)}, u32[]{:S(2)}) collective-permute-start(f32[1,512,512]{2,1,0:T(8,128)} %shard_map.118.refs_15_), channel_id=1, source_target_pairs={{0,4},{4,0},{1,5},{5,1},{2,6},{6,2},{3,7},{7,3},{8,12},{12,8},{9,1... | collective-permute-start | bytes 3145736 | tf_op jit(solution)/shard_map/ppermute | solution.py:353
  274.9 14.1 %copy-start.10 = (f32[512,512]{1,0:T(8,128)}, f32[512,512]{1,0:T(8,128)S(1)}, u32[]{:S(2)}) copy-start(f32[512,512]{1,0:T(8,128)S(1)} %collective-permute-done.15.refs_11_) | copy-start | bytes 3145732
  274.9 14.1 %copy-start.11 = (f32[512,512]{1,0:T(8,128)}, f32[512,512]{1,0:T(8,128)S(1)}, u32[]{:S(2)}) copy-start(f32[512,512]{1,0:T(8,128)S(1)} %collective-permute-done.16.refs_12_) | copy-start | bytes 3145732
  295.2 34.6 %collective-permute-start.20 = (f32[1,512,512]{2,1,0:T(8,128)}, f32[1,512,512]{2,1,0:T(8,128)S(1)}, u32[]{:S(2)}, u32[]{:S(2)}) collective-permute-start(f32[1,512,512]{2,1,0:T(8,128)} %shard_map.119.refs_15_), channel_id=1, source_target_pairs={{0,4},{4,0},{1,5},{5,1},{2,6},{6,2},{3,7},{7,3},{8,12},{12,8},{9,1... | collective-permute-start | bytes 3145736 | tf_op jit(solution)/shard_map/ppermute | solution.py:353
  329.8 2.2 copy-start.14
  (9 other events, 10.1 us)
Sparse Core Ops, SparseCore 0:
  52.3 115.0 all-gather.2

commit v8 on v7

--- a/solution.py
+++ b/solution.py
@@ -70,7 +70,7 @@
                 slot = entry // (lay.leaves + 1)
                 position = entry - slot * (lay.leaves + 1)
                 pltpu.make_async_copy(
-                    gathered.at[slot * lay.cols + col, position, :, lanes],
+                    gathered.at[col * lay.leaves + slot, position, :, lanes],
                     t.at[k, s, pl.ds(j * lay.part, lay.part)],
                     sems.at[k, s],
                 ).start()
@@ -257,7 +257,7 @@
                         slot = entry // (parts + 1)
                         position = entry - slot * (parts + 1)
                         pltpu.make_async_copy(
-                            g_ref.at[slot * lay.cols + col, position],
+                            g_ref.at[col * lay.leaves + slot, position],
                             held.at[a, i, s, pl.ds(j * part, part)],
                             sems.at[a, i, s],
                         ).start()
@@ -395,7 +395,7 @@
     other = lax.ppermute(both[part:], "leaf", [(chip, chip + 1) for chip in range(0, leaves, 2)])
     extra = jnp.where(me_leaf % 2 == 0, both[:part], other)
     held = jnp.concatenate([whole.reshape(parts, part, width), extra[None]], axis=0)
-    gathered = lax.all_gather(after(held, pieces[1, 0], pieces[-1, 0]), ("leaf", "col"), axis=0, tiled=False)
+    gathered = lax.all_gather(after(held, pieces[1, 0], pieces[-1, 0]), ("col", "leaf"), axis=0, tiled=False)
     own = jnp.stack([lower, swapped])
     hop(1, 0, gathered)
 
@@ -421,9 +421,10 @@
         if step + 1 < cols - 1:
             hop(0, step + 1, *sent)
     kept = own_panel_product(lay, pattern[0], table, order, gathered, turned, early_in)
-    late = top_product(lay, table, order[: rows - 1], *top_args, 1, [kept])
+    tops = top_product(lay, table, order[rows - 1 :], *top_args, 0, [kept])
+    late = top_product(lay, table, order[: rows - 1], *top_args, 1, tops)
     sigma_panel = -sum(sent_in, kept).reshape(-1, normed.shape[1])
-    late = [after(value, sigma_panel) for value in late]
+    late = [after(value, *sent_in) for value in late]
     late_in = send_over_rows(late)
     for step in range(middle, cols - 1):
         hop(1, step, sigma_panel)
@@ -438,7 +439,7 @@
         tokens = term + late_in
     mine = diagonal_product(info, (rows - 1) * each, each, pieces, sigma_panel, term)
     rest = diag_inverse[0] - mine.reshape(diag_inverse.shape[1:])
-    tops = [top_product(lay, table, order[rows - 1 :], *top_args, chunk, [mine])[0] for chunk in range(chunks)]
+    tops = [*tops, *top_product(lay, table, order[rows - 1 :], *top_args, 1, [mine])]
     update = []
     for block in range(each):
         total = 0.0

time: 345 us -> 344 us (level)
    all_gather x1, waiting for transfers between devices: 108 us -> 101 us  [per_device(): lax.all_gather(after(held, pieces[1, 0], pieces[-1, 0]), ('col', 'leaf'),...]
    ppermute x1, waiting for transfers between devices: 3.65 us -> 8.96 us  [per_device(): lax.ppermute(upper, 'row', [(r, rows - 1 - r) for r in range(rows)])]
    ppermute x5, waiting for transfers between devices: 14.8 us -> 18.9 us  [send_over_rows(): lax.ppermute(value, 'row', [(i, (i + a + 1) % rows) for i in range(rows)])]
  transfers between devices with their start and end apart: 22 -> 22, of which waited for: 8 -> 7; matrix products, arithmetic and copies ran while one was open for 8% -> 8% of each run, Pallas kernels for 26% -> 26%
where the time goes in v8:
time: 344 us; the launch traced here: 343 us
  waiting for transfers between devices  153 us (44%)
  Pallas kernels  87.6 us (25%)
  starting transfers between devices  43.7 us (13%)
  other arithmetic  21.5 us (6%)
  between operations  19.4 us (6%)
  local copies, waits for them, and re-layouts  17 us (5%)
    all_gather x1, waiting for transfers between devices, per_device(): lax.all_gather(after(held, pieces[1, 0], pieces[-1, 0]), ('col', 'leaf'),...  101 us
    pallas_call x4, Pallas kernels, top_product(): pl.pallas_call(functools.partial(top_kernel, lay, chunks, chunk, len(toke...  31.2 us
    ppermute x12, waiting for transfers between devices, hop(): lax.ppermute(pieces[-way * step, run], 'col', [(i, i + way) for i in at])  24.3 us
    pallas_call x1, Pallas kernels, panel_product(): pl.pallas_call(functools.partial(panel_kernel, lay, rows, len(tokens)), o...  21.5 us
    ppermute x12, starting transfers between devices, hop(): lax.ppermute(pieces[-way * step, run], 'col', [(i, i + way) for i in at])  20.8 us
    pallas_call x3, Pallas kernels, diagonal_product(): pl.pallas_call(functools.partial(diagonal_kernel, tuple(pieces), first, l...  20.8 us
    ppermute x5, waiting for transfers between devices, send_over_rows(): lax.ppermute(value, 'row', [(i, (i + a + 1) % rows) for i in range(rows)])  18.9 us
    pallas_call x1, Pallas kernels, own_panel_product(): pl.pallas_call(functools.partial(own_panel_kernel, lay, rows, len(tokens)...  14.2 us
  transfers between devices with their start and end apart: 22, of which 7 were waited for; matrix products, arithmetic and copies ran while one was open for 8% of the time, Pallas kernels for 26%

profile of v8, /device:TPU:0, one launch (start us, length us, event | category | flops | bytes accessed | tf_op | source)
XLA Modules:
  0.0 342.5 jit_solution(808442269500849413)
XLA Ops:
  7.2 1.9 slice.44
  9.1 5.7 %collective-permute-start.2 = (f32[512,256]{1,0:T(8,128)}, f32[512,256]{1,0:T(8,128)}, u32[]{:S(2)}, u32[]{:S(2)}) collective-permute-start(f32[512,256]{1,0:T(8,128)} %slice.44), channel_id=1, source_target_pairs={{0,16},{1,17},{2,18},{3,19},{4,20},{5,21},{6,22},{7,23}} | collective-permute-start | bytes 1572872 | tf_op jit(solution)/shard_map/ppermute | solution.py:394
  14.8 3.0 fusion.3
  17.8 1.6 collective-permute-start.1
  20.9 2.7 dynamic-slice_bitcast_fusion
  23.6 3.7 %collective-permute-start.5 = (f32[512,512]{1,0:T(8,128)S(1)}, f32[512,512]{1,0:T(8,128)S(1)}, u32[]{:S(2)}, u32[]{:S(2)}) collective-permute-start(f32[512,512]{1,0:T(8,128)S(1)} %get-tuple-element.21.refs_0_), channel_id=1, source_target_pairs={{0,1},{1,2},{2,3},{4,5},{5,6},{6,7},{8,9},{9,10},{10,11},{12,13},{... | collective-permute-start | bytes 3145736 | tf_op jit(solution)/shard_map/ppermute | solution.py:373
  30.6 2.0 collective-permute-start.3
  35.4 9.0 %collective-permute-done = f32[1024,256]{1,0:T(8,128)} collective-permute-done((f32[1024,256]{1,0:T(8,128)}, f32[1024,256]{1,0:T(8,128)}, u32[]{:S(2)}, u32[]{:S(2)}) %collective-permute-start) | collective-permute-done | bytes 1048608 | tf_op jit(solution)/shard_map/ppermute | solution.py:389
  44.3 3.3 slice_bitcast_fusion
  48.8 3.2 collective-permute-done.4.refs_1_.refs_0_
  57.4 3.0 pad_maximum_fusion.own_ref
  60.4 101.1 %all-gather.3.cloned.1.call-done = f32[80,256,256]{2,1,0:T(8,128)} async-done(((f32[5,256,256]{2,1,0:T(8,128)}), f32[80,256,256]{2,1,0:T(8,128)}) %all-gather.3.cloned.1.call-update) | async-done | bytes 20971536 | tf_op jit(solution)/shard_map/all_gather | solution.py:398
  162.8 4.6 %collective-permute-start.7 = (f32[512,512]{1,0:T(8,128)}, f32[512,512]{1,0:T(8,128)S(1)}, u32[]{:S(2)}, u32[]{:S(2)}) collective-permute-start(f32[512,512]{1,0:T(8,128)} %shard_map.108.refs_1_), channel_id=1, source_target_pairs={{0,1},{1,2},{2,3},{4,5},{5,6},{6,7},{8,9},{9,10},{10,11},{12,13},{... | collective-permute-start | bytes 3145736 | tf_op jit(solution)/shard_map/ppermute | solution.py:373
  167.4 7.2 %shard_map.104.refs_0_.refs_1_ = f32[4,256,256]{2,1,0:T(8,128)} custom-call(s32[2,4,4]{2,1,0:T(4,128)} %dynamic-slice_bitcast_fusion.2.tab, s32[1]{0:T(128)} %get-tuple-element.30.dests, s32[1]{0:T(128)} %bitcast.1.leaf_ref, f32[16,5,256,256]{3,2,1,0:T(8,128)} %bitcast.33, f32[2,1024,256]{2,1,0:T(8,128)} %pad_maximum_fusion.own_ref, s32[5]{0:T(128)} %pad_add_fusion.refs_0_.info), custom_call_target="tpu_custom_call" | custom-call | flops 3221225472 | bytes 8388608 | tf_op jit(solution)/shard_map/pallas_call | solution.py:291
  174.6 4.1 %collective-permute-start.6 = (f32[4,256,256]{2,1,0:T(8,128)}, f32[4,256,256]{2,1,0:T(8,128)}, u32[]{:S(2)}, u32[]{:S(2)}) collective-permute-start(f32[4,256,256]{2,1,0:T(8,128)} %shard_map.104.refs_0_.refs_1_), channel_id=1, source_target_pairs={{0,4},{4,0},{1,5},{5,1},{2,6},{6,2},{3,7},{7,3},{8,12},{12,8},{9,1... | collective-permute-start | bytes 3145736 | tf_op jit(solution)/shard_map/ppermute | solution.py:353
  178.7 1.6 collective-permute-start.9
  181.6 21.5 %shard_map.105 = (f32[4,256,512]{2,1,0:T(8,128)}, bf16[2,512,1024]{2,1,0:T(8,128)(2,1)}, bf16[2,512,1024]{2,1,0:T(8,128)(2,1)}) custom-call(s32[16]{0:T(128)} %bitcast.49, s32[2,4,4]{2,1,0:T(4,128)} %dynamic-slice_bitcast_fusion.2.tab, s32[2]{0:T(128)} %copy-done.16, f32[16,5,256,256]{3,2,1,0:T(8,128)} %bitcast.34, f32[2048,512]{1,0:T(8,128)} %bitcast.48, ...), custom_call_target="tpu_custom_call" | custom-call | flops 19327352832 | bytes 16777216 | tf_op jit(solution)/shard_map/pallas_call | solution.py:197
  203.1 4.3 %collective-permute-start.12 = (f32[4,256,512]{2,1,0:T(8,128)}, f32[4,256,512]{2,1,0:T(8,128)}, u32[]{:S(2)}, u32[]{:S(2)}) collective-permute-start(f32[4,256,512]{2,1,0:T(8,128)} %get-tuple-element.8.refs_1_), channel_id=1, source_target_pairs={{0,4},{4,0},{1,5},{5,1},{2,6},{6,2},{3,7},{7,3},{8,12},{12,8},{9,1... | collective-permute-start | bytes 6291464 | tf_op jit(solution)/shard_map/ppermute | solution.py:353
  209.7 1.8 collective-permute-done.10.refs_0_
  213.7 14.2 %shard_map.106.refs_0_ = f32[4,256,512]{2,1,0:T(8,128)} custom-call(s32[16]{0:T(128)} %bitcast.50, s32[2,4,4]{2,1,0:T(4,128)} %dynamic-slice_bitcast_fusion.2.tab, s32[2]{0:T(128)} %copy-done.16, f32[16,5,256,256]{3,2,1,0:T(8,128)} %bitcast.35, bf16[2,512,1024]{2,1,0:T(8,128)(2,1)} %get-tuple-element.6.turned_high, ...), custom_call_target="tpu_custom_call" | custom-call | flops 25769803776 | bytes 8388608 | tf_op jit(solution)/shard_map/pallas_call | solution.py:218
  227.9 9.7 %shard_map.107.refs_0_ = f32[4,256,256]{2,1,0:T(8,128)} custom-call(s32[2,4,4]{2,1,0:T(4,128)} %dynamic-slice_bitcast_fusion.2.tab, s32[1]{0:T(128)} %get-tuple-element.31.dests, s32[1]{0:T(128)} %bitcast.1.leaf_ref, f32[16,5,256,256]{3,2,1,0:T(8,128)} %bitcast.36, f32[2,1024,256]{2,1,0:T(8,128)} %pad_maximum_fusion.own_ref, f32[4,256,512]{2,1,0:T(8,128)} %shard_map.106.refs_0_), custom_call_target="tpu_custom_call" | custom-call | flops 3221225472 | bytes 8388608 | tf_op jit(solution)/shard_map/pallas_call | solution.py:291
  237.6 4.5 %shard_map.117.refs_0_ = f32[4,256,256]{2,1,0:T(8,128)} custom-call(s32[2,4,4]{2,1,0:T(4,128)} %dynamic-slice_bitcast_fusion.2.tab, s32[1]{0:T(128)} %get-tuple-element.30.dests, s32[1]{0:T(128)} %bitcast.1.leaf_ref, f32[16,5,256,256]{3,2,1,0:T(8,128)} %bitcast.37, f32[2,1024,256]{2,1,0:T(8,128)} %pad_maximum_fusion.own_ref, f32[4,256,256]{2,1,0:T(8,128)} %shard_map.107.refs_0_), custom_call_target="tpu_custom_call" | custom-call | flops 3221225472 | bytes 8388608 | tf_op jit(solution)/shard_map/pallas_call | solution.py:291
  242.1 11.6 %collective-permute-done.12.refs_1_ = f32[4,256,512]{2,1,0:T(8,128)} collective-permute-done((f32[4,256,512]{2,1,0:T(8,128)}, f32[4,256,512]{2,1,0:T(8,128)}, u32[]{:S(2)}, u32[]{:S(2)}) %collective-permute-start.12) | collective-permute-done | bytes 2097184 | tf_op jit(solution)/shard_map/ppermute | solution.py:353
  253.7 3.4 add_negate_fusion
  262.0 1.8 collective-permute-start.18
  263.8 6.1 %shard_map.119.refs_15_ = f32[1,512,512]{2,1,0:T(8,128)} custom-call(s32[5]{0:T(128)} %pad_add_fusion.refs_0_.info, f32[512,512]{1,0:T(8,128)} %copy-done.3, f32[512,512]{1,0:T(8,128)} %shard_map.108.refs_1_, f32[512,512]{1,0:T(8,128)} %shard_map.109.refs_2_, f32[512,512]{1,0:T(8,128)} %shard_map.110.refs_3_, f32[512,512]{1,0:T(8,128)} %shard_map.111.refs_4_, ...), custom_call_target="tpu_custom_call" | custom-call | flops 1610612736 | bytes 4194304 | tf_op jit(solution)/shard_map/pallas_call | solution.py:329
  270.3 19.2 %collective-permute-done.17.refs_13_ = f32[512,512]{1,0:T(8,128)} collective-permute-done((f32[512,512]{1,0:T(8,128)}, f32[512,512]{1,0:T(8,128)}, u32[]{:S(2)}, u32[]{:S(2)}) %collective-permute-start.17) | collective-permute-done | bytes 1048608 | tf_op jit(solution)/shard_map/ppermute | solution.py:373
  290.5 6.1 %shard_map.120.refs_15_ = f32[1,512,512]{2,1,0:T(8,128)} custom-call(s32[5]{0:T(128)} %pad_add_fusion.refs_0_.info, f32[512,512]{1,0:T(8,128)} %copy-done.3, f32[512,512]{1,0:T(8,128)} %shard_map.108.refs_1_, f32[512,512]{1,0:T(8,128)} %shard_map.109.refs_2_, f32[512,512]{1,0:T(8,128)} %shard_map.110.refs_3_, f32[512,512]{1,0:T(8,128)} %shard_map.111.refs_4_, ...), custom_call_target="tpu_custom_call" | custom-call | flops 1610612736 | bytes 4194304 | tf_op jit(solution)/shard_map/pallas_call | solution.py:329
  303.4 8.5 %shard_map.121.refs_0_ = f32[2,512,512]{2,1,0:T(8,128)} custom-call(s32[5]{0:T(128)} %pad_add_fusion.refs_0_.info, f32[512,512]{1,0:T(8,128)} %copy-done.3, f32[512,512]{1,0:T(8,128)} %shard_map.108.refs_1_, f32[512,512]{1,0:T(8,128)} %shard_map.109.refs_2_, f32[512,512]{1,0:T(8,128)} %shard_map.110.refs_3_, f32[512,512]{1,0:T(8,128)} %shard_map.111.refs_4_, ...), custom_call_target="tpu_custom_call" | custom-call | flops 3221225472 | bytes 6291456 | tf_op jit(solution)/shard_map/pallas_call | solution.py:329
  312.0 9.8 %shard_map.122 = f32[4,256,256]{2,1,0:T(8,128)} custom-call(s32[2,4,4]{2,1,0:T(4,128)} %dynamic-slice_bitcast_fusion.2.tab, s32[1]{0:T(128)} %get-tuple-element.31.dests, s32[1]{0:T(128)} %bitcast.1.leaf_ref, f32[16,5,256,256]{3,2,1,0:T(8,128)} %bitcast.38, f32[2,1024,256]{2,1,0:T(8,128)} %pad_maximum_fusion.own_ref, f32[2,512,512]{2,1,0:T(8,128)} %shard_map.121.refs_0_), custom_call_target="tpu_custom_call" | custom-call | flops 3221225472 | bytes 8388608 | tf_op jit(solution)/shard_map/pallas_call | solution.py:291
  324.7 7.3 %collective-permute-done.20 = f32[1,512,512]{2,1,0:T(8,128)S(1)} collective-permute-done((f32[1,512,512]{2,1,0:T(8,128)}, f32[1,512,512]{2,1,0:T(8,128)S(1)}, u32[]{:S(2)}, u32[]{:S(2)}) %collective-permute-start.20) | collective-permute-done | bytes 1048608 | tf_op jit(solution)/shard_map/ppermute | solution.py:353
  333.6 2.1 maximum_subtract_fusion
  (95 shorter events, 33.5 us)
Async XLA Ops:
  7.2 154.3 %all-gather.3.cloned.1.call-start = ((), (), s32[]{:S(2)}) async-start(), calls=%async_computation | async-start | bytes 22282240 | tf_op jit(solution)/shard_map/all_gather | solution.py:398
  9.1 19.5 %collective-permute-start.2 = (f32[512,256]{1,0:T(8,128)}, f32[512,256]{1,0:T(8,128)}, u32[]{:S(2)}, u32[]{:S(2)}) collective-permute-start(f32[512,256]{1,0:T(8,128)} %slice.44), channel_id=1, source_target_pairs={{0,16},{1,17},{2,18},{3,19},{4,20},{5,21},{6,22},{7,23}} | collective-permute-start | bytes 1572872 | tf_op jit(solution)/shard_map/ppermute | solution.py:394
  17.8 17.6 %collective-permute-start.1 = (f32[1024,256]{1,0:T(8,128)}, f32[1024,256]{1,0:T(8,128)}, u32[]{:S(2)}, u32[]{:S(2)}) collective-permute-start(f32[1024,256]{1,0:T(8,128)} %get-tuple-element.26), channel_id=1, source_target_pairs={{8,24},{9,25},{10,26},{11,27}} | collective-permute-start | bytes 3145736 | tf_op jit(solution)/shard_map/ppermute | solution.py:390
  19.4 24.9 %collective-permute-start = (f32[1024,256]{1,0:T(8,128)}, f32[1024,256]{1,0:T(8,128)}, u32[]{:S(2)}, u32[]{:S(2)}) collective-permute-start(f32[1024,256]{1,0:T(8,128)} %get-tuple-element.27), channel_id=1, source_target_pairs={{0,4},{4,0},{1,5},{5,1},{2,6},{6,2},{3,7},{7,3},{8,12},{12,8},{9,1... | collective-permute-start | bytes 3145736 | tf_op jit(solution)/shard_map/ppermute | solution.py:389
  23.6 24.0 %copy-start.3 = (f32[512,512]{1,0:T(8,128)}, f32[512,512]{1,0:T(8,128)S(1)}, u32[]{:S(2)}) copy-start(f32[512,512]{1,0:T(8,128)S(1)} %get-tuple-element.21.refs_0_) | copy-start | bytes 3145732
  23.6 9.0 %copy-start.18 = (s32[2]{0:T(128)S(1)}, s32[2]{0:T(128)}, u32[]{:S(2)}) copy-start(s32[2]{0:T(128)} %constant.94.clone) | copy-start | bytes 28
  23.6 10.1 %copy-start.17 = (pred[2,4]{1,0:T(4,128)(4,1)S(1)}, pred[2,4]{1,0:T(4,128)(4,1)}, u32[]{:S(2)}) copy-start(pred[2,4]{1,0:T(4,128)(4,1)} %constant.95.clone) | copy-start | bytes 28
  23.6 25.2 %collective-permute-start.5 = (f32[512,512]{1,0:T(8,128)S(1)}, f32[512,512]{1,0:T(8,128)S(1)}, u32[]{:S(2)}, u32[]{:S(2)}) collective-permute-start(f32[512,512]{1,0:T(8,128)S(1)} %get-tuple-element.21.refs_0_), channel_id=1, source_target_pairs={{0,1},{1,2},{2,3},{4,5},{5,6},{6,7},{8,9},{9,10},{10,11},{12,13},{... | collective-permute-start | bytes 3145736 | tf_op jit(solution)/shard_map/ppermute | solution.py:373
  27.3 24.7 %collective-permute-start.4 = (f32[512,512]{1,0:T(8,128)S(1)}, f32[512,512]{1,0:T(8,128)S(1)}, u32[]{:S(2)}, u32[]{:S(2)}) collective-permute-start(f32[512,512]{1,0:T(8,128)S(1)} %get-tuple-element.21.refs_0_), channel_id=1, source_target_pairs={{1,0},{2,1},{3,2},{5,4},{6,5},{7,6},{9,8},{10,9},{11,10},{13,12},{... | collective-permute-start | bytes 3145736 | tf_op jit(solution)/shard_map/ppermute | solution.py:373
  30.6 3.8 %collective-permute-start.3 = (f32[256,256]{1,0:T(8,128)S(1)}, f32[256,256]{1,0:T(8,128)}, u32[]{:S(2)}, u32[]{:S(2)}) collective-permute-start(f32[256,256]{1,0:T(8,128)S(1)} %slice.61), channel_id=1, source_target_pairs={{0,8},{16,24},{1,9},{17,25},{2,10},{18,26},{3,11},{19,27},{4,12},{... | collective-permute-start | bytes 786440 | tf_op jit(solution)/shard_map/ppermute | solution.py:395
  48.8 8.0 %copy-start.15 = (s32[2,2,4,4]{3,2,1,0:T(4,128)S(1)}, s32[2,2,4,4]{3,2,1,0:T(4,128)}, u32[]{:S(2)}) copy-start(s32[2,2,4,4]{3,2,1,0:T(4,128)} %constant.93.clone) | copy-start | bytes 772
  161.5 45.9 %collective-permute-start.8 = (f32[512,512]{1,0:T(8,128)}, f32[512,512]{1,0:T(8,128)S(1)}, u32[]{:S(2)}, u32[]{:S(2)}) collective-permute-start(f32[512,512]{1,0:T(8,128)} %shard_map.108.refs_1_), channel_id=1, source_target_pairs={{1,0},{2,1},{3,2},{5,4},{6,5},{7,6},{9,8},{10,9},{11,10},{13,12},{... | collective-permute-start | bytes 3145736 | tf_op jit(solution)/shard_map/ppermute | solution.py:373
  162.8 40.3 %collective-permute-start.7 = (f32[512,512]{1,0:T(8,128)}, f32[512,512]{1,0:T(8,128)S(1)}, u32[]{:S(2)}, u32[]{:S(2)}) collective-permute-start(f32[512,512]{1,0:T(8,128)} %shard_map.108.refs_1_), channel_id=1, source_target_pairs={{0,1},{1,2},{2,3},{4,5},{5,6},{6,7},{8,9},{9,10},{10,11},{12,13},{... | collective-permute-start | bytes 3145736 | tf_op jit(solution)/shard_map/ppermute | solution.py:373
  174.6 37.6 %collective-permute-start.6 = (f32[4,256,256]{2,1,0:T(8,128)}, f32[4,256,256]{2,1,0:T(8,128)}, u32[]{:S(2)}, u32[]{:S(2)}) collective-permute-start(f32[4,256,256]{2,1,0:T(8,128)} %shard_map.104.refs_0_.refs_1_), channel_id=1, source_target_pairs={{0,4},{4,0},{1,5},{5,1},{2,6},{6,2},{3,7},{7,3},{8,12},{12,8},{9,1... | collective-permute-start | bytes 3145736 | tf_op jit(solution)/shard_map/ppermute | solution.py:353
  178.7 29.7 %collective-permute-start.9 = (f32[512,512]{1,0:T(8,128)}, f32[512,512]{1,0:T(8,128)}, u32[]{:S(2)}, u32[]{:S(2)}) collective-permute-start(f32[512,512]{1,0:T(8,128)} %shard_map.109.refs_2_), channel_id=1, source_target_pairs={{1,2},{2,3},{5,6},{6,7},{9,10},{10,11},{13,14},{14,15},{17,18},{18... | collective-permute-start | bytes 3145736 | tf_op jit(solution)/shard_map/ppermute | solution.py:373
  180.3 31.2 %collective-permute-start.10 = (f32[512,512]{1,0:T(8,128)}, f32[512,512]{1,0:T(8,128)}, u32[]{:S(2)}, u32[]{:S(2)}) collective-permute-start(f32[512,512]{1,0:T(8,128)} %shard_map.110.refs_3_), channel_id=1, source_target_pairs={{1,0},{2,1},{5,4},{6,5},{9,8},{10,9},{13,12},{14,13},{17,16},{18,1... | collective-permute-start | bytes 3145736 | tf_op jit(solution)/shard_map/ppermute | solution.py:373
  203.1 50.6 %collective-permute-start.12 = (f32[4,256,512]{2,1,0:T(8,128)}, f32[4,256,512]{2,1,0:T(8,128)}, u32[]{:S(2)}, u32[]{:S(2)}) collective-permute-start(f32[4,256,512]{2,1,0:T(8,128)} %get-tuple-element.8.refs_1_), channel_id=1, source_target_pairs={{0,4},{4,0},{1,5},{5,1},{2,6},{6,2},{3,7},{7,3},{8,12},{12,8},{9,1... | collective-permute-start | bytes 6291464 | tf_op jit(solution)/shard_map/ppermute | solution.py:353
  207.4 49.7 %collective-permute-start.11 = (f32[512,512]{1,0:T(8,128)}, f32[512,512]{1,0:T(8,128)S(1)}, u32[]{:S(2)}, u32[]{:S(2)}) collective-permute-start(f32[512,512]{1,0:T(8,128)} %shard_map.111.refs_4_), channel_id=1, source_target_pairs={{1,2},{2,3},{5,6},{6,7},{9,10},{10,11},{13,14},{14,15},{17,18},{18... | collective-permute-start | bytes 3145736 | tf_op jit(solution)/shard_map/ppermute | solution.py:373
  208.4 51.4 %collective-permute-start.13 = (f32[512,512]{1,0:T(8,128)}, f32[512,512]{1,0:T(8,128)S(1)}, u32[]{:S(2)}, u32[]{:S(2)}) collective-permute-start(f32[512,512]{1,0:T(8,128)} %shard_map.112.refs_5_), channel_id=1, source_target_pairs={{1,0},{2,1},{5,4},{6,5},{9,8},{10,9},{13,12},{14,13},{17,16},{18,1... | collective-permute-start | bytes 3145736 | tf_op jit(solution)/shard_map/ppermute | solution.py:373
  211.5 58.5 %collective-permute-start.14 = (f32[512,512]{1,0:T(8,128)}, f32[512,512]{1,0:T(8,128)S(1)}, u32[]{:S(2)}, u32[]{:S(2)}) collective-permute-start(f32[512,512]{1,0:T(8,128)} %shard_map.113.refs_6_), channel_id=1, source_target_pairs={{2,3},{6,7},{10,11},{14,15},{18,19},{22,23},{26,27},{30,31}} | collective-permute-start | bytes 3145736 | tf_op jit(solution)/shard_map/ppermute | solution.py:373
  212.2 58.1 %collective-permute-start.15 = (f32[512,512]{1,0:T(8,128)}, f32[512,512]{1,0:T(8,128)}, u32[]{:S(2)}, u32[]{:S(2)}) collective-permute-start(f32[512,512]{1,0:T(8,128)} %shard_map.114.refs_7_), channel_id=1, source_target_pairs={{1,0},{5,4},{9,8},{13,12},{17,16},{21,20},{25,24},{29,28}} | collective-permute-start | bytes 3145736 | tf_op jit(solution)/shard_map/ppermute | solution.py:373
  237.6 16.1 %copy-start.9 = (f32[4,256,512]{2,1,0:T(8,128)S(1)}, f32[4,256,512]{2,1,0:T(8,128)}, u32[]{:S(2)}) copy-start(f32[4,256,512]{2,1,0:T(8,128)} %shard_map.106.refs_0_) | copy-start | bytes 6291460
  258.1 12.2 %collective-permute-start.16 = (f32[512,512]{1,0:T(8,128)}, f32[512,512]{1,0:T(8,128)}, u32[]{:S(2)}, u32[]{:S(2)}) collective-permute-start(f32[512,512]{1,0:T(8,128)} %shard_map.115.refs_8_), channel_id=1, source_target_pairs={{2,3},{6,7},{10,11},{14,15},{18,19},{22,23},{26,27},{30,31}} | collective-permute-start | bytes 3145736 | tf_op jit(solution)/shard_map/ppermute | solution.py:373
  260.7 28.9 %collective-permute-start.17 = (f32[512,512]{1,0:T(8,128)}, f32[512,512]{1,0:T(8,128)}, u32[]{:S(2)}, u32[]{:S(2)}) collective-permute-start(f32[512,512]{1,0:T(8,128)} %shard_map.116.refs_9_), channel_id=1, source_target_pairs={{1,0},{5,4},{9,8},{13,12},{17,16},{21,20},{25,24},{29,28}} | collective-permute-start | bytes 3145736 | tf_op jit(solution)/shard_map/ppermute | solution.py:373
  262.0 27.6 %collective-permute-start.18 = (f32[4,256,256]{2,1,0:T(8,128)}, f32[4,256,256]{2,1,0:T(8,128)S(1)}, u32[]{:S(2)}, u32[]{:S(2)}) collective-permute-start(f32[4,256,256]{2,1,0:T(8,128)} %shard_map.118.refs_11_), channel_id=1, source_target_pairs={{0,4},{4,0},{1,5},{5,1},{2,6},{6,2},{3,7},{7,3},{8,12},{12,8},{9,1... | collective-permute-start | bytes 3145736 | tf_op jit(solution)/shard_map/ppermute | solution.py:353
  269.9 32.1 %copy-start.8 = (f32[4,256,256]{2,1,0:T(8,128)S(1)}, f32[4,256,256]{2,1,0:T(8,128)}, u32[]{:S(2)}) copy-start(f32[4,256,256]{2,1,0:T(8,128)} %shard_map.107.refs_0_) | copy-start | bytes 3145732
  269.9 19.6 %copy-start.10 = (f32[512,512]{1,0:T(8,128)}, f32[512,512]{1,0:T(8,128)S(1)}, u32[]{:S(2)}) copy-start(f32[512,512]{1,0:T(8,128)S(1)} %collective-permute-done.14.refs_10_) | copy-start | bytes 3145732
  270.0 54.7 %collective-permute-start.19 = (f32[1,512,512]{2,1,0:T(8,128)}, f32[1,512,512]{2,1,0:T(8,128)}, u32[]{:S(2)}, u32[]{:S(2)}) collective-permute-start(f32[1,512,512]{2,1,0:T(8,128)} %shard_map.119.refs_15_), channel_id=1, source_target_pairs={{0,4},{4,0},{1,5},{5,1},{2,6},{6,2},{3,7},{7,3},{8,12},{12,8},{9,1... | collective-permute-start | bytes 3145736 | tf_op jit(solution)/shard_map/ppermute | solution.py:353
  296.7 35.3 %collective-permute-start.20 = (f32[1,512,512]{2,1,0:T(8,128)}, f32[1,512,512]{2,1,0:T(8,128)S(1)}, u32[]{:S(2)}, u32[]{:S(2)}) collective-permute-start(f32[1,512,512]{2,1,0:T(8,128)} %shard_map.120.refs_15_), channel_id=1, source_target_pairs={{0,4},{4,0},{1,5},{5,1},{2,6},{6,2},{3,7},{7,3},{8,12},{12,8},{9,1... | collective-permute-start | bytes 3145736 | tf_op jit(solution)/shard_map/ppermute | solution.py:353
  311.9 9.8 %copy-start.12 = (f32[4,256,256]{2,1,0:T(8,128)S(1)}, f32[4,256,256]{2,1,0:T(8,128)}, u32[]{:S(2)}) copy-start(f32[4,256,256]{2,1,0:T(8,128)} %copy-done.11) | copy-start | bytes 3145732
  324.7 8.9 %copy-start.2 = (f32[2,512,512]{2,1,0:T(8,128)S(1)}, f32[2,512,512]{2,1,0:T(8,128)}, u32[]{:S(2)}) copy-start(f32[2,512,512]{2,1,0:T(8,128)} %shard_map.121.refs_0_) | copy-start | bytes 6291460
  324.7 8.9 %copy-start.14 = (f32[1,1024,512]{2,1,0:T(8,128)S(1)}, f32[1,1024,512]{2,1,0:T(8,128)}, u32[]{:S(2)}) copy-start(f32[1,1024,512]{2,1,0:T(8,128)} %param.11) | copy-start | bytes 6291460
  (9 other events, 20.5 us)
Sparse Core Ops, SparseCore 0:
  53.1 108.2 all-gather.2

commit v9 on v8

--- a/solution.py
+++ b/solution.py
@@ -63,16 +63,20 @@
     for s in range(2):
         here = tab[s, leaf, 0] >= 0
 
-        @pl.when(here)
+        shared = leaf == 0 if s == 0 else False
+
+        @pl.when(jnp.logical_and(here, jnp.logical_not(shared)))
+        def _():
+            slot = tab[s, leaf, 0] // (lay.leaves + 1)
+            pltpu.make_async_copy(
+                gathered.at[col * lay.leaves + slot, pl.ds(0, lay.leaves), :, lanes], t.at[k, s], sems.at[k, s]
+            ).start()
+
+        @pl.when(jnp.logical_and(here, shared))
         def _():
             for j in range(lay.leaves):
-                entry = tab[s, leaf, j]
-                slot = entry // (lay.leaves + 1)
-                position = entry - slot * (lay.leaves + 1)
                 pltpu.make_async_copy(
-                    gathered.at[col * lay.leaves + slot, position, :, lanes],
-                    t.at[k, s, pl.ds(j * lay.part, lay.part)],
-                    sems.at[k, s],
+                    gathered.at[col * lay.leaves + j, lay.leaves, :, lanes], t.at[k, s, j], sems.at[k, s]
                 ).start()
 
         @pl.when(jnp.logical_not(here))
@@ -93,6 +97,10 @@
         @pl.when(tab[s, place_of(lay, pat, k)[0], 0] >= 0)
         def _():
             pltpu.make_async_copy(t.at[k, s], t.at[k, s], sems.at[k, s]).wait()
+
+
+def entry_pair(t, kp, s):
+    return jnp.concatenate([t[2 * kp + m, s].reshape(-1, BLK) for m in range(2)], axis=1)
 
 
 def back_product(turned_high, turned_low, high, low, s):
@@ -111,14 +119,10 @@
 
     image[...] = jnp.zeros_like(image)
 
-    group = 2 if number % 4 == 0 else 1
+    group = number // 2 // p_ref.shape[0]
 
     @pl.loop(0, number // 2 // group)
     def _(step):
-        deep = 2 * group * BLK
-        span = pl.ds(pl.multiple_of(step * deep, deep), deep)
-        p_high, p_low = halves(p_ref[span, :])
-        stacked = jnp.concatenate([p_high, p_low, p_high], axis=0)
         pairs = [step * group + m for m in range(group)]
         for s in range(2):
             found = False
@@ -130,15 +134,20 @@
             def _():
                 highs, lows = [], []
                 for kp in pairs:
-                    high, low = halves(jnp.concatenate([t[2 * kp, s], t[2 * kp + 1, s]], axis=1))
+                    high, low = halves(entry_pair(t, kp, s))
                     th[kp, s] = high
                     tl[kp, s] = low
                     highs.append(high)
                     lows.append(low)
-                image[s] += dot(jnp.concatenate(highs + highs + lows, axis=1), stacked)
+                image[s] += lax.dot_general(
+                    p_ref[step],
+                    jnp.concatenate(highs + highs + lows, axis=1),
+                    (((1,), (1,)), ((), ())),
+                    preferred_element_type=jnp.float32,
+                )
 
     for s in range(2):
-        high, low = halves(image[s].T)
+        high, low = halves(image[s])
         turned_high[s] = high
         turned_low[s] = low
 
@@ -175,7 +184,7 @@
 
             @pl.when(any_valid(lay, pat, tab, kp, s))
             def _():
-                high, low = halves(jnp.concatenate([t[2 * kp, s], t[2 * kp + 1, s]], axis=1))
+                high, low = halves(entry_pair(t, kp, s))
                 out[...] += back_product(turned_high, turned_low, high, low, s).T
 
 
@@ -188,8 +197,32 @@
     return pl.CostEstimate(flops=flops, bytes_accessed=4 * values, transcendentals=0)
 
 
-def panel_product(lay, pattern, table, order, gathered, normed, tokens):
-    number, wide, rows = pattern.shape[0], normed.shape[1], order.shape[0]
+def split_kernel(p_ref, *refs):
+    out_ref = refs[-1]
+    deep = out_ref.shape[2] // 3
+
+    @pl.loop(0, out_ref.shape[0])
+    def _(step):
+        high, low = halves(p_ref[pl.ds(pl.multiple_of(step * deep, deep), deep), :].T)
+        out_ref[step] = jnp.concatenate([high, low, high], axis=1)
+
+
+def split_panel(normed, tokens):
+    depth, wide = normed.shape
+    group = 4 if depth % (4 * BLK) == 0 else 2
+    steps, deep = depth // (group * BLK), group * BLK
+    return pl.pallas_call(
+        split_kernel,
+        out_shape=jax.ShapeDtypeStruct((steps, wide, 3 * deep), jnp.bfloat16),
+        in_specs=[VMEM] + [ANY] * len(tokens),
+        out_specs=VMEM,
+        compiler_params=pltpu.CompilerParams(vmem_limit_bytes=VMEM_BYTES),
+        cost_estimate=estimate(8 * depth * wide, 3 * depth * wide),
+    )(normed, *tokens)
+
+
+def panel_product(lay, pattern, table, order, gathered, split, tokens):
+    number, wide, rows = pattern.shape[0], split.shape[1], order.shape[0]
     half = lay.half
     pairs = number // 2
     block = jax.ShapeDtypeStruct((pairs // rows, 2 * BLK, wide), jnp.float32)
@@ -200,15 +233,15 @@
         in_specs=[SMEM] * 3 + [ANY, VMEM] + [ANY] * len(tokens),
         out_specs=[VMEM] * (rows + 1),
         scratch_shapes=[
-            pltpu.VMEM((number, 2, half, BLK), jnp.float32),
+            pltpu.VMEM((number, 2, lay.leaves, lay.part, BLK), jnp.float32),
             pltpu.VMEM((pairs, 2, half, 2 * BLK), jnp.bfloat16),
             pltpu.VMEM((pairs, 2, half, 2 * BLK), jnp.bfloat16),
-            pltpu.VMEM((2, half, wide), jnp.float32),
+            pltpu.VMEM((2, wide, half), jnp.float32),
             pltpu.SemaphoreType.DMA((number, 2)),
         ],
         compiler_params=pltpu.CompilerParams(vmem_limit_bytes=VMEM_BYTES),
         cost_estimate=estimate(18 * half * number * BLK * wide, 2 * half * number * BLK),
-    )(pattern, table, order, gathered, normed, *tokens)
+    )(pattern, table, order, gathered, split, *tokens)
     return result[: rows - 1], result[rows - 1 :]
 
 
@@ -221,7 +254,7 @@
         in_specs=[SMEM] * 3 + [ANY, VMEM, VMEM] + [ANY] * len(tokens),
         out_specs=VMEM,
         scratch_shapes=[
-            pltpu.VMEM((number, 2, half, BLK), jnp.float32),
+            pltpu.VMEM((number, 2, lay.leaves, lay.part, BLK), jnp.float32),
             pltpu.SemaphoreType.DMA((number, 2)),
         ],
         compiler_params=pltpu.CompilerParams(vmem_limit_bytes=VMEM_BYTES),
@@ -392,10 +425,11 @@
     both = lower[: 2 * part]
     for chip in range(2, leaves, 2):
         both = jnp.where(me_leaf == chip, lax.ppermute(lower[chip * part : (chip + 2) * part], "leaf", [(0, chip)]), both)
+    split = split_panel(normed, [both])
     other = lax.ppermute(both[part:], "leaf", [(chip, chip + 1) for chip in range(0, leaves, 2)])
     extra = jnp.where(me_leaf % 2 == 0, both[:part], other)
     held = jnp.concatenate([whole.reshape(parts, part, width), extra[None]], axis=0)
-    gathered = lax.all_gather(after(held, pieces[1, 0], pieces[-1, 0]), ("col", "leaf"), axis=0, tiled=False)
+    gathered = lax.all_gather(after(held, pieces[1, 0], pieces[-1, 0], split), ("col", "leaf"), axis=0, tiled=False)
     own = jnp.stack([lower, swapped])
     hop(1, 0, gathered)
 
@@ -413,7 +447,7 @@
     early_in = send_over_rows(early)
     if cols > 2:
         hop(0, 1, *early)
-    sent, turned = panel_product(lay, pattern[0], table, order, gathered, normed, early)
+    sent, turned = panel_product(lay, pattern[0], table, order, gathered, split, early)
     sent_in = send_over_rows(sent)
     middle = cols // 2
     for step in range(1, middle):
@@ -438,16 +472,13 @@
         terms_in.append(send_over_rows(term))
         tokens = term + late_in
     mine = diagonal_product(info, (rows - 1) * each, each, pieces, sigma_panel, term)
-    rest = diag_inverse[0] - mine.reshape(diag_inverse.shape[1:])
+    rest = diag_inverse[0].reshape(mine.shape) - mine
     tops = [*tops, *top_product(lay, table, order[rows - 1 :], *top_args, 1, [mine])]
-    update = []
-    for block in range(each):
-        total = 0.0
-        for i in range(each):
-            for value in terms_in[i]:
-                total += jnp.where(near_here[me_row, i] == me_row * each + block, value[0], 0.0)
-        update.append(total)
-    sigma_diag = rest - jnp.concatenate(update, axis=0)
+    for i in range(each):
+        here = near_here[me_row, i] == me_row * each + jnp.arange(each)
+        for value in terms_in[i]:
+            rest -= jnp.where(here[:, None, None], value, 0.0)
+    sigma_diag = rest.reshape(diag_inverse.shape[1:])
 
     sigma_top = jnp.concatenate([sum(early_in, tops[0]), sum(late_in, tops[1])], axis=0).reshape(-1, width)
     return (sigma_top, sigma_panel[None], sigma_diag[None])

time: 344 us -> 350 us (1.017); the launches traced: 343 us -> 344 us
  Pallas kernels: 87.6 us -> 93.6 us
  waiting for transfers between devices: 153 us -> 149 us
    pallas_call x0 -> x1, Pallas kernels: none -> 6.48 us  [split_panel(): pl.pallas_call(split_kernel, out_shape=jax.ShapeDtypeStruct((steps, wide,...]
    ppermute x1, waiting for transfers between devices: 8.96 us -> 3.27 us  [per_device(): lax.ppermute(upper, 'row', [(r, rows - 1 - r) for r in range(rows)])]
    ppermute x12, waiting for transfers between devices: 24.3 us -> 29.7 us  [hop(): lax.ppermute(pieces[-way * step, run], 'col', [(i, i + way) for i in at])]
    ppermute x5, waiting for transfers between devices: 18.9 us -> 15 us  [send_over_rows(): lax.ppermute(value, 'row', [(i, (i + a + 1) % rows) for i in range(rows)])]
  transfers between devices with their start and end apart: 22 -> 22, of which waited for: 7 -> 9; matrix products, arithmetic and copies ran while one was open for 8% -> 8% of each run, Pallas kernels for 26% -> 27%
where the time goes in v9:
time: 350 us; the launch traced here: 344 us
  waiting for transfers between devices  149 us (43%)
  Pallas kernels  93.6 us (27%)
  starting transfers between devices  46.8 us (13%)
  other arithmetic  21.2 us (6%)
  between operations  17 us (5%)
  local copies, waits for them, and re-layouts  16.8 us (5%)
    all_gather x1, waiting for transfers between devices, per_device(): lax.all_gather(after(held, pieces[1, 0], pieces[-1, 0], split), ('col', '...  101 us
    pallas_call x4, Pallas kernels, top_product(): pl.pallas_call(functools.partial(top_kernel, lay, chunks, chunk, len(toke...  31.5 us
    ppermute x12, waiting for transfers between devices, hop(): lax.ppermute(pieces[-way * step, run], 'col', [(i, i + way) for i in at])  29.7 us
    ppermute x12, starting transfers between devices, hop(): lax.ppermute(pieces[-way * step, run], 'col', [(i, i + way) for i in at])  21.8 us
    pallas_call x3, Pallas kernels, diagonal_product(): pl.pallas_call(functools.partial(diagonal_kernel, tuple(pieces), first, l...  20.8 us
    pallas_call x1, Pallas kernels, panel_product(): pl.pallas_call(functools.partial(panel_kernel, lay, rows, len(tokens)), o...  20.8 us
    ppermute x5, waiting for transfers between devices, send_over_rows(): lax.ppermute(value, 'row', [(i, (i + a + 1) % rows) for i in range(rows)])  15 us
    pallas_call x1, Pallas kernels, own_panel_product(): pl.pallas_call(functools.partial(own_panel_kernel, lay, rows, len(tokens)...  14.2 us
  transfers between devices with their start and end apart: 22, of which 9 were waited for; matrix products, arithmetic and copies ran while one was open for 8% of the time, Pallas kernels for 27%

profile of v9, /device:TPU:0, one launch (start us, length us, event | category | flops | bytes accessed | tf_op | source)
XLA Modules:
  0.0 344.4 jit_solution(11371263960379685666)
XLA Ops:
  7.2 1.9 slice.44
  9.1 5.7 %collective-permute-start.2 = (f32[512,256]{1,0:T(8,128)}, f32[512,256]{1,0:T(8,128)}, u32[]{:S(2)}, u32[]{:S(2)}) collective-permute-start(f32[512,256]{1,0:T(8,128)} %slice.44), channel_id=1, source_target_pairs={{0,16},{1,17},{2,18},{3,19},{4,20},{5,21},{6,22},{7,23}} | collective-permute-start | bytes 1572872 | tf_op jit(solution)/shard_map/ppermute | solution.py:427
  14.8 3.0 fusion.3
  20.9 2.7 dynamic-slice_bitcast_fusion
  23.6 3.7 %collective-permute-start.5 = (f32[512,512]{1,0:T(8,128)S(1)}, f32[512,512]{1,0:T(8,128)S(1)}, u32[]{:S(2)}, u32[]{:S(2)}) collective-permute-start(f32[512,512]{1,0:T(8,128)S(1)} %get-tuple-element.21.refs_0_), channel_id=1, source_target_pairs={{0,1},{1,2},{2,3},{4,5},{5,6},{6,7},{8,9},{9,10},{10,11},{12,13},{... | collective-permute-start | bytes 3145736 | tf_op jit(solution)/shard_map/ppermute | solution.py:406
  30.5 2.1 collective-permute-start.3
  34.5 6.5 %shard_map.103.refs_3_.p_ref = bf16[4,512,1536]{2,1,0:T(8,128)(2,1)} custom-call(f32[2048,512]{1,0:T(8,128)} %bitcast.44, f32[512,256]{1,0:T(8,128)} %copy-done.12), custom_call_target="tpu_custom_call" | custom-call | flops 8388608 | bytes 12582912 | tf_op jit(solution)/shard_map/pallas_call | solution.py:214
  41.0 3.3 collective-permute-done
  44.3 3.0 slice_bitcast_fusion
  48.5 3.5 %collective-permute-done.4.refs_1_.refs_0_ = f32[512,512]{1,0:T(8,128)S(1)} collective-permute-done((f32[512,512]{1,0:T(8,128)S(1)}, f32[512,512]{1,0:T(8,128)S(1)}, u32[]{:S(2)}, u32[]{:S(2)}) %collective-permute-start.4) | collective-permute-done | bytes 1048608 | tf_op jit(solution)/shard_map/ppermute | solution.py:406
  57.5 3.0 pad_maximum_fusion.own_ref
  60.5 101.0 %all-gather.3.cloned.1.call-done = f32[80,256,256]{2,1,0:T(8,128)} async-done(((f32[5,256,256]{2,1,0:T(8,128)}), f32[80,256,256]{2,1,0:T(8,128)}) %all-gather.3.cloned.1.call-update) | async-done | bytes 20971536 | tf_op jit(solution)/shard_map/all_gather | solution.py:432
  162.8 4.6 %collective-permute-start.7 = (f32[512,512]{1,0:T(8,128)}, f32[512,512]{1,0:T(8,128)S(1)}, u32[]{:S(2)}, u32[]{:S(2)}) collective-permute-start(f32[512,512]{1,0:T(8,128)} %shard_map.109.refs_1_), channel_id=1, source_target_pairs={{0,1},{1,2},{2,3},{4,5},{5,6},{6,7},{8,9},{9,10},{10,11},{12,13},{... | collective-permute-start | bytes 3145736 | tf_op jit(solution)/shard_map/ppermute | solution.py:406
  167.4 7.3 %shard_map.105.refs_0_.refs_1_ = f32[4,256,256]{2,1,0:T(8,128)} custom-call(s32[2,4,4]{2,1,0:T(4,128)} %dynamic-slice_bitcast_fusion.2.tab, s32[1]{0:T(128)} %get-tuple-element.28.dests, s32[1]{0:T(128)} %bitcast.1.leaf_ref, f32[16,5,256,256]{3,2,1,0:T(8,128)} %bitcast.32, f32[2,1024,256]{2,1,0:T(8,128)} %pad_maximum_fusion.own_ref, s32[5]{0:T(128)} %pad_add_fusion.refs_0_.info), custom_call_target="tpu_custom_call" | custom-call | flops 3221225472 | bytes 8388608 | tf_op jit(solution)/shard_map/pallas_call | solution.py:324
  174.6 4.1 %collective-permute-start.6 = (f32[4,256,256]{2,1,0:T(8,128)}, f32[4,256,256]{2,1,0:T(8,128)}, u32[]{:S(2)}, u32[]{:S(2)}) collective-permute-start(f32[4,256,256]{2,1,0:T(8,128)} %shard_map.105.refs_0_.refs_1_), channel_id=1, source_target_pairs={{0,4},{4,0},{1,5},{5,1},{2,6},{6,2},{3,7},{7,3},{8,12},{12,8},{9,1... | collective-permute-start | bytes 3145736 | tf_op jit(solution)/shard_map/ppermute | solution.py:386
  181.6 20.8 %shard_map.106 = (f32[4,256,512]{2,1,0:T(8,128)}, bf16[2,512,1024]{2,1,0:T(8,128)(2,1)}, bf16[2,512,1024]{2,1,0:T(8,128)(2,1)}) custom-call(s32[16]{0:T(128)} %bitcast.50, s32[2,4,4]{2,1,0:T(4,128)} %dynamic-slice_bitcast_fusion.2.tab, s32[2]{0:T(128)} %copy-done.19, f32[16,5,256,256]{3,2,1,0:T(8,128)} %bitcast.33, ...), custom_call_target="tpu_custom_call" | custom-call | flops 19327352832 | bytes 16777216 | tf_op jit(solution)/shard_map/pallas_call | solution.py:230
  202.4 7.2 %collective-permute-start.12 = (f32[4,256,512]{2,1,0:T(8,128)}, f32[4,256,512]{2,1,0:T(8,128)}, u32[]{:S(2)}, u32[]{:S(2)}) collective-permute-start(f32[4,256,512]{2,1,0:T(8,128)} %get-tuple-element.8.refs_1_), channel_id=1, source_target_pairs={{0,4},{4,0},{1,5},{5,1},{2,6},{6,2},{3,7},{7,3},{8,12},{12,8},{9,1... | collective-permute-start | bytes 6291464 | tf_op jit(solution)/shard_map/ppermute | solution.py:386
  209.6 1.8 collective-permute-done.10.refs_0_
  211.4 1.7 collective-permute-start.14
  216.7 14.2 %shard_map.107.refs_0_ = f32[4,256,512]{2,1,0:T(8,128)} custom-call(s32[16]{0:T(128)} %bitcast.51, s32[2,4,4]{2,1,0:T(4,128)} %dynamic-slice_bitcast_fusion.2.tab, s32[2]{0:T(128)} %copy-done.19, f32[16,5,256,256]{3,2,1,0:T(8,128)} %bitcast.34, bf16[2,512,1024]{2,1,0:T(8,128)(2,1)} %get-tuple-element.6.turned_high, ...), custom_call_target="tpu_custom_call" | custom-call | flops 25769803776 | bytes 8388608 | tf_op jit(solution)/shard_map/pallas_call | solution.py:251
  230.8 9.8 %shard_map.108.refs_0_ = f32[4,256,256]{2,1,0:T(8,128)} custom-call(s32[2,4,4]{2,1,0:T(4,128)} %dynamic-slice_bitcast_fusion.2.tab, s32[1]{0:T(128)} %get-tuple-element.29.dests, s32[1]{0:T(128)} %bitcast.1.leaf_ref, f32[16,5,256,256]{3,2,1,0:T(8,128)} %bitcast.35, f32[2,1024,256]{2,1,0:T(8,128)} %pad_maximum_fusion.own_ref, f32[4,256,512]{2,1,0:T(8,128)} %shard_map.107.refs_0_), custom_call_target="tpu_custom_call" | custom-call | flops 3221225472 | bytes 8388608 | tf_op jit(solution)/shard_map/pallas_call | solution.py:324
  240.7 4.5 %shard_map.118.refs_0_ = f32[4,256,256]{2,1,0:T(8,128)} custom-call(s32[2,4,4]{2,1,0:T(4,128)} %dynamic-slice_bitcast_fusion.2.tab, s32[1]{0:T(128)} %get-tuple-element.28.dests, s32[1]{0:T(128)} %bitcast.1.leaf_ref, f32[16,5,256,256]{3,2,1,0:T(8,128)} %bitcast.36, f32[2,1024,256]{2,1,0:T(8,128)} %pad_maximum_fusion.own_ref, f32[4,256,256]{2,1,0:T(8,128)} %shard_map.108.refs_0_), custom_call_target="tpu_custom_call" | custom-call | flops 3221225472 | bytes 8388608 | tf_op jit(solution)/shard_map/pallas_call | solution.py:324
  245.2 5.0 %collective-permute-done.12.refs_1_ = f32[4,256,512]{2,1,0:T(8,128)} collective-permute-done((f32[4,256,512]{2,1,0:T(8,128)}, f32[4,256,512]{2,1,0:T(8,128)}, u32[]{:S(2)}, u32[]{:S(2)}) %collective-permute-start.12) | collective-permute-done | bytes 2097184 | tf_op jit(solution)/shard_map/ppermute | solution.py:386
  250.2 3.4 add_negate_fusion
  256.2 7.2 %collective-permute-done.13.refs_0_ = f32[512,512]{1,0:T(8,128)S(1)} collective-permute-done((f32[512,512]{1,0:T(8,128)}, f32[512,512]{1,0:T(8,128)S(1)}, u32[]{:S(2)}, u32[]{:S(2)}) %collective-permute-start.13) | collective-permute-done | bytes 1048608 | tf_op jit(solution)/shard_map/ppermute | solution.py:406
  266.3 6.1 %shard_map.120.refs_15_ = f32[1,512,512]{2,1,0:T(8,128)} custom-call(s32[5]{0:T(128)} %pad_add_fusion.refs_0_.info, f32[512,512]{1,0:T(8,128)} %copy-done.3, f32[512,512]{1,0:T(8,128)} %shard_map.109.refs_1_, f32[512,512]{1,0:T(8,128)} %shard_map.110.refs_2_, f32[512,512]{1,0:T(8,128)} %shard_map.111.refs_3_, f32[512,512]{1,0:T(8,128)} %shard_map.112.refs_4_, ...), custom_call_target="tpu_custom_call" | custom-call | flops 1610612736 | bytes 4194304 | tf_op jit(solution)/shard_map/pallas_call | solution.py:362
  274.0 17.2 %collective-permute-done.17.refs_13_ = f32[512,512]{1,0:T(8,128)} collective-permute-done((f32[512,512]{1,0:T(8,128)}, f32[512,512]{1,0:T(8,128)}, u32[]{:S(2)}, u32[]{:S(2)}) %collective-permute-start.17) | collective-permute-done | bytes 1048608 | tf_op jit(solution)/shard_map/ppermute | solution.py:406
  293.1 6.1 %shard_map.121.refs_15_ = f32[1,512,512]{2,1,0:T(8,128)} custom-call(s32[5]{0:T(128)} %pad_add_fusion.refs_0_.info, f32[512,512]{1,0:T(8,128)} %copy-done.3, f32[512,512]{1,0:T(8,128)} %shard_map.109.refs_1_, f32[512,512]{1,0:T(8,128)} %shard_map.110.refs_2_, f32[512,512]{1,0:T(8,128)} %shard_map.111.refs_3_, f32[512,512]{1,0:T(8,128)} %shard_map.112.refs_4_, ...), custom_call_target="tpu_custom_call" | custom-call | flops 1610612736 | bytes 4194304 | tf_op jit(solution)/shard_map/pallas_call | solution.py:362
  303.7 8.5 %shard_map.122.refs_0_ = f32[2,512,512]{2,1,0:T(8,128)} custom-call(s32[5]{0:T(128)} %pad_add_fusion.refs_0_.info, f32[512,512]{1,0:T(8,128)} %copy-done.3, f32[512,512]{1,0:T(8,128)} %shard_map.109.refs_1_, f32[512,512]{1,0:T(8,128)} %shard_map.110.refs_2_, f32[512,512]{1,0:T(8,128)} %shard_map.111.refs_3_, f32[512,512]{1,0:T(8,128)} %shard_map.112.refs_4_, ...), custom_call_target="tpu_custom_call" | custom-call | flops 3221225472 | bytes 6291456 | tf_op jit(solution)/shard_map/pallas_call | solution.py:362
  312.3 9.9 %shard_map.123 = f32[4,256,256]{2,1,0:T(8,128)} custom-call(s32[2,4,4]{2,1,0:T(4,128)} %dynamic-slice_bitcast_fusion.2.tab, s32[1]{0:T(128)} %get-tuple-element.29.dests, s32[1]{0:T(128)} %bitcast.1.leaf_ref, f32[16,5,256,256]{3,2,1,0:T(8,128)} %bitcast.37, f32[2,1024,256]{2,1,0:T(8,128)} %pad_maximum_fusion.own_ref, f32[2,512,512]{2,1,0:T(8,128)} %shard_map.122.refs_0_), custom_call_target="tpu_custom_call" | custom-call | flops 3221225472 | bytes 8388608 | tf_op jit(solution)/shard_map/pallas_call | solution.py:324
  325.1 9.1 %collective-permute-done.20 = f32[1,512,512]{2,1,0:T(8,128)S(1)} collective-permute-done((f32[1,512,512]{2,1,0:T(8,128)}, f32[1,512,512]{2,1,0:T(8,128)S(1)}, u32[]{:S(2)}, u32[]{:S(2)}) %collective-permute-start.20) | collective-permute-done | bytes 1048608 | tf_op jit(solution)/shard_map/ppermute | solution.py:386
  334.2 3.4 select_subtract_fusion
  (102 shorter events, 36.4 us)
Async XLA Ops:
  7.2 154.3 %all-gather.3.cloned.1.call-start = ((), (), s32[]{:S(2)}) async-start(), calls=%async_computation | async-start | bytes 22282240 | tf_op jit(solution)/shard_map/all_gather | solution.py:432
  9.1 19.5 %collective-permute-start.2 = (f32[512,256]{1,0:T(8,128)}, f32[512,256]{1,0:T(8,128)}, u32[]{:S(2)}, u32[]{:S(2)}) collective-permute-start(f32[512,256]{1,0:T(8,128)} %slice.44), channel_id=1, source_target_pairs={{0,16},{1,17},{2,18},{3,19},{4,20},{5,21},{6,22},{7,23}} | collective-permute-start | bytes 1572872 | tf_op jit(solution)/shard_map/ppermute | solution.py:427
  17.8 23.3 %collective-permute-start.1 = (f32[1024,256]{1,0:T(8,128)}, f32[1024,256]{1,0:T(8,128)}, u32[]{:S(2)}, u32[]{:S(2)}) collective-permute-start(f32[1024,256]{1,0:T(8,128)} %get-tuple-element.24), channel_id=1, source_target_pairs={{8,24},{9,25},{10,26},{11,27}} | collective-permute-start | bytes 3145736 | tf_op jit(solution)/shard_map/ppermute | solution.py:423
  19.4 24.9 %collective-permute-start = (f32[1024,256]{1,0:T(8,128)}, f32[1024,256]{1,0:T(8,128)}, u32[]{:S(2)}, u32[]{:S(2)}) collective-permute-start(f32[1024,256]{1,0:T(8,128)} %get-tuple-element.25), channel_id=1, source_target_pairs={{0,4},{4,0},{1,5},{5,1},{2,6},{6,2},{3,7},{7,3},{8,12},{12,8},{9,1... | collective-permute-start | bytes 3145736 | tf_op jit(solution)/shard_map/ppermute | solution.py:422
  23.6 17.4 %copy-start.3 = (f32[512,512]{1,0:T(8,128)}, f32[512,512]{1,0:T(8,128)S(1)}, u32[]{:S(2)}) copy-start(f32[512,512]{1,0:T(8,128)S(1)} %get-tuple-element.21.refs_0_) | copy-start | bytes 3145732
  23.6 9.0 %copy-start.21 = (s32[2]{0:T(128)S(1)}, s32[2]{0:T(128)}, u32[]{:S(2)}) copy-start(s32[2]{0:T(128)} %constant.94.clone) | copy-start | bytes 28
  23.6 10.2 %copy-start.20 = (pred[2,4]{1,0:T(4,128)(4,1)S(1)}, pred[2,4]{1,0:T(4,128)(4,1)}, u32[]{:S(2)}) copy-start(pred[2,4]{1,0:T(4,128)(4,1)} %constant.95.clone) | copy-start | bytes 28
  23.6 24.9 %collective-permute-start.5 = (f32[512,512]{1,0:T(8,128)S(1)}, f32[512,512]{1,0:T(8,128)S(1)}, u32[]{:S(2)}, u32[]{:S(2)}) collective-permute-start(f32[512,512]{1,0:T(8,128)S(1)} %get-tuple-element.21.refs_0_), channel_id=1, source_target_pairs={{0,1},{1,2},{2,3},{4,5},{5,6},{6,7},{8,9},{9,10},{10,11},{12,13},{... | collective-permute-start | bytes 3145736 | tf_op jit(solution)/shard_map/ppermute | solution.py:406
  27.3 24.7 %collective-permute-start.4 = (f32[512,512]{1,0:T(8,128)S(1)}, f32[512,512]{1,0:T(8,128)S(1)}, u32[]{:S(2)}, u32[]{:S(2)}) collective-permute-start(f32[512,512]{1,0:T(8,128)S(1)} %get-tuple-element.21.refs_0_), channel_id=1, source_target_pairs={{1,0},{2,1},{3,2},{5,4},{6,5},{7,6},{9,8},{10,9},{11,10},{13,12},{... | collective-permute-start | bytes 3145736 | tf_op jit(solution)/shard_map/ppermute | solution.py:406
  30.5 10.4 %collective-permute-start.3 = (f32[256,256]{1,0:T(8,128)S(1)}, f32[256,256]{1,0:T(8,128)}, u32[]{:S(2)}, u32[]{:S(2)}) collective-permute-start(f32[256,256]{1,0:T(8,128)S(1)} %slice.61), channel_id=1, source_target_pairs={{0,8},{16,24},{1,9},{17,25},{2,10},{18,26},{3,11},{19,27},{4,12},{... | collective-permute-start | bytes 786440 | tf_op jit(solution)/shard_map/ppermute | solution.py:429
  34.5 9.8 %copy-start.10 = (f32[2048,256]{1,0:T(8,128)S(1)}, f32[2048,256]{1,0:T(8,128)}, u32[]{:S(2)}) copy-start(f32[2048,256]{1,0:T(8,128)} %param.8) | copy-start | bytes 6291460
  161.5 51.6 %collective-permute-start.8 = (f32[512,512]{1,0:T(8,128)}, f32[512,512]{1,0:T(8,128)S(1)}, u32[]{:S(2)}, u32[]{:S(2)}) collective-permute-start(f32[512,512]{1,0:T(8,128)} %shard_map.109.refs_1_), channel_id=1, source_target_pairs={{1,0},{2,1},{3,2},{5,4},{6,5},{7,6},{9,8},{10,9},{11,10},{13,12},{... | collective-permute-start | bytes 3145736 | tf_op jit(solution)/shard_map/ppermute | solution.py:406
  162.8 51.6 %collective-permute-start.7 = (f32[512,512]{1,0:T(8,128)}, f32[512,512]{1,0:T(8,128)S(1)}, u32[]{:S(2)}, u32[]{:S(2)}) collective-permute-start(f32[512,512]{1,0:T(8,128)} %shard_map.109.refs_1_), channel_id=1, source_target_pairs={{0,1},{1,2},{2,3},{4,5},{5,6},{6,7},{8,9},{9,10},{10,11},{12,13},{... | collective-permute-start | bytes 3145736 | tf_op jit(solution)/shard_map/ppermute | solution.py:406
  174.6 41.1 %collective-permute-start.6 = (f32[4,256,256]{2,1,0:T(8,128)}, f32[4,256,256]{2,1,0:T(8,128)}, u32[]{:S(2)}, u32[]{:S(2)}) collective-permute-start(f32[4,256,256]{2,1,0:T(8,128)} %shard_map.105.refs_0_.refs_1_), channel_id=1, source_target_pairs={{0,4},{4,0},{1,5},{5,1},{2,6},{6,2},{3,7},{7,3},{8,12},{12,8},{9,1... | collective-permute-start | bytes 3145736 | tf_op jit(solution)/shard_map/ppermute | solution.py:386
  178.7 23.7 %collective-permute-start.9 = (f32[512,512]{1,0:T(8,128)}, f32[512,512]{1,0:T(8,128)}, u32[]{:S(2)}, u32[]{:S(2)}) collective-permute-start(f32[512,512]{1,0:T(8,128)} %shard_map.110.refs_2_), channel_id=1, source_target_pairs={{1,2},{2,3},{5,6},{6,7},{9,10},{10,11},{13,14},{14,15},{17,18},{18... | collective-permute-start | bytes 3145736 | tf_op jit(solution)/shard_map/ppermute | solution.py:406
  180.3 31.0 %collective-permute-start.10 = (f32[512,512]{1,0:T(8,128)}, f32[512,512]{1,0:T(8,128)S(1)}, u32[]{:S(2)}, u32[]{:S(2)}) collective-permute-start(f32[512,512]{1,0:T(8,128)} %shard_map.111.refs_3_), channel_id=1, source_target_pairs={{1,0},{2,1},{5,4},{6,5},{9,8},{10,9},{13,12},{14,13},{17,16},{18,1... | collective-permute-start | bytes 3145736 | tf_op jit(solution)/shard_map/ppermute | solution.py:406
  202.4 47.8 %collective-permute-start.12 = (f32[4,256,512]{2,1,0:T(8,128)}, f32[4,256,512]{2,1,0:T(8,128)}, u32[]{:S(2)}, u32[]{:S(2)}) collective-permute-start(f32[4,256,512]{2,1,0:T(8,128)} %get-tuple-element.8.refs_1_), channel_id=1, source_target_pairs={{0,4},{4,0},{1,5},{5,1},{2,6},{6,2},{3,7},{7,3},{8,12},{12,8},{9,1... | collective-permute-start | bytes 6291464 | tf_op jit(solution)/shard_map/ppermute | solution.py:386
  211.4 61.1 %collective-permute-start.14 = (f32[512,512]{1,0:T(8,128)}, f32[512,512]{1,0:T(8,128)}, u32[]{:S(2)}, u32[]{:S(2)}) collective-permute-start(f32[512,512]{1,0:T(8,128)} %shard_map.114.refs_6_), channel_id=1, source_target_pairs={{2,3},{6,7},{10,11},{14,15},{18,19},{22,23},{26,27},{30,31}} | collective-permute-start | bytes 3145736 | tf_op jit(solution)/shard_map/ppermute | solution.py:406
  213.1 61.0 %collective-permute-start.15 = (f32[512,512]{1,0:T(8,128)}, f32[512,512]{1,0:T(8,128)S(1)}, u32[]{:S(2)}, u32[]{:S(2)}) collective-permute-start(f32[512,512]{1,0:T(8,128)} %shard_map.115.refs_7_), channel_id=1, source_target_pairs={{1,0},{5,4},{9,8},{13,12},{17,16},{21,20},{25,24},{29,28}} | collective-permute-start | bytes 3145736 | tf_op jit(solution)/shard_map/ppermute | solution.py:406
  214.4 49.0 %collective-permute-start.13 = (f32[512,512]{1,0:T(8,128)}, f32[512,512]{1,0:T(8,128)S(1)}, u32[]{:S(2)}, u32[]{:S(2)}) collective-permute-start(f32[512,512]{1,0:T(8,128)} %shard_map.113.refs_5_), channel_id=1, source_target_pairs={{1,0},{2,1},{5,4},{6,5},{9,8},{10,9},{13,12},{14,13},{17,16},{18,1... | collective-permute-start | bytes 3145736 | tf_op jit(solution)/shard_map/ppermute | solution.py:406
  215.7 37.9 %collective-permute-start.11 = (f32[512,512]{1,0:T(8,128)}, f32[512,512]{1,0:T(8,128)S(1)}, u32[]{:S(2)}, u32[]{:S(2)}) collective-permute-start(f32[512,512]{1,0:T(8,128)} %shard_map.112.refs_4_), channel_id=1, source_target_pairs={{1,2},{2,3},{5,6},{6,7},{9,10},{10,11},{13,14},{14,15},{17,18},{18... | collective-permute-start | bytes 3145736 | tf_op jit(solution)/shard_map/ppermute | solution.py:406
  240.6 9.5 %copy-start.11 = (f32[4,256,512]{2,1,0:T(8,128)S(1)}, f32[4,256,512]{2,1,0:T(8,128)}, u32[]{:S(2)}) copy-start(f32[4,256,512]{2,1,0:T(8,128)} %shard_map.107.refs_0_) | copy-start | bytes 6291460
  254.6 19.5 %collective-permute-start.16 = (f32[512,512]{1,0:T(8,128)}, f32[512,512]{1,0:T(8,128)}, u32[]{:S(2)}, u32[]{:S(2)}) collective-permute-start(f32[512,512]{1,0:T(8,128)} %shard_map.116.refs_8_), channel_id=1, source_target_pairs={{2,3},{6,7},{10,11},{14,15},{18,19},{22,23},{26,27},{30,31}} | collective-permute-start | bytes 3145736 | tf_op jit(solution)/shard_map/ppermute | solution.py:406
  264.4 26.8 %collective-permute-start.17 = (f32[512,512]{1,0:T(8,128)}, f32[512,512]{1,0:T(8,128)}, u32[]{:S(2)}, u32[]{:S(2)}) collective-permute-start(f32[512,512]{1,0:T(8,128)} %shard_map.117.refs_9_), channel_id=1, source_target_pairs={{1,0},{5,4},{9,8},{13,12},{17,16},{21,20},{25,24},{29,28}} | collective-permute-start | bytes 3145736 | tf_op jit(solution)/shard_map/ppermute | solution.py:406
  265.7 26.4 %collective-permute-start.18 = (f32[4,256,256]{2,1,0:T(8,128)}, f32[4,256,256]{2,1,0:T(8,128)S(1)}, u32[]{:S(2)}, u32[]{:S(2)}) collective-permute-start(f32[4,256,256]{2,1,0:T(8,128)} %shard_map.119.refs_11_), channel_id=1, source_target_pairs={{0,4},{4,0},{1,5},{5,1},{2,6},{6,2},{3,7},{7,3},{8,12},{12,8},{9,1... | collective-permute-start | bytes 3145736 | tf_op jit(solution)/shard_map/ppermute | solution.py:386
  272.5 29.9 %copy-start.9 = (f32[4,256,256]{2,1,0:T(8,128)S(1)}, f32[4,256,256]{2,1,0:T(8,128)}, u32[]{:S(2)}) copy-start(f32[4,256,256]{2,1,0:T(8,128)} %shard_map.108.refs_0_) | copy-start | bytes 3145732
  272.5 52.6 %collective-permute-start.19 = (f32[1,512,512]{2,1,0:T(8,128)}, f32[1,512,512]{2,1,0:T(8,128)}, u32[]{:S(2)}, u32[]{:S(2)}) collective-permute-start(f32[1,512,512]{2,1,0:T(8,128)} %shard_map.120.refs_15_), channel_id=1, source_target_pairs={{0,4},{4,0},{1,5},{5,1},{2,6},{6,2},{3,7},{7,3},{8,12},{12,8},{9,1... | collective-permute-start | bytes 3145736 | tf_op jit(solution)/shard_map/ppermute | solution.py:386
  274.0 18.1 %copy-start.14 = (f32[512,512]{1,0:T(8,128)}, f32[512,512]{1,0:T(8,128)S(1)}, u32[]{:S(2)}) copy-start(f32[512,512]{1,0:T(8,128)S(1)} %collective-permute-done.15.refs_11_) | copy-start | bytes 3145732
  299.2 35.0 %collective-permute-start.20 = (f32[1,512,512]{2,1,0:T(8,128)}, f32[1,512,512]{2,1,0:T(8,128)S(1)}, u32[]{:S(2)}, u32[]{:S(2)}) collective-permute-start(f32[1,512,512]{2,1,0:T(8,128)} %shard_map.121.refs_15_), channel_id=1, source_target_pairs={{0,4},{4,0},{1,5},{5,1},{2,6},{6,2},{3,7},{7,3},{8,12},{12,8},{9,1... | collective-permute-start | bytes 3145736 | tf_op jit(solution)/shard_map/ppermute | solution.py:386
  312.3 9.9 %copy-start.16 = (f32[4,256,256]{2,1,0:T(8,128)S(1)}, f32[4,256,256]{2,1,0:T(8,128)}, u32[]{:S(2)}) copy-start(f32[4,256,256]{2,1,0:T(8,128)} %copy-done.15) | copy-start | bytes 3145732
  323.6 10.7 %copy-start.2 = (f32[2,512,512]{2,1,0:T(8,128)S(1)}, f32[2,512,512]{2,1,0:T(8,128)}, u32[]{:S(2)}) copy-start(f32[2,512,512]{2,1,0:T(8,128)} %shard_map.122.refs_0_) | copy-start | bytes 6291460
  323.6 10.6 %copy-start.17 = (f32[1,1024,512]{2,1,0:T(8,128)S(1)}, f32[1,1024,512]{2,1,0:T(8,128)}, u32[]{:S(2)}) copy-start(f32[1,1024,512]{2,1,0:T(8,128)} %param.11) | copy-start | bytes 6291460
  (12 other events, 34.7 us)
Sparse Core Ops, SparseCore 0:
  53.1 108.2 all-gather.2

commit v10 on v8

--- a/solution.py
+++ b/solution.py
@@ -63,16 +63,20 @@
     for s in range(2):
         here = tab[s, leaf, 0] >= 0
 
-        @pl.when(here)
+        shared = leaf == 0 if s == 0 else False
+
+        @pl.when(jnp.logical_and(here, jnp.logical_not(shared)))
+        def _():
+            slot = tab[s, leaf, 0] // (lay.leaves + 1)
+            pltpu.make_async_copy(
+                gathered.at[col * lay.leaves + slot, pl.ds(0, lay.leaves), :, lanes], t.at[k, s], sems.at[k, s]
+            ).start()
+
+        @pl.when(jnp.logical_and(here, shared))
         def _():
             for j in range(lay.leaves):
-                entry = tab[s, leaf, j]
-                slot = entry // (lay.leaves + 1)
-                position = entry - slot * (lay.leaves + 1)
                 pltpu.make_async_copy(
-                    gathered.at[col * lay.leaves + slot, position, :, lanes],
-                    t.at[k, s, pl.ds(j * lay.part, lay.part)],
-                    sems.at[k, s],
+                    gathered.at[col * lay.leaves + j, lay.leaves, :, lanes], t.at[k, s, j], sems.at[k, s]
                 ).start()
 
         @pl.when(jnp.logical_not(here))
@@ -93,6 +97,10 @@
         @pl.when(tab[s, place_of(lay, pat, k)[0], 0] >= 0)
         def _():
             pltpu.make_async_copy(t.at[k, s], t.at[k, s], sems.at[k, s]).wait()
+
+
+def entry_pair(t, kp, s):
+    return jnp.concatenate([t[2 * kp + m, s].reshape(-1, BLK) for m in range(2)], axis=1)
 
 
 def back_product(turned_high, turned_low, high, low, s):
@@ -130,7 +138,7 @@
             def _():
                 highs, lows = [], []
                 for kp in pairs:
-                    high, low = halves(jnp.concatenate([t[2 * kp, s], t[2 * kp + 1, s]], axis=1))
+                    high, low = halves(entry_pair(t, kp, s))
                     th[kp, s] = high
                     tl[kp, s] = low
                     highs.append(high)
@@ -175,7 +183,7 @@
 
             @pl.when(any_valid(lay, pat, tab, kp, s))
             def _():
-                high, low = halves(jnp.concatenate([t[2 * kp, s], t[2 * kp + 1, s]], axis=1))
+                high, low = halves(entry_pair(t, kp, s))
                 out[...] += back_product(turned_high, turned_low, high, low, s).T
 
 
@@ -200,7 +208,7 @@
         in_specs=[SMEM] * 3 + [ANY, VMEM] + [ANY] * len(tokens),
         out_specs=[VMEM] * (rows + 1),
         scratch_shapes=[
-            pltpu.VMEM((number, 2, half, BLK), jnp.float32),
+            pltpu.VMEM((number, 2, lay.leaves, lay.part, BLK), jnp.float32),
             pltpu.VMEM((pairs, 2, half, 2 * BLK), jnp.bfloat16),
             pltpu.VMEM((pairs, 2, half, 2 * BLK), jnp.bfloat16),
             pltpu.VMEM((2, half, wide), jnp.float32),
@@ -221,7 +229,7 @@
         in_specs=[SMEM] * 3 + [ANY, VMEM, VMEM] + [ANY] * len(tokens),
         out_specs=VMEM,
         scratch_shapes=[
-            pltpu.VMEM((number, 2, half, BLK), jnp.float32),
+            pltpu.VMEM((number, 2, lay.leaves, lay.part, BLK), jnp.float32),
             pltpu.SemaphoreType.DMA((number, 2)),
         ],
         compiler_params=pltpu.CompilerParams(vmem_limit_bytes=VMEM_BYTES),
@@ -426,16 +434,20 @@
     sigma_panel = -sum(sent_in, kept).reshape(-1, normed.shape[1])
     late = [after(value, *sent_in) for value in late]
     late_in = send_over_rows(late)
-    for step in range(middle, cols - 1):
-        hop(1, step, sigma_panel)
-        if step + 1 < cols - 1:
-            hop(0, step + 1, sigma_panel)
+    waiting = []
+    for run, step in [(run, step + 1 - run) for step in range(middle, cols - 1) for run in (1, 0)]:
+        if step < cols - 1 and step < reach[0]:
+            hop(run, step, sigma_panel, *late)
+        elif step < cols - 1:
+            waiting.append((run, step))
 
     terms_in, tokens = [], late
     for i in range(each):
         there = {key: piece for key, piece in pieces.items() if abs(key[0]) <= reach[i]}
         term = [diagonal_product(info, a * each + i, 1, there, sigma_panel, tokens) for a in range(rows - 1)]
         terms_in.append(send_over_rows(term))
+        while waiting:
+            hop(*waiting.pop(0), *term)
         tokens = term + late_in
     mine = diagonal_product(info, (rows - 1) * each, each, pieces, sigma_panel, term)
     rest = diag_inverse[0] - mine.reshape(diag_inverse.shape[1:])

time: 344 us -> 348 us (1.012); the launches traced: 343 us -> 343 us
    ppermute x5, waiting for transfers between devices: 18.9 us -> 15.1 us  [send_over_rows(): lax.ppermute(value, 'row', [(i, (i + a + 1) % rows) for i in range(rows)])]
  transfers between devices with their start and end apart: 22 -> 22, of which waited for: 7 -> 8; matrix products, arithmetic and copies ran while one was open for 8% -> 8% of each run, Pallas kernels for 26% -> 25%
where the time goes in v10:
time: 348 us; the launch traced here: 343 us
  waiting for transfers between devices  153 us (44%)
  Pallas kernels  87.4 us (25%)
  starting transfers between devices  45.4 us (13%)
  other arithmetic  22.2 us (6%)
  between operations  19.1 us (5%)
  local copies, waits for them, and re-layouts  16.4 us (5%)
    all_gather x1, waiting for transfers between devices, per_device(): lax.all_gather(after(held, pieces[1, 0], pieces[-1, 0]), ('col', 'leaf'),...  101 us
    pallas_call x4, Pallas kernels, top_product(): pl.pallas_call(functools.partial(top_kernel, lay, chunks, chunk, len(toke...  31.2 us
    ppermute x12, waiting for transfers between devices, hop(): lax.ppermute(pieces[-way * step, run], 'col', [(i, i + way) for i in at])  27.4 us
    ppermute x12, starting transfers between devices, hop(): lax.ppermute(pieces[-way * step, run], 'col', [(i, i + way) for i in at])  22.3 us
    pallas_call x1, Pallas kernels, panel_product(): pl.pallas_call(functools.partial(panel_kernel, lay, rows, len(tokens)), o...  21.3 us
    pallas_call x3, Pallas kernels, diagonal_product(): pl.pallas_call(functools.partial(diagonal_kernel, tuple(pieces), first, l...  20.8 us
    ppermute x5, waiting for transfers between devices, send_over_rows(): lax.ppermute(value, 'row', [(i, (i + a + 1) % rows) for i in range(rows)])  15.1 us
    pallas_call x1, Pallas kernels, own_panel_product(): pl.pallas_call(functools.partial(own_panel_kernel, lay, rows, len(tokens)...  14.2 us
  transfers between devices with their start and end apart: 22, of which 8 were waited for; matrix products, arithmetic and copies ran while one was open for 8% of the time, Pallas kernels for 25%

profile of v10, /device:TPU:0, one launch (start us, length us, event | category | flops | bytes accessed | tf_op | source)
XLA Modules:
  0.0 343.0 jit_solution(2151701467336785903)
XLA Ops:
  7.2 1.9 slice.44
  9.1 5.6 %collective-permute-start.2 = (f32[512,256]{1,0:T(8,128)}, f32[512,256]{1,0:T(8,128)}, u32[]{:S(2)}, u32[]{:S(2)}) collective-permute-start(f32[512,256]{1,0:T(8,128)} %slice.44), channel_id=1, source_target_pairs={{0,16},{1,17},{2,18},{3,19},{4,20},{5,21},{6,22},{7,23}} | collective-permute-start | bytes 1572872 | tf_op jit(solution)/shard_map/ppermute | solution.py:402
  14.7 3.0 fusion.3
  20.9 2.7 dynamic-slice_bitcast_fusion
  23.6 3.7 %collective-permute-start.5 = (f32[512,512]{1,0:T(8,128)S(1)}, f32[512,512]{1,0:T(8,128)S(1)}, u32[]{:S(2)}, u32[]{:S(2)}) collective-permute-start(f32[512,512]{1,0:T(8,128)S(1)} %get-tuple-element.21.refs_0_), channel_id=1, source_target_pairs={{0,1},{1,2},{2,3},{4,5},{5,6},{6,7},{8,9},{9,10},{10,11},{12,13},{... | collective-permute-start | bytes 3145736 | tf_op jit(solution)/shard_map/ppermute | solution.py:381
  30.5 2.0 collective-permute-start.3
  35.3 9.0 %collective-permute-done = f32[1024,256]{1,0:T(8,128)} collective-permute-done((f32[1024,256]{1,0:T(8,128)}, f32[1024,256]{1,0:T(8,128)}, u32[]{:S(2)}, u32[]{:S(2)}) %collective-permute-start) | collective-permute-done | bytes 1048608 | tf_op jit(solution)/shard_map/ppermute | solution.py:397
  44.3 3.3 slice_bitcast_fusion
  48.8 3.2 collective-permute-done.4.refs_1_.refs_0_
  57.5 3.0 pad_maximum_fusion.own_ref
  60.5 101.0 %all-gather.3.cloned.1.call-done = f32[80,256,256]{2,1,0:T(8,128)} async-done(((f32[5,256,256]{2,1,0:T(8,128)}), f32[80,256,256]{2,1,0:T(8,128)}) %all-gather.3.cloned.1.call-update) | async-done | bytes 20971536 | tf_op jit(solution)/shard_map/all_gather | solution.py:406
  162.7 4.6 %collective-permute-start.7 = (f32[512,512]{1,0:T(8,128)}, f32[512,512]{1,0:T(8,128)S(1)}, u32[]{:S(2)}, u32[]{:S(2)}) collective-permute-start(f32[512,512]{1,0:T(8,128)} %shard_map.108.refs_1_), channel_id=1, source_target_pairs={{0,1},{1,2},{2,3},{4,5},{5,6},{6,7},{8,9},{9,10},{10,11},{12,13},{... | collective-permute-start | bytes 3145736 | tf_op jit(solution)/shard_map/ppermute | solution.py:381
  167.3 7.2 %shard_map.104.refs_0_.refs_1_ = f32[4,256,256]{2,1,0:T(8,128)} custom-call(s32[2,4,4]{2,1,0:T(4,128)} %dynamic-slice_bitcast_fusion.2.tab, s32[1]{0:T(128)} %get-tuple-element.30.dests, s32[1]{0:T(128)} %bitcast.1.leaf_ref, f32[16,5,256,256]{3,2,1,0:T(8,128)} %bitcast.33, f32[2,1024,256]{2,1,0:T(8,128)} %pad_maximum_fusion.own_ref, s32[5]{0:T(128)} %pad_add_fusion.refs_0_.info), custom_call_target="tpu_custom_call" | custom-call | flops 3221225472 | bytes 8388608 | tf_op jit(solution)/shard_map/pallas_call | solution.py:299
  174.6 4.1 %collective-permute-start.6 = (f32[4,256,256]{2,1,0:T(8,128)}, f32[4,256,256]{2,1,0:T(8,128)}, u32[]{:S(2)}, u32[]{:S(2)}) collective-permute-start(f32[4,256,256]{2,1,0:T(8,128)} %shard_map.104.refs_0_.refs_1_), channel_id=1, source_target_pairs={{0,4},{4,0},{1,5},{5,1},{2,6},{6,2},{3,7},{7,3},{8,12},{12,8},{9,1... | collective-permute-start | bytes 3145736 | tf_op jit(solution)/shard_map/ppermute | solution.py:361
  181.6 21.3 %shard_map.105 = (f32[4,256,512]{2,1,0:T(8,128)}, bf16[2,512,1024]{2,1,0:T(8,128)(2,1)}, bf16[2,512,1024]{2,1,0:T(8,128)(2,1)}) custom-call(s32[16]{0:T(128)} %bitcast.47, s32[2,4,4]{2,1,0:T(4,128)} %dynamic-slice_bitcast_fusion.2.tab, s32[2]{0:T(128)} %copy-done.17, f32[16,5,256,256]{3,2,1,0:T(8,128)} %bitcast.34, f32[2048,512]{1,0:T(8,128)} %bitcast.46, ...), custom_call_target="tpu_custom_call" | custom-call | flops 19327352832 | bytes 16777216 | tf_op jit(solution)/shard_map/pallas_call | solution.py:205
  202.9 4.3 %collective-permute-start.13 = (f32[4,256,512]{2,1,0:T(8,128)}, f32[4,256,512]{2,1,0:T(8,128)}, u32[]{:S(2)}, u32[]{:S(2)}) collective-permute-start(f32[4,256,512]{2,1,0:T(8,128)} %get-tuple-element.8.refs_1_), channel_id=1, source_target_pairs={{0,4},{4,0},{1,5},{5,1},{2,6},{6,2},{3,7},{7,3},{8,12},{12,8},{9,1... | collective-permute-start | bytes 6291464 | tf_op jit(solution)/shard_map/ppermute | solution.py:361
  209.5 2.0 collective-permute-done.10.refs_0_
  214.5 14.2 %shard_map.106.refs_0_ = f32[4,256,512]{2,1,0:T(8,128)} custom-call(s32[16]{0:T(128)} %bitcast.48, s32[2,4,4]{2,1,0:T(4,128)} %dynamic-slice_bitcast_fusion.2.tab, s32[2]{0:T(128)} %copy-done.17, f32[16,5,256,256]{3,2,1,0:T(8,128)} %bitcast.35, bf16[2,512,1024]{2,1,0:T(8,128)(2,1)} %get-tuple-element.6.turned_high, ...), custom_call_target="tpu_custom_call" | custom-call | flops 25769803776 | bytes 8388608 | tf_op jit(solution)/shard_map/pallas_call | solution.py:226
  228.7 9.8 %shard_map.107.refs_0_ = f32[4,256,256]{2,1,0:T(8,128)} custom-call(s32[2,4,4]{2,1,0:T(4,128)} %dynamic-slice_bitcast_fusion.2.tab, s32[1]{0:T(128)} %get-tuple-element.31.dests, s32[1]{0:T(128)} %bitcast.1.leaf_ref, f32[16,5,256,256]{3,2,1,0:T(8,128)} %bitcast.36, f32[2,1024,256]{2,1,0:T(8,128)} %pad_maximum_fusion.own_ref, f32[4,256,512]{2,1,0:T(8,128)} %shard_map.106.refs_0_), custom_call_target="tpu_custom_call" | custom-call | flops 3221225472 | bytes 8388608 | tf_op jit(solution)/shard_map/pallas_call | solution.py:299
  238.5 4.4 %shard_map.115.refs_0_ = f32[4,256,256]{2,1,0:T(8,128)} custom-call(s32[2,4,4]{2,1,0:T(4,128)} %dynamic-slice_bitcast_fusion.2.tab, s32[1]{0:T(128)} %get-tuple-element.30.dests, s32[1]{0:T(128)} %bitcast.1.leaf_ref, f32[16,5,256,256]{3,2,1,0:T(8,128)} %bitcast.37, f32[2,1024,256]{2,1,0:T(8,128)} %pad_maximum_fusion.own_ref, f32[4,256,256]{2,1,0:T(8,128)} %shard_map.107.refs_0_), custom_call_target="tpu_custom_call" | custom-call | flops 3221225472 | bytes 8388608 | tf_op jit(solution)/shard_map/pallas_call | solution.py:299
  242.9 7.8 %collective-permute-done.13.refs_1_ = f32[4,256,512]{2,1,0:T(8,128)} collective-permute-done((f32[4,256,512]{2,1,0:T(8,128)}, f32[4,256,512]{2,1,0:T(8,128)}, u32[]{:S(2)}, u32[]{:S(2)}) %collective-permute-start.13) | collective-permute-done | bytes 2097184 | tf_op jit(solution)/shard_map/ppermute | solution.py:361
  250.6 4.0 %add_negate_fusion = f32[4,256,512]{2,1,0:T(8,128)} fusion(f32[4,256,512]{2,1,0:T(8,128)} %shard_map.106.refs_0_, f32[4,256,512]{2,1,0:T(8,128)} %collective-permute-done.13.refs_1_), kind=kLoop, calls=%fused_computation.4 | loop fusion | flops 1048576 | bytes 6291456 | tf_op jit(solution)/shard_map/neg | solution.py:434
  256.0 6.1 %shard_map.117.refs_1_.refs_15_ = f32[1,512,512]{2,1,0:T(8,128)} custom-call(s32[5]{0:T(128)} %pad_add_fusion.refs_0_.info, f32[512,512]{1,0:T(8,128)} %copy-done.3, f32[512,512]{1,0:T(8,128)} %shard_map.108.refs_1_, f32[512,512]{1,0:T(8,128)} %shard_map.109.refs_2_, f32[512,512]{1,0:T(8,128)} %shard_map.110.refs_3_, f32[512,512]{1,0:T(8,128)} %shard_map.111.refs_4_, ...), custom_call_target="tpu_custom_call" | custom-call | flops 1610612736 | bytes 4194304 | tf_op jit(solution)/shard_map/pallas_call | solution.py:337
  265.6 1.8 collective-permute-start.18
  267.7 22.2 %collective-permute-done.17.refs_13_ = f32[512,512]{1,0:T(8,128)S(1)} collective-permute-done((f32[512,512]{1,0:T(8,128)}, f32[512,512]{1,0:T(8,128)S(1)}, u32[]{:S(2)}, u32[]{:S(2)}) %collective-permute-start.17) | collective-permute-done | bytes 1048608 | tf_op jit(solution)/shard_map/ppermute | solution.py:381
  289.9 1.8 collective-permute-done.18.refs_16_
  292.8 6.1 %shard_map.120.refs_15_ = f32[1,512,512]{2,1,0:T(8,128)} custom-call(s32[5]{0:T(128)} %pad_add_fusion.refs_0_.info, f32[512,512]{1,0:T(8,128)} %copy-done.3, f32[512,512]{1,0:T(8,128)} %shard_map.108.refs_1_, f32[512,512]{1,0:T(8,128)} %shard_map.109.refs_2_, f32[512,512]{1,0:T(8,128)} %shard_map.110.refs_3_, f32[512,512]{1,0:T(8,128)} %shard_map.111.refs_4_, ...), custom_call_target="tpu_custom_call" | custom-call | flops 1610612736 | bytes 4194304 | tf_op jit(solution)/shard_map/pallas_call | solution.py:337
  299.0 1.8 collective-permute-start.20
  305.7 8.5 %shard_map.121.refs_0_ = f32[2,512,512]{2,1,0:T(8,128)} custom-call(s32[5]{0:T(128)} %pad_add_fusion.refs_0_.info, f32[512,512]{1,0:T(8,128)} %copy-done.3, f32[512,512]{1,0:T(8,128)} %shard_map.108.refs_1_, f32[512,512]{1,0:T(8,128)} %shard_map.109.refs_2_, f32[512,512]{1,0:T(8,128)} %shard_map.110.refs_3_, f32[512,512]{1,0:T(8,128)} %shard_map.111.refs_4_, ...), custom_call_target="tpu_custom_call" | custom-call | flops 3221225472 | bytes 6291456 | tf_op jit(solution)/shard_map/pallas_call | solution.py:337
  314.2 9.9 %shard_map.122 = f32[4,256,256]{2,1,0:T(8,128)} custom-call(s32[2,4,4]{2,1,0:T(4,128)} %dynamic-slice_bitcast_fusion.2.tab, s32[1]{0:T(128)} %get-tuple-element.31.dests, s32[1]{0:T(128)} %bitcast.1.leaf_ref, f32[16,5,256,256]{3,2,1,0:T(8,128)} %bitcast.38, f32[2,1024,256]{2,1,0:T(8,128)} %pad_maximum_fusion.own_ref, f32[2,512,512]{2,1,0:T(8,128)} %shard_map.121.refs_0_), custom_call_target="tpu_custom_call" | custom-call | flops 3221225472 | bytes 8388608 | tf_op jit(solution)/shard_map/pallas_call | solution.py:299
  327.0 5.5 %collective-permute-done.20 = f32[1,512,512]{2,1,0:T(8,128)S(1)} collective-permute-done((f32[1,512,512]{2,1,0:T(8,128)}, f32[1,512,512]{2,1,0:T(8,128)S(1)}, u32[]{:S(2)}, u32[]{:S(2)}) %collective-permute-start.20) | collective-permute-done | bytes 1048608 | tf_op jit(solution)/shard_map/ppermute | solution.py:361
  334.0 2.1 maximum_subtract_fusion
  (97 shorter events, 36.1 us)
Async XLA Ops:
  7.2 154.3 %all-gather.3.cloned.1.call-start = ((), (), s32[]{:S(2)}) async-start(), calls=%async_computation | async-start | bytes 22282240 | tf_op jit(solution)/shard_map/all_gather | solution.py:406
  9.1 19.5 %collective-permute-start.2 = (f32[512,256]{1,0:T(8,128)}, f32[512,256]{1,0:T(8,128)}, u32[]{:S(2)}, u32[]{:S(2)}) collective-permute-start(f32[512,256]{1,0:T(8,128)} %slice.44), channel_id=1, source_target_pairs={{0,16},{1,17},{2,18},{3,19},{4,20},{5,21},{6,22},{7,23}} | collective-permute-start | bytes 1572872 | tf_op jit(solution)/shard_map/ppermute | solution.py:402
  17.7 17.6 %collective-permute-start.1 = (f32[1024,256]{1,0:T(8,128)}, f32[1024,256]{1,0:T(8,128)}, u32[]{:S(2)}, u32[]{:S(2)}) collective-permute-start(f32[1024,256]{1,0:T(8,128)} %get-tuple-element.26), channel_id=1, source_target_pairs={{8,24},{9,25},{10,26},{11,27}} | collective-permute-start | bytes 3145736 | tf_op jit(solution)/shard_map/ppermute | solution.py:398
  19.4 24.9 %collective-permute-start = (f32[1024,256]{1,0:T(8,128)}, f32[1024,256]{1,0:T(8,128)}, u32[]{:S(2)}, u32[]{:S(2)}) collective-permute-start(f32[1024,256]{1,0:T(8,128)} %get-tuple-element.27), channel_id=1, source_target_pairs={{0,4},{4,0},{1,5},{5,1},{2,6},{6,2},{3,7},{7,3},{8,12},{12,8},{9,1... | collective-permute-start | bytes 3145736 | tf_op jit(solution)/shard_map/ppermute | solution.py:397
  23.6 24.0 %copy-start.3 = (f32[512,512]{1,0:T(8,128)}, f32[512,512]{1,0:T(8,128)S(1)}, u32[]{:S(2)}) copy-start(f32[512,512]{1,0:T(8,128)S(1)} %get-tuple-element.21.refs_0_) | copy-start | bytes 3145732
  23.6 8.9 %copy-start.19 = (s32[2]{0:T(128)S(1)}, s32[2]{0:T(128)}, u32[]{:S(2)}) copy-start(s32[2]{0:T(128)} %constant.94.clone) | copy-start | bytes 28
  23.6 10.1 %copy-start.18 = (pred[2,4]{1,0:T(4,128)(4,1)S(1)}, pred[2,4]{1,0:T(4,128)(4,1)}, u32[]{:S(2)}) copy-start(pred[2,4]{1,0:T(4,128)(4,1)} %constant.95.clone) | copy-start | bytes 28
  23.6 25.2 %collective-permute-start.5 = (f32[512,512]{1,0:T(8,128)S(1)}, f32[512,512]{1,0:T(8,128)S(1)}, u32[]{:S(2)}, u32[]{:S(2)}) collective-permute-start(f32[512,512]{1,0:T(8,128)S(1)} %get-tuple-element.21.refs_0_), channel_id=1, source_target_pairs={{0,1},{1,2},{2,3},{4,5},{5,6},{6,7},{8,9},{9,10},{10,11},{12,13},{... | collective-permute-start | bytes 3145736 | tf_op jit(solution)/shard_map/ppermute | solution.py:381
  27.3 24.7 %collective-permute-start.4 = (f32[512,512]{1,0:T(8,128)S(1)}, f32[512,512]{1,0:T(8,128)S(1)}, u32[]{:S(2)}, u32[]{:S(2)}) collective-permute-start(f32[512,512]{1,0:T(8,128)S(1)} %get-tuple-element.21.refs_0_), channel_id=1, source_target_pairs={{1,0},{2,1},{3,2},{5,4},{6,5},{7,6},{9,8},{10,9},{11,10},{13,12},{... | collective-permute-start | bytes 3145736 | tf_op jit(solution)/shard_map/ppermute | solution.py:381
  30.5 3.8 %collective-permute-start.3 = (f32[256,256]{1,0:T(8,128)S(1)}, f32[256,256]{1,0:T(8,128)}, u32[]{:S(2)}, u32[]{:S(2)}) collective-permute-start(f32[256,256]{1,0:T(8,128)S(1)} %slice.61), channel_id=1, source_target_pairs={{0,8},{16,24},{1,9},{17,25},{2,10},{18,26},{3,11},{19,27},{4,12},{... | collective-permute-start | bytes 786440 | tf_op jit(solution)/shard_map/ppermute | solution.py:403
  48.8 8.1 %copy-start.16 = (s32[2,2,4,4]{3,2,1,0:T(4,128)S(1)}, s32[2,2,4,4]{3,2,1,0:T(4,128)}, u32[]{:S(2)}) copy-start(s32[2,2,4,4]{3,2,1,0:T(4,128)} %constant.93.clone) | copy-start | bytes 772
  53.0 7.5 %copy-start.17 = (s32[2]{0:T(128)}, s32[2]{0:T(128)S(1)}, u32[]{:S(2)}) copy-start(s32[2]{0:T(128)S(1)} %and_select_fusion.order) | copy-start | bytes 28
  161.4 45.7 %collective-permute-start.8 = (f32[512,512]{1,0:T(8,128)}, f32[512,512]{1,0:T(8,128)S(1)}, u32[]{:S(2)}, u32[]{:S(2)}) collective-permute-start(f32[512,512]{1,0:T(8,128)} %shard_map.108.refs_1_), channel_id=1, source_target_pairs={{1,0},{2,1},{3,2},{5,4},{6,5},{7,6},{9,8},{10,9},{11,10},{13,12},{... | collective-permute-start | bytes 3145736 | tf_op jit(solution)/shard_map/ppermute | solution.py:381
  162.7 40.1 %collective-permute-start.7 = (f32[512,512]{1,0:T(8,128)}, f32[512,512]{1,0:T(8,128)S(1)}, u32[]{:S(2)}, u32[]{:S(2)}) collective-permute-start(f32[512,512]{1,0:T(8,128)} %shard_map.108.refs_1_), channel_id=1, source_target_pairs={{0,1},{1,2},{2,3},{4,5},{5,6},{6,7},{8,9},{9,10},{10,11},{12,13},{... | collective-permute-start | bytes 3145736 | tf_op jit(solution)/shard_map/ppermute | solution.py:381
  174.6 38.5 %collective-permute-start.6 = (f32[4,256,256]{2,1,0:T(8,128)}, f32[4,256,256]{2,1,0:T(8,128)}, u32[]{:S(2)}, u32[]{:S(2)}) collective-permute-start(f32[4,256,256]{2,1,0:T(8,128)} %shard_map.104.refs_0_.refs_1_), channel_id=1, source_target_pairs={{0,4},{4,0},{1,5},{5,1},{2,6},{6,2},{3,7},{7,3},{8,12},{12,8},{9,1... | collective-permute-start | bytes 3145736 | tf_op jit(solution)/shard_map/ppermute | solution.py:361
  178.7 29.5 %collective-permute-start.9 = (f32[512,512]{1,0:T(8,128)}, f32[512,512]{1,0:T(8,128)}, u32[]{:S(2)}, u32[]{:S(2)}) collective-permute-start(f32[512,512]{1,0:T(8,128)} %shard_map.109.refs_2_), channel_id=1, source_target_pairs={{1,2},{2,3},{5,6},{6,7},{9,10},{10,11},{13,14},{14,15},{17,18},{18... | collective-permute-start | bytes 3145736 | tf_op jit(solution)/shard_map/ppermute | solution.py:381
  180.3 31.1 %collective-permute-start.10 = (f32[512,512]{1,0:T(8,128)}, f32[512,512]{1,0:T(8,128)}, u32[]{:S(2)}, u32[]{:S(2)}) collective-permute-start(f32[512,512]{1,0:T(8,128)} %shard_map.110.refs_3_), channel_id=1, source_target_pairs={{1,0},{2,1},{5,4},{6,5},{9,8},{10,9},{13,12},{14,13},{17,16},{18,1... | collective-permute-start | bytes 3145736 | tf_op jit(solution)/shard_map/ppermute | solution.py:381
  202.9 47.8 %collective-permute-start.13 = (f32[4,256,512]{2,1,0:T(8,128)}, f32[4,256,512]{2,1,0:T(8,128)}, u32[]{:S(2)}, u32[]{:S(2)}) collective-permute-start(f32[4,256,512]{2,1,0:T(8,128)} %get-tuple-element.8.refs_1_), channel_id=1, source_target_pairs={{0,4},{4,0},{1,5},{5,1},{2,6},{6,2},{3,7},{7,3},{8,12},{12,8},{9,1... | collective-permute-start | bytes 6291464 | tf_op jit(solution)/shard_map/ppermute | solution.py:361
  207.2 47.5 %collective-permute-start.11 = (f32[512,512]{1,0:T(8,128)}, f32[512,512]{1,0:T(8,128)S(1)}, u32[]{:S(2)}, u32[]{:S(2)}) collective-permute-start(f32[512,512]{1,0:T(8,128)} %shard_map.111.refs_4_), channel_id=1, source_target_pairs={{1,2},{2,3},{5,6},{6,7},{9,10},{10,11},{13,14},{14,15},{17,18},{18... | collective-permute-start | bytes 3145736 | tf_op jit(solution)/shard_map/ppermute | solution.py:381
  208.2 46.5 %collective-permute-start.12 = (f32[512,512]{1,0:T(8,128)}, f32[512,512]{1,0:T(8,128)S(1)}, u32[]{:S(2)}, u32[]{:S(2)}) collective-permute-start(f32[512,512]{1,0:T(8,128)} %shard_map.112.refs_5_), channel_id=1, source_target_pairs={{1,0},{2,1},{5,4},{6,5},{9,8},{10,9},{13,12},{14,13},{17,16},{18,1... | collective-permute-start | bytes 3145736 | tf_op jit(solution)/shard_map/ppermute | solution.py:381
  211.4 56.0 %collective-permute-start.14 = (f32[512,512]{1,0:T(8,128)}, f32[512,512]{1,0:T(8,128)}, u32[]{:S(2)}, u32[]{:S(2)}) collective-permute-start(f32[512,512]{1,0:T(8,128)} %shard_map.113.refs_6_), channel_id=1, source_target_pairs={{2,3},{6,7},{10,11},{14,15},{18,19},{22,23},{26,27},{30,31}} | collective-permute-start | bytes 3145736 | tf_op jit(solution)/shard_map/ppermute | solution.py:381
  213.1 54.7 %collective-permute-start.15 = (f32[512,512]{1,0:T(8,128)}, f32[512,512]{1,0:T(8,128)}, u32[]{:S(2)}, u32[]{:S(2)}) collective-permute-start(f32[512,512]{1,0:T(8,128)} %shard_map.114.refs_7_), channel_id=1, source_target_pairs={{1,0},{5,4},{9,8},{13,12},{17,16},{21,20},{25,24},{29,28}} | collective-permute-start | bytes 3145736 | tf_op jit(solution)/shard_map/ppermute | solution.py:381
  262.2 5.2 %copy-start.4 = (f32[1,512,512]{2,1,0:T(8,128)S(1)}, f32[1,512,512]{2,1,0:T(8,128)}, u32[]{:S(2)}) copy-start(f32[1,512,512]{2,1,0:T(8,128)} %shard_map.117.refs_1_.refs_15_) | copy-start | bytes 3145732
  262.2 5.5 %collective-permute-start.16 = (f32[512,512]{1,0:T(8,128)}, f32[512,512]{1,0:T(8,128)}, u32[]{:S(2)}, u32[]{:S(2)}) collective-permute-start(f32[512,512]{1,0:T(8,128)} %shard_map.118.refs_8_), channel_id=1, source_target_pairs={{2,3},{6,7},{10,11},{14,15},{18,19},{22,23},{26,27},{30,31}} | collective-permute-start | bytes 3145736 | tf_op jit(solution)/shard_map/ppermute | solution.py:381
  264.0 40.3 %copy-start.9 = (f32[4,256,256]{2,1,0:T(8,128)S(1)}, f32[4,256,256]{2,1,0:T(8,128)}, u32[]{:S(2)}) copy-start(f32[4,256,256]{2,1,0:T(8,128)} %shard_map.107.refs_0_) | copy-start | bytes 3145732
  264.0 26.0 %collective-permute-start.17 = (f32[512,512]{1,0:T(8,128)}, f32[512,512]{1,0:T(8,128)S(1)}, u32[]{:S(2)}, u32[]{:S(2)}) collective-permute-start(f32[512,512]{1,0:T(8,128)} %shard_map.119.refs_9_), channel_id=1, source_target_pairs={{1,0},{5,4},{9,8},{13,12},{17,16},{21,20},{25,24},{29,28}} | collective-permute-start | bytes 3145736 | tf_op jit(solution)/shard_map/ppermute | solution.py:381
  265.6 26.2 %collective-permute-start.18 = (f32[4,256,256]{2,1,0:T(8,128)S(1)}, f32[4,256,256]{2,1,0:T(8,128)S(1)}, u32[]{:S(2)}, u32[]{:S(2)}) collective-permute-start(f32[4,256,256]{2,1,0:T(8,128)S(1)} %copy-done.10), channel_id=1, source_target_pairs={{0,4},{4,0},{1,5},{5,1},{2,6},{6,2},{3,7},{7,3},{8,12},{12,8},{9,1... | collective-permute-start | bytes 3145736 | tf_op jit(solution)/shard_map/ppermute | solution.py:361
  267.4 59.5 %collective-permute-start.19 = (f32[1,512,512]{2,1,0:T(8,128)S(1)}, f32[1,512,512]{2,1,0:T(8,128)}, u32[]{:S(2)}, u32[]{:S(2)}) collective-permute-start(f32[1,512,512]{2,1,0:T(8,128)S(1)} %copy-done.4), channel_id=1, source_target_pairs={{0,4},{4,0},{1,5},{5,1},{2,6},{6,2},{3,7},{7,3},{8,12},{12,8},{9,1... | collective-permute-start | bytes 3145736 | tf_op jit(solution)/shard_map/ppermute | solution.py:361
  299.0 33.5 %collective-permute-start.20 = (f32[1,512,512]{2,1,0:T(8,128)}, f32[1,512,512]{2,1,0:T(8,128)S(1)}, u32[]{:S(2)}, u32[]{:S(2)}) collective-permute-start(f32[1,512,512]{2,1,0:T(8,128)} %shard_map.120.refs_15_), channel_id=1, source_target_pairs={{0,4},{4,0},{1,5},{5,1},{2,6},{6,2},{3,7},{7,3},{8,12},{12,8},{9,1... | collective-permute-start | bytes 3145736 | tf_op jit(solution)/shard_map/ppermute | solution.py:361
  314.2 9.9 %copy-start.12 = (f32[4,256,256]{2,1,0:T(8,128)S(1)}, f32[4,256,256]{2,1,0:T(8,128)}, u32[]{:S(2)}) copy-start(f32[4,256,256]{2,1,0:T(8,128)} %copy-done.11) | copy-start | bytes 3145732
  327.0 7.1 %copy-start.2 = (f32[2,512,512]{2,1,0:T(8,128)S(1)}, f32[2,512,512]{2,1,0:T(8,128)}, u32[]{:S(2)}) copy-start(f32[2,512,512]{2,1,0:T(8,128)} %shard_map.121.refs_0_) | copy-start | bytes 6291460
  327.0 7.1 %copy-start.15 = (f32[1,1024,512]{2,1,0:T(8,128)S(1)}, f32[1,1024,512]{2,1,0:T(8,128)}, u32[]{:S(2)}) copy-start(f32[1,1024,512]{2,1,0:T(8,128)} %param.11) | copy-start | bytes 6291460
  (10 other events, 18.9 us)
Sparse Core Ops, SparseCore 0:
  53.1 108.2 all-gather.2
